TPU v7x, 256 devices: a whole 4x4x8 slice. The times are simulated.
256 devices in a mesh: lat: 16 (over x, y), lon: 16 (over z, core).
Axes of the slice: x: 4, y: 4, z: 8, core: 2. Of those that a mesh axis runs over, the one named last changes fastest.
Arguments:
- fields: float32 [4, 8, 1024, 2048], P(None, None, 'lat', 'lon'), may hold values from -6 to 6
- hyper_coef: float32 [4, 8], replicated, may hold values from 0.004 to 0.03
- vert_coef: float32 [4, 7], replicated, may hold values from 0.2 to 5
- dep_owner: int32 [16, 16, 8, 1], P('lat', 'lon'), may hold values from 0 to 15, as said below
- dep_row: int32 [16, 16, 8, 1], P('lat', 'lon'), may hold values from 0 to 2
- dep_col: int32 [16, 16, 8, 1], P('lat', 'lon'), may hold values from 0 to 3
- shifts: int32 [16, 16, 8, 2], P('lat', 'lon'), may hold values from 1 to 29
- fracs: int32 [16, 16, 8, 2], P('lat', 'lon'), may hold values from 0 to 15
Outputs:
- advected: float32 [4, 8, 1024, 2048], P(None, None, 'lat', 'lon')
Inputs may be any that keep to these rules, and one draw needn't show every extreme that they name: `dep_owner`: among the 8 arrival tiles of one device, no value is named more than 2 times, and every device names some value exactly 2 times. In the first and last latitude band the values may be any longitude index; in every other band they lie within 2 of the device's own longitude index, counted around the circle.
All inputs are finite; a program needn't handle non-finite values.
Results may differ from a plain program's by a relative error of at most 0.00007.
Values sent between devices are 32-bit elements; how exact they have to be, the bound alone decides.
No kernel may reach another device: no remote copies, remote signals or barrier semaphores. Data moves between devices by JAX's collectives and lax.ppermute only.
A program may use at most 128 MiB of HBM per device.

v0:
```python
import jax
import jax.numpy as jnp
from jax import lax
from jax.sharding import PartitionSpec as P

TILE = 32
CAP = 2
FRACS = 16


HIGHEST_PRECISION = lax.Precision.HIGHEST


def padded(block, sides, width, periodic):
    for axis, dim in sides:
        count = lax.axis_size(axis)
        forward = [(i, i + 1) for i in range(count - 1)]
        if periodic:
            forward.append((count - 1, 0))
        backward = [(target, source) for source, target in forward]
        low = lax.ppermute(
            lax.slice_in_dim(block, block.shape[dim] - width, None, axis=dim), axis, forward
        )
        high = lax.ppermute(lax.slice_in_dim(block, 0, width, axis=dim), axis, backward)
        block = jnp.concatenate([low, block, high], axis=dim)
    return block


def from_behind(value, axis, by):
    peers = lax.axis_size(axis)
    return lax.ppermute(value, axis, [(i, (i + by) % peers) for i in range(peers)])


def cubic_weights(fraction_index):
    fraction = fraction_index.astype(jnp.float32) / FRACS
    return jnp.stack(
        [
            -fraction * (fraction - 1.0) * (fraction - 2.0) / 6.0,
            (fraction + 1.0) * (fraction - 1.0) * (fraction - 2.0) / 2.0,
            -(fraction + 1.0) * fraction * (fraction - 2.0) / 2.0,
            (fraction + 1.0) * fraction * (fraction - 1.0) / 6.0,
        ],
        axis=-1,
    )


def stencil_matrix(weights):
    row_ids = jnp.arange(TILE, dtype=jnp.int32)[:, None]
    col_ids = jnp.arange(TILE + 3, dtype=jnp.int32)[None, :]
    offset = col_ids - row_ids
    matrix = jnp.zeros(weights.shape[:-1] + (TILE, TILE + 3), jnp.float32)
    for step_index in range(4):
        matrix = matrix + weights[..., step_index, None, None] * (offset == step_index).astype(
            jnp.float32
        )
    return matrix


def placed_stencil(weights, lane_count):
    tile_total = weights.shape[0]
    tile_cols = lane_count // TILE
    position = jnp.arange(tile_total, dtype=jnp.int32) % tile_cols
    lanes = jnp.arange(lane_count, dtype=jnp.int32)
    target = lanes[None, :] - TILE * position[:, None]
    inside = ((target >= 0) & (target < TILE)).astype(jnp.float32)
    source = jnp.arange(TILE + 3, dtype=jnp.int32)
    offset = source[None, :, None] - target[:, None, :]
    matrix = jnp.zeros((tile_total, TILE + 3, lane_count), jnp.float32)
    for step_index in range(4):
        matrix = matrix + weights[:, step_index, None, None] * (offset == step_index).astype(
            jnp.float32
        )
    return matrix * inside[:, None, :]


def vertical_solve(psi_field, vert_coef):
    fcount = psi_field.shape[0]
    levels = psi_field.shape[1]
    zero_column = jnp.zeros((fcount, 1), jnp.float32)
    lower_coef = jnp.concatenate([zero_column, vert_coef], axis=1)
    upper_coef = jnp.concatenate([vert_coef, zero_column], axis=1)
    diagonal = 1.0 + lower_coef + upper_coef
    sweep_upper = []
    sweep_rhs = []
    for level_index in range(levels):
        lower_now = lower_coef[:, level_index][:, None, None]
        if level_index == 0:
            denominator = diagonal[:, 0][:, None, None]
            rhs_now = psi_field[:, 0]
        else:
            denominator = diagonal[:, level_index][:, None, None] + lower_now * sweep_upper[-1]
            rhs_now = psi_field[:, level_index] + lower_now * sweep_rhs[-1]
        sweep_upper.append(-upper_coef[:, level_index][:, None, None] / denominator)
        sweep_rhs.append(rhs_now / denominator)
    solution = [sweep_rhs[-1]]
    for level_index in range(levels - 2, -1, -1):
        solution.insert(0, sweep_rhs[level_index] - sweep_upper[level_index] * solution[0])
    return jnp.stack(solution, axis=1)


def face_laplacian(field_values):
    lat_padded = padded(field_values, (("lat", 2),), 1, False)
    lon_padded = padded(field_values, (("lon", 3),), 1, True)
    beside = (
        lat_padded[:, :, 2:, :]
        + lat_padded[:, :, :-2, :]
        + lon_padded[:, :, :, :-2]
        + lon_padded[:, :, :, 2:]
    )
    return beside - 4.0 * field_values


def body(fields, hyper_coef, vert_coef, dep_owner, dep_row, dep_col, shifts, fracs):
    fcount, levels, lat_cells, lon_cells = fields.shape
    tile_rows = lat_cells // TILE
    tile_cols = lon_cells // TILE
    lon_devs = lax.axis_size("lon")
    lat_devs = lax.axis_size("lat")
    band_index = lax.axis_index("lat")
    window_size = TILE + 3
    window_cells = window_size * window_size
    padded_size = (window_cells + 127) // 128 * 128
    band_ext = padded(fields, (("lat", 2),), TILE, False)
    east_cells = from_behind(band_ext[:, :, :, :TILE], "lon", -1)
    extended = jnp.concatenate([band_ext, east_cells], axis=3)
    ext_width = extended.shape[3]
    ext_flat = extended.reshape(fcount * levels, extended.shape[2] * ext_width)
    owners = dep_owner.reshape(-1)
    tiles_dev = owners.shape[0]
    dep_tile = jnp.clip(
        band_index * tile_rows - 1 + dep_row.reshape(-1), 0, tile_rows * lat_devs - 2
    )
    local_row = dep_tile - (band_index * tile_rows - 1)
    shift_pair = shifts.reshape(tiles_dev, 2)
    frac_pair = fracs.reshape(tiles_dev, 2)
    row_start = TILE * local_row + shift_pair[:, 0] - 1
    col_start = TILE * dep_col.reshape(-1) + shift_pair[:, 1] - 1
    tile_ids = jnp.arange(tiles_dev, dtype=jnp.int32)
    earlier = (owners[:, None] == owners[None, :]) & (tile_ids[None, :] < tile_ids[:, None])
    ranking = jnp.sum(earlier.astype(jnp.int32), axis=1)
    slot_index = owners * CAP + ranking
    record = jnp.stack(
        [row_start, col_start, frac_pair[:, 0], frac_pair[:, 1], jnp.ones_like(row_start)], axis=1
    )
    placing = (slot_index[:, None] == jnp.arange(lon_devs * CAP, dtype=jnp.int32)[None, :]).astype(
        jnp.int32
    )
    request_table = jnp.sum(placing[:, :, None] * record[:, None, :], axis=0).reshape(
        lon_devs, CAP, 5
    )
    cell_ids = jnp.arange(padded_size, dtype=jnp.int32)
    valid_cell = cell_ids < window_cells
    cell_row = jnp.where(valid_cell, cell_ids // window_size, 0)
    cell_col = jnp.where(valid_cell, cell_ids % window_size, 0)
    item_block = lax.all_to_all(request_table, "lon", split_axis=0, concat_axis=0, tiled=True)
    flat_items = item_block.reshape(-1, 5)
    item_count = flat_items.shape[0]
    flat_index = (
        (flat_items[:, 0:1] + cell_row[None, :]) * ext_width
        + flat_items[:, 1:2]
        + cell_col[None, :]
    )
    picked = jnp.take(ext_flat, flat_index.reshape(-1), axis=1)
    picked = picked.reshape(fcount * levels, item_count, padded_size)
    picked = jnp.where(valid_cell[None, None, :], picked, 0.0)
    windows = picked.transpose(1, 0, 2).reshape(item_count, fcount, levels, padded_size)
    gathered = windows.reshape(
        item_block.shape[0], item_block.shape[1], fcount, levels, windows.shape[-1]
    )
    returned = lax.all_to_all(gathered, "lon", split_axis=0, concat_axis=0, tiled=True)
    received_rows = returned.reshape(lon_devs * CAP, fcount, levels, returned.shape[-1])[slot_index]
    own_windows = received_rows[:, :, :, :window_cells].reshape(
        tiles_dev, fcount, levels, window_size, window_size
    )
    weight_rows = stencil_matrix(cubic_weights(frac_pair[:, 0]))
    column_place = placed_stencil(cubic_weights(frac_pair[:, 1]), lon_cells)
    column_pass = jnp.einsum(
        "tflab,tbk->tflak", own_windows, column_place, precision=HIGHEST_PRECISION
    )
    column_pass = column_pass.reshape(tile_rows, tile_cols, fcount, levels, window_size, lon_cells)
    row_weights = weight_rows.reshape(tile_rows, tile_cols, TILE, window_size)
    phi_blocks = jnp.einsum(
        "rcia,rcflak->flrik", row_weights, column_pass, precision=HIGHEST_PRECISION
    )
    phi_field = phi_blocks.reshape(fcount, levels, lat_cells, lon_cells)
    second_lap = face_laplacian(face_laplacian(phi_field))
    psi_field = phi_field - hyper_coef[:, :, None, None] * second_lap
    return vertical_solve(psi_field, vert_coef)


def solution(mesh):
    in_specs = (
        P(None, None, "lat", "lon"),
        P(),
        P(),
        P("lat", "lon", None, None),
        P("lat", "lon", None, None),
        P("lat", "lon", None, None),
        P("lat", "lon", None, None),
        P("lat", "lon", None, None),
    )
    out_specs = P(None, None, "lat", "lon")
    return jax.shard_map(body, mesh=mesh, in_specs=in_specs, out_specs=out_specs, check_vma=False)
```

profile of v0, /device:TPU:36, one launch (start us, length us, event | category | flops | bytes accessed | tf_op | source)
XLA Modules:
  0.0 401.1 jit_solution(14165805729621629376)
XLA Ops:
  0.0 0.9 convert_reduce_fusion
  0.9 0.7 multiply_add_fusion.7
  1.7 0.8 fusion.104
  2.5 0.8 add_add_fusion.1
  3.2 0.1 multiply_reduce_fusion
  3.3 0.7 copy.56
  4.0 8.6 %all-to-all-start = ((s32[16,2,5]{2,1,0:T(2,128)}), s32[16,2,5]{2,1,0:T(2,128)S(1)}, u32[]{:S(2)}, u32[]{:S(2)}) async-start(s32[16,2,5]{2,1,0:T(2,128)} %bitcast.5), calls=%async_computation | async-start | bytes 32768 | tf_op jit(solution)/shard_map/all_to_all | solution.py:155
  12.6 2.2 fusion.118
  14.8 3.5 collective-permute-start
  18.3 4.5 %collective-permute-start.1 = (f32[4,8,32,128]{3,2,1,0:T(8,128)}, f32[4,8,32,128]{3,2,1,0:T(8,128)S(1)}, u32[]{:S(2)}, u32[]{:S(2)}) collective-permute-start(f32[4,8,32,128]{3,2,1,0:T(8,128)} %get-tuple-element.52), channel_id=1, source_target_pairs={{16,0},{32,16},{48,32},{64,48},{80,64},{96,80},{112,96},{128,112},... | collective-permute-start | bytes 1572872 | tf_op jit(solution)/shard_map/ppermute | solution.py:24
  22.8 1.8 copy.58
  24.7 0.2 slice_reduce_fusion.1
  24.9 0.1 fusion.24
  25.0 0.2 copy.76
  25.1 0.2 compare_select_fusion
  25.3 7.7 %collective-permute-done = f32[4,8,32,128]{3,2,1,0:T(8,128)S(1)} collective-permute-done((f32[4,8,32,128]{3,2,1,0:T(8,128)}, f32[4,8,32,128]{3,2,1,0:T(8,128)S(1)}, u32[]{:S(2)}, u32[]{:S(2)}) %collective-permute-start) | collective-permute-done | bytes 524320 | tf_op jit(solution)/shard_map/ppermute | solution.py:21
  33.0 2.0 copy.57
  35.0 1.9 copy.59
  36.9 1.7 pad_maximum_fusion.9
  38.7 0.1 fusion.27
  38.8 6.5 %collective-permute-done.2 = f32[4,8,128,32]{2,3,1,0:T(8,128)S(1)} collective-permute-done((f32[4,8,128,32]{2,3,1,0:T(8,128)S(1)}, f32[4,8,128,32]{2,3,1,0:T(8,128)S(1)}, u32[]{:S(2)}, u32[]{:S(2)}) %collective-permute-start.2) | collective-permute-done | bytes 524320 | tf_op jit(solution)/shard_map/ppermute | solution.py:31
  45.3 2.7 pad_maximum_fusion
  48.0 4.7 %copy.60 = f32[4,8,128,160]{3,2,1,0:T(8,128)} copy(f32[4,8,128,160]{2,3,1,0:T(8,128)} %pad_maximum_fusion) | data formatting | bytes 5242880 | tf_op jit(solution)/shard_map/concatenate | solution.py:125
  52.7 4.9 %reshape.1024 = f32[32,20480]{1,0:T(8,128)S(1)} reshape(f32[4,8,128,160]{3,2,1,0:T(8,128)} %copy.60) | data formatting | bytes 5242880 | tf_op jit(solution)/shard_map/reshape | solution.py:127
  57.7 6.0 %copy.61 = f32[32,20480]{0,1:T(8,128)} copy(f32[32,20480]{1,0:T(8,128)S(1)} %reshape.1024) | data formatting | bytes 5242880 | tf_op jit(solution)/shard_map/reshape | solution.py:127
  63.7 139.0 %gather_fusion = f32[40960,32]{1,0:T(8,128)} fusion(f32[32,20480]{0,1:T(8,128)} %copy.61, s32[40960]{0:T(1024)S(1)} %broadcast_clamp_fusion), kind=kCustom, calls=%fused_computation | custom fusion | bytes 10649600 | tf_op jit(solution)/shard_map/jit(_take)/gather | solution.py:163
  202.7 14.0 %copy.62 = f32[32,32,1280]{2,0,1:T(8,128)} copy(f32[32,32,1280]{0,2,1:T(8,128)} %bitcast.104) | data formatting | bytes 10485760 | tf_op jit(solution)/shard_map/jit(_take)/gather | solution.py:163
  216.7 5.8 %select_select_fusion = f32[32,32,1280]{2,0,1:T(8,128)} fusion(f32[32,32,1280]{2,0,1:T(8,128)} %copy.62, pred[32,1280]{1,0:T(8,128)(4,1)S(1)} %fusion.27, pred[1280]{0:T(1024)(128)(4,1)S(1)} %iota_compare_fusion), kind=kLoop, calls=%fused_computation.2 | loop fusion | flops 2621440 | bytes 10528000 | tf_op jit(solution)/shard_map/jit(_where)/select_n | solution.py:165
  222.4 8.2 %all-to-all-start.1 = ((f32[16,2,4,8,1280]{4,3,2,1,0:T(8,128)}), f32[16,2,4,8,1280]{4,3,2,1,0:T(8,128)}, u32[]{:S(2)}, u32[]{:S(2)}) async-start(f32[16,2,4,8,1280]{4,3,2,1,0:T(8,128)} %bitcast.108), calls=%async_computation.1 | async-start | bytes 10485760 | tf_op jit(solution)/shard_map/all_to_all | solution.py:170
  230.6 0.1 div.385
  231.0 114.6 %all-to-all-done.1 = f32[16,2,4,8,1280]{4,3,2,1,0:T(8,128)} async-done(((f32[16,2,4,8,1280]{4,3,2,1,0:T(8,128)}), f32[16,2,4,8,1280]{4,3,2,1,0:T(8,128)}, u32[]{:S(2)}, u32[]{:S(2)}) %all-to-all-start.1) | async-done | bytes 5242912 | tf_op jit(solution)/shard_map/all_to_all | solution.py:170
  345.6 3.1 gather_fusion.1
  348.8 3.4 reshape.1026
  352.1 6.9 %fusion.10 = f32[8,4,8,35,128]{4,3,2,1,0:T(8,128)S(1)} fusion(f32[8,4,8,35,35]{4,3,2,1,0:T(8,128)} %reshape.1026, f32[8,128]{1,0:T(8,128)S(1)} %and_convert_fusion, f32[8]{0:T(128)S(1)} %get-tuple-element.58, f32[8]{0:T(128)S(1)} %get-tuple-element.59, f32[8]{0:T(128)S(1)} %get-tuple-element.60, f32[8]{0:T(128)S(1)} %get-tuple-element.57, ...), kind=kOutput, calls=%fused_computation.27 | convolution fusion | flops 482155520 | bytes 5850240 | tf_op jit(solution)/shard_map/tflab,tbk->tflak/dot_general | solution.py:177
  359.1 3.9 convolution_bitcast_fusion
  363.0 0.1 copy.64
  363.1 0.4 fusion.117
  363.5 0.4 copy.65
  363.9 0.3 collective-permute-start.5
  364.2 0.4 copy.67
  364.6 1.5 collective-permute-start.6
  366.0 5.4 %collective-permute-start.3 = (f32[4,8,1,128]{3,2,1,0:T(1,128)S(1)}, f32[4,8,1,128]{3,2,1,0:T(1,128)S(1)}, u32[]{:S(2)}, u32[]{:S(2)}) collective-permute-start(f32[4,8,1,128]{3,2,1,0:T(1,128)S(1)} %get-tuple-element.47), channel_id=1, source_target_pairs={{16,0},{32,16},{48,32},{64,48},{80,64},{96,80},{112,96},{128,112},... | collective-permute-start | bytes 49160 | tf_op jit(solution)/shard_map/ppermute | solution.py:24
  371.4 1.9 collective-permute-start.4
  373.3 0.4 slice_reduce_fusion.2
  373.8 0.4 copy.66
  374.2 1.4 copy.68
  375.6 3.6 collective-permute-done.4
  379.2 2.1 fusion.7
  381.3 1.4 fusion.115
  382.7 1.6 copy.69
  384.3 0.4 copy.71
  384.6 1.8 collective-permute-start.10
  386.4 2.5 collective-permute-start.7
  388.9 3.4 collective-permute-start.8
  392.3 0.4 copy.70
  392.7 1.4 copy.72
  394.1 2.5 collective-permute-done.8
  396.6 2.1 fusion.3
  398.7 0.3 subtract_dynamic-update-slice_fusion
  399.1 0.1 fusion.68
  399.2 0.1 fusion.67
  399.3 0.1 fusion.66
  399.4 1.0 copy-done.3
  400.3 0.7 constant_dynamic-update-slice_fusion
  (45 shorter events, 0.7 us)
Async XLA Ops:
  4.0 20.7 %all-to-all-start = ((s32[16,2,5]{2,1,0:T(2,128)}), s32[16,2,5]{2,1,0:T(2,128)S(1)}, u32[]{:S(2)}, u32[]{:S(2)}) async-start(s32[16,2,5]{2,1,0:T(2,128)} %bitcast.5), calls=%async_computation | async-start | bytes 32768 | tf_op jit(solution)/shard_map/all_to_all | solution.py:155
  14.8 18.2 %collective-permute-start = (f32[4,8,32,128]{3,2,1,0:T(8,128)}, f32[4,8,32,128]{3,2,1,0:T(8,128)S(1)}, u32[]{:S(2)}, u32[]{:S(2)}) collective-permute-start(f32[4,8,32,128]{3,2,1,0:T(8,128)} %get-tuple-element.51), channel_id=1, source_target_pairs={{0,16},{16,32},{32,48},{48,64},{64,80},{80,96},{96,112},{112,128},... | collective-permute-start | bytes 1572872 | tf_op jit(solution)/shard_map/ppermute | solution.py:21
  18.3 16.7 %collective-permute-start.1 = (f32[4,8,32,128]{3,2,1,0:T(8,128)}, f32[4,8,32,128]{3,2,1,0:T(8,128)S(1)}, u32[]{:S(2)}, u32[]{:S(2)}) collective-permute-start(f32[4,8,32,128]{3,2,1,0:T(8,128)} %get-tuple-element.52), channel_id=1, source_target_pairs={{16,0},{32,16},{48,32},{64,48},{80,64},{96,80},{112,96},{128,112},... | collective-permute-start | bytes 1572872 | tf_op jit(solution)/shard_map/ppermute | solution.py:24
  36.9 8.4 %copy-start = (f32[4,8,32,128]{2,3,1,0:T(8,128)S(1)}, f32[4,8,32,128]{2,3,1,0:T(8,128)}, u32[]{:S(2)}) copy-start(f32[4,8,32,128]{2,3,1,0:T(8,128)} %copy.57) | copy-start | bytes 1572868
  36.9 8.4 %copy-start.1 = (f32[4,8,32,128]{2,3,1,0:T(8,128)S(1)}, f32[4,8,32,128]{2,3,1,0:T(8,128)}, u32[]{:S(2)}) copy-start(f32[4,8,32,128]{2,3,1,0:T(8,128)} %copy.59) | copy-start | bytes 1572868
  38.6 6.7 %collective-permute-start.2 = (f32[4,8,128,32]{2,3,1,0:T(8,128)S(1)}, f32[4,8,128,32]{2,3,1,0:T(8,128)S(1)}, u32[]{:S(2)}, u32[]{:S(2)}) collective-permute-start(f32[4,8,128,32]{2,3,1,0:T(8,128)S(1)} %pad_maximum_fusion.9), channel_id=1, source_target_pairs={{0,15},{1,0},{2,1},{3,2},{4,3},{5,4},{6,5},{7,6},{8,7},{9,8},{10,9... | collective-permute-start | bytes 1572872 | tf_op jit(solution)/shard_map/ppermute | solution.py:31
  222.4 8.2 %copy-start.4 = (s32[1,1,8,2]{2,3,1,0:T(2,128)S(1)}, s32[1,1,8,2]{2,3,1,0:T(2,128)}, u32[]{:S(2)}) copy-start(s32[1,1,8,2]{2,3,1,0:T(2,128)} %param.15) | copy-start | bytes 196
  222.4 8.3 %copy-start.2 = (f32[4,7]{1,0:T(4,128)S(1)}, f32[4,7]{1,0:T(4,128)}, u32[]{:S(2)}) copy-start(f32[4,7]{1,0:T(4,128)} %param.10) | copy-start | bytes 340
  222.4 8.4 %copy-start.6 = (s32[1,1,8,1]{2,3,1,0:T(1,128)S(1)}, s32[1,1,8,1]{2,3,1,0:T(1,128)}, u32[]{:S(2)}) copy-start(s32[1,1,8,1]{2,3,1,0:T(1,128)} %param.11) | copy-start | bytes 100
  222.4 123.2 %all-to-all-start.1 = ((f32[16,2,4,8,1280]{4,3,2,1,0:T(8,128)}), f32[16,2,4,8,1280]{4,3,2,1,0:T(8,128)}, u32[]{:S(2)}, u32[]{:S(2)}) async-start(f32[16,2,4,8,1280]{4,3,2,1,0:T(8,128)} %bitcast.108), calls=%async_computation.1 | async-start | bytes 10485760 | tf_op jit(solution)/shard_map/all_to_all | solution.py:170
  363.9 9.9 %collective-permute-start.5 = (f32[4,8,64,1]{2,1,3,0:T(8,128)S(1)}, f32[4,8,64,1]{2,1,3,0:T(8,128)S(1)}, u32[]{:S(2)}, u32[]{:S(2)}) collective-permute-start(f32[4,8,64,1]{2,1,3,0:T(8,128)S(1)} %copy.65), channel_id=1, source_target_pairs={{0,1},{1,2},{2,3},{3,4},{4,5},{5,6},{6,7},{7,8},{8,9},{9,10},{10,1... | collective-permute-start | bytes 24584 | tf_op jit(solution)/shard_map/ppermute | solution.py:21
  364.6 9.6 %collective-permute-start.6 = (f32[4,8,64,1]{2,1,3,0:T(8,128)S(1)}, f32[4,8,64,1]{2,1,3,0:T(8,128)S(1)}, u32[]{:S(2)}, u32[]{:S(2)}) collective-permute-start(f32[4,8,64,1]{2,1,3,0:T(8,128)S(1)} %copy.67), channel_id=1, source_target_pairs={{1,0},{2,1},{3,2},{4,3},{5,4},{6,5},{7,6},{8,7},{9,8},{10,9},{11,1... | collective-permute-start | bytes 24584 | tf_op jit(solution)/shard_map/ppermute | solution.py:24
  366.0 9.6 %collective-permute-start.3 = (f32[4,8,1,128]{3,2,1,0:T(1,128)S(1)}, f32[4,8,1,128]{3,2,1,0:T(1,128)S(1)}, u32[]{:S(2)}, u32[]{:S(2)}) collective-permute-start(f32[4,8,1,128]{3,2,1,0:T(1,128)S(1)} %get-tuple-element.47), channel_id=1, source_target_pairs={{16,0},{32,16},{48,32},{64,48},{80,64},{96,80},{112,96},{128,112},... | collective-permute-start | bytes 49160 | tf_op jit(solution)/shard_map/ppermute | solution.py:24
  371.4 7.7 %collective-permute-start.4 = (f32[4,8,1,128]{3,2,1,0:T(1,128)S(1)}, f32[4,8,1,128]{3,2,1,0:T(1,128)S(1)}, u32[]{:S(2)}, u32[]{:S(2)}) collective-permute-start(f32[4,8,1,128]{3,2,1,0:T(1,128)S(1)} %get-tuple-element.48), channel_id=1, source_target_pairs={{0,16},{16,32},{32,48},{48,64},{64,80},{80,96},{96,112},{112,128},... | collective-permute-start | bytes 49160 | tf_op jit(solution)/shard_map/ppermute | solution.py:21
  381.3 15.3 %copy-start.5 = (f32[4,8]{1,0:T(4,128)S(1)}, f32[4,8]{1,0:T(4,128)}, u32[]{:S(2)}) copy-start(f32[4,8]{1,0:T(4,128)} %param.9) | copy-start | bytes 388
  384.2 8.1 %collective-permute-start.9 = (f32[4,8,64,1]{2,1,3,0:T(8,128)S(1)}, f32[4,8,64,1]{2,1,3,0:T(8,128)S(1)}, u32[]{:S(2)}, u32[]{:S(2)}) collective-permute-start(f32[4,8,64,1]{2,1,3,0:T(8,128)S(1)} %copy.69), channel_id=1, source_target_pairs={{0,1},{1,2},{2,3},{3,4},{4,5},{5,6},{6,7},{7,8},{8,9},{9,10},{10,1... | collective-permute-start | bytes 24584 | tf_op jit(solution)/shard_map/ppermute | solution.py:21
  384.6 8.1 %collective-permute-start.10 = (f32[4,8,64,1]{2,1,3,0:T(8,128)S(1)}, f32[4,8,64,1]{2,1,3,0:T(8,128)S(1)}, u32[]{:S(2)}, u32[]{:S(2)}) collective-permute-start(f32[4,8,64,1]{2,1,3,0:T(8,128)S(1)} %copy.71), channel_id=1, source_target_pairs={{1,0},{2,1},{3,2},{4,3},{5,4},{6,5},{7,6},{8,7},{9,8},{10,9},{11,1... | collective-permute-start | bytes 24584 | tf_op jit(solution)/shard_map/ppermute | solution.py:24
  386.4 7.7 %collective-permute-start.7 = (f32[4,8,1,128]{3,2,1,0:T(1,128)S(1)}, f32[4,8,1,128]{3,2,1,0:T(1,128)S(1)}, u32[]{:S(2)}, u32[]{:S(2)}) collective-permute-start(f32[4,8,1,128]{3,2,1,0:T(1,128)S(1)} %get-tuple-element.43), channel_id=1, source_target_pairs={{16,0},{32,16},{48,32},{64,48},{80,64},{96,80},{112,96},{128,112},... | collective-permute-start | bytes 49160 | tf_op jit(solution)/shard_map/ppermute | solution.py:24
  388.9 7.7 %collective-permute-start.8 = (f32[4,8,1,128]{3,2,1,0:T(1,128)S(1)}, f32[4,8,1,128]{3,2,1,0:T(1,128)S(1)}, u32[]{:S(2)}, u32[]{:S(2)}) collective-permute-start(f32[4,8,1,128]{3,2,1,0:T(1,128)S(1)} %get-tuple-element.44), channel_id=1, source_target_pairs={{0,16},{16,32},{32,48},{48,64},{64,80},{80,96},{96,112},{112,128},... | collective-permute-start | bytes 49160 | tf_op jit(solution)/shard_map/ppermute | solution.py:21
  399.4 1.0 copy-start.3
where the time goes:
time: 406 us; the launch traced here: 401 us
  local copies, waits for them, and re-layouts  194 us (48%)
  waiting for transfers between devices  135 us (33%)
  starting transfers between devices  41.4 us (10%)
  other arithmetic  19.7 us (5%)
  matrix products  10.9 us (3%)
    gather x2, local copies, waits for them, and re-layouts, body(): picked = jnp.take(ext_flat, flat_index.reshape(-1), axis=1)  153 us
    all_to_all x1, waiting for transfers between devices, body(): lax.all_to_all(gathered, 'lon', split_axis=0, concat_axis=0, tiled=True)  115 us
    ppermute x5, starting transfers between devices, padded(): lax.ppermute(lax.slice_in_dim(block, 0, width, axis=dim), axis, backward)  15.5 us
    ppermute x5, waiting for transfers between devices, padded(): lax.ppermute(lax.slice_in_dim(block, block.shape[dim] - width, None, axis...  13.8 us
    reshape x2, local copies, waits for them, and re-layouts, body(): ext_flat = extended.reshape(fcount * levels, extended.shape[2] * ext_width)  11 us
    ppermute x5, starting transfers between devices, padded(): lax.ppermute(lax.slice_in_dim(block, block.shape[dim] - width, None, axis...  9.08 us
    all_to_all x1, starting transfers between devices, body(): lax.all_to_all(request_table, 'lon', split_axis=0, concat_axis=0, tiled=T...  8.59 us
    all_to_all x1, starting transfers between devices, body(): lax.all_to_all(gathered, 'lon', split_axis=0, concat_axis=0, tiled=True)  8.18 us
  transfers between devices with their start and end apart: 13, of which 5 were waited for; matrix products, arithmetic and copies ran while one was open for 3% of the time, Pallas kernels for 0%

commit v1 on v0

v1 whole, which is shorter than its diff:
```python
import functools

import jax
import jax.numpy as jnp
from jax import lax
from jax.experimental import pallas as pl
from jax.experimental.pallas import tpu as pltpu
from jax.sharding import Mesh, PartitionSpec as P

TILE = 32
FRACS = 16
LANES = 128
INFO_ROWS = 8
PAIR = 2


def cubic_weights(fraction_index):
    fraction = fraction_index.astype(jnp.float32) / FRACS
    return (
        -fraction * (fraction - 1.0) * (fraction - 2.0) / 6.0,
        (fraction + 1.0) * (fraction - 1.0) * (fraction - 2.0) / 2.0,
        -(fraction + 1.0) * fraction * (fraction - 2.0) / 2.0,
        (fraction + 1.0) * fraction * (fraction - 1.0) / 6.0,
    )


def pack_kernel(tile_cols, row_limits, fields_ref, place_ref, owner_ref, row_ref, col_ref, shifts_ref, fracs_ref, out_ref):
    cells = fields_ref.shape[1]
    out_ref[:, :cells, :] = fields_ref[...]
    first_row = place_ref[0]
    group_row = place_ref[1]
    shape = (INFO_ROWS, LANES)
    lane = lax.broadcasted_iota(jnp.int32, shape, 1)
    tile = lax.broadcasted_iota(jnp.int32, shape, 0)

    def wide(value):
        return jnp.broadcast_to(value, shape)

    dep_tile = jnp.clip(first_row + wide(row_ref[...]), row_limits[0], row_limits[1])
    row_start = TILE * (dep_tile - group_row) + wide(shifts_ref[:, 0:1]) - 1
    dep_col = wide(col_ref[...])
    last = (dep_col == tile_cols - 1).astype(jnp.int32)
    chunk = wide(owner_ref[...]) + last * row_limits[2]
    lane_start = TILE * (dep_col - last) + wide(shifts_ref[:, 1:2]) - 1
    turn = LANES + TILE * lax.rem(tile, tile_cols) - lane_start
    info = jnp.where(lane == 0, row_start, jnp.where(lane == 1, chunk, turn)).astype(jnp.float32)
    for which in range(2):
        weights = cubic_weights(wide(fracs_ref[:, which : which + 1]))
        for tap in range(4):
            info = jnp.where(lane == 3 + 4 * which + tap, weights[tap], info)
    for block in range(out_ref.shape[0]):
        out_ref[block, cells:, :] = info


def interpolate_kernel(info_ref, blocks_ref, north_ref, south_ref, phi_ref, top_ref, bottom_ref, ext_ref, sem):
    chunks, halo = north_ref.shape[0], north_ref.shape[1]
    cells = phi_ref.shape[1] // PAIR
    tile_rows = cells // TILE
    tile_cols = LANES // TILE
    copies = [
        pltpu.make_async_copy(north_ref, ext_ref.at[0:chunks, 0:halo, :], sem.at[0]),
        pltpu.make_async_copy(south_ref, ext_ref.at[0:chunks, halo + PAIR * cells : 2 * halo + PAIR * cells, :], sem.at[1]),
    ]
    for band in range(PAIR):
        copies.append(
            pltpu.make_async_copy(
                blocks_ref.at[band * chunks : (band + 1) * chunks, 0:cells, :],
                ext_ref.at[0:chunks, halo + band * cells : halo + (band + 1) * cells, :],
                sem.at[2 + band],
            )
        )
    for copy in copies:
        copy.start()
    for copy in copies:
        copy.wait()
    rows = ext_ref.shape[1]
    lane_rows = lax.broadcasted_iota(jnp.int32, (rows, LANES), 1)

    def shifted(chunk, carry):
        after = lax.rem(chunk + 1, chunks)
        mixed = jnp.where(lane_rows < TILE, ext_ref[after], ext_ref[chunk])
        ext_ref[chunks + chunk] = pltpu.roll(mixed, LANES - TILE, 1)
        return carry

    lax.fori_loop(0, chunks, shifted, 0)
    lane = lax.broadcasted_iota(jnp.int32, (TILE, LANES), 1)
    group = lane // TILE

    def one_device(device, carry):
        band = device // chunks
        chunk_out = lax.rem(device, chunks)
        for tile_row in range(tile_rows):
            taps = [None] * 4
            col_weights = [None] * 4
            for tile_col in range(tile_cols):
                tile = tile_row * tile_cols + tile_col
                base = tile * 16
                start = info_ref[device, base].astype(jnp.int32)
                source = info_ref[device, base + 1].astype(jnp.int32)
                turn = info_ref[device, base + 2].astype(jnp.int32)
                total = None
                for tap in range(4):
                    part = info_ref[device, base + 3 + tap] * ext_ref[source, pl.ds(start + tap, TILE), :]
                    total = part if total is None else total + part
                for tap in range(4):
                    turned = pltpu.roll(total, lax.bitwise_and(turn - tap, LANES - 1), 1)
                    weight = jnp.full((1, LANES), info_ref[device, base + 7 + tap], jnp.float32)
                    if tile_col == 0:
                        taps[tap] = turned
                        col_weights[tap] = weight
                    else:
                        here = group == tile_col
                        taps[tap] = jnp.where(here, turned, taps[tap])
                        col_weights[tap] = jnp.where(here[0:1], weight, col_weights[tap])
            value = col_weights[0] * taps[0]
            for tap in range(1, 4):
                value = value + col_weights[tap] * taps[tap]
            phi_ref[chunk_out, pl.ds(band * cells + tile_row * TILE, TILE), :] = value
        return carry

    lax.fori_loop(0, PAIR * chunks, one_device, 0)
    for chunk in range(chunks):
        top_ref[2 * chunk : 2 * chunk + 2, :] = phi_ref[chunk, 0:2, :]
        bottom_ref[2 * chunk : 2 * chunk + 2, :] = phi_ref[chunk, PAIR * cells - 2 : PAIR * cells, :]


PAD = 16


def diffuse_kernel(scalars_ref, phi_ref, north_ref, south_ref, psi_ref, ext_ref, lap_ref):
    chunks, rows = phi_ref.shape[0], phi_ref.shape[1]
    cells = rows // PAIR
    coef, has_north, has_south = scalars_ref[0], scalars_ref[1], scalars_ref[2]

    for chunk in range(chunks):
        ext_ref[chunk, 0:PAD, :] = jnp.zeros((PAD, LANES), jnp.float32)
        ext_ref[chunk, PAD + rows :, :] = jnp.zeros((PAD, LANES), jnp.float32)
        ext_ref[chunk, PAD : PAD + rows, :] = phi_ref[chunk]
        ext_ref[chunk, PAD - 2 : PAD, :] = north_ref[2 * chunk : 2 * chunk + 2, :]
        ext_ref[chunk, PAD + rows : PAD + rows + 2, :] = south_ref[2 * chunk : 2 * chunk + 2, :]

    def laplacian(ref, chunk, first, count):
        lane = lax.broadcasted_iota(jnp.int32, (count, LANES), 1)
        west = lax.rem(chunk + chunks - 1, chunks)
        east = lax.rem(chunk + 1, chunks)
        here = ref[chunk, first : first + count, :]
        from_west = pltpu.roll(jnp.where(lane == LANES - 1, ref[west, first : first + count, :], here), 1, 1)
        from_east = pltpu.roll(jnp.where(lane == 0, ref[east, first : first + count, :], here), LANES - 1, 1)
        beside = ref[chunk, first + 1 : first + 1 + count, :] + ref[chunk, first - 1 : first - 1 + count, :] + from_west + from_east
        return beside - 4.0 * here

    def first_pass(chunk, carry):
        lap_ref[chunk, PAD - 8 : PAD, :] = laplacian(ext_ref, chunk, PAD - 8, 8) * has_north
        lap_ref[chunk, PAD : PAD + rows, :] = laplacian(ext_ref, chunk, PAD, rows)
        lap_ref[chunk, PAD + rows : PAD + rows + 8, :] = laplacian(ext_ref, chunk, PAD + rows, 8) * has_south
        return carry

    def second_pass(chunk, carry):
        psi = phi_ref[chunk] - coef * laplacian(lap_ref, chunk, PAD, rows)
        for band in range(PAIR):
            psi_ref[band * chunks + chunk] = psi[band * cells : (band + 1) * cells]
        return carry

    lax.fori_loop(0, chunks, first_pass, 0)
    lax.fori_loop(0, chunks, second_pass, 0)


def vertical_kernel(levels, lower_ref, upper_ref, inverse_ref, psi_ref, out_ref):
    field = pl.program_id(0)
    sweep = []
    for level in range(levels):
        rhs = psi_ref[level]
        if level:
            rhs = rhs + lower_ref[field, level] * sweep[-1]
        sweep.append(rhs * inverse_ref[field, level])
    value = sweep[-1]
    out_ref[0, levels - 1] = value
    for level in range(levels - 2, -1, -1):
        value = sweep[level] - upper_ref[field, level] * value
        out_ref[0, level] = value


def vertical_tables(vert_coef):
    fcount = vert_coef.shape[0]
    levels = vert_coef.shape[1] + 1
    zero_column = jnp.zeros((fcount, 1), jnp.float32)
    lower_coef = jnp.concatenate([zero_column, vert_coef], axis=1)
    upper_coef = jnp.concatenate([vert_coef, zero_column], axis=1)
    diagonal = 1.0 + lower_coef + upper_coef
    uppers, inverses = [], []
    for level in range(levels):
        denominator = diagonal[:, level]
        if level:
            denominator = denominator + lower_coef[:, level] * uppers[-1]
        inverses.append(1.0 / denominator)
        uppers.append(-upper_coef[:, level] / denominator)
    return lower_coef, jnp.stack(uppers, axis=1), jnp.stack(inverses, axis=1)


SMEM = pltpu.MemorySpace.SMEM
VMEM = pltpu.MemorySpace.VMEM


def smem():
    return pl.BlockSpec(memory_space=SMEM)


def vmem():
    return pl.BlockSpec(memory_space=VMEM)


def anywhere():
    return pl.BlockSpec(memory_space=pl.ANY)


def body(fields, hyper_coef, vert_coef, dep_owner, dep_row, dep_col, shifts, fracs):
    fcount, levels, cells, width = fields.shape
    count = fcount * levels
    chunks = lax.axis_size("lon")
    groups = lax.axis_size("group")
    tile_rows = cells // TILE
    tile_cols = width // TILE
    tiles = tile_rows * tile_cols
    group = lax.axis_index("group")
    band = group * PAIR + lax.axis_index("part")
    rows = PAIR * cells
    f32 = jnp.float32
    limit = pltpu.CompilerParams(vmem_limit_bytes=48 * 1024 * 1024)

    place = jnp.stack([band * tile_rows - 1, group * PAIR * tile_rows - 1]).astype(jnp.int32)
    blocks = pl.pallas_call(
        functools.partial(pack_kernel, tile_cols, (0, groups * PAIR * tile_rows - 2, chunks)),
        out_shape=jax.ShapeDtypeStruct((count, cells + INFO_ROWS, width), f32),
        in_specs=[vmem(), smem(), vmem(), vmem(), vmem(), vmem(), vmem()],
        out_specs=vmem(),
        compiler_params=limit,
    )(
        fields.reshape(count, cells, width),
        place,
        dep_owner.reshape(tiles, 1),
        dep_row.reshape(tiles, 1),
        dep_col.reshape(tiles, 1),
        shifts.reshape(tiles, 2),
        fracs.reshape(tiles, 2),
    )
    blocks = lax.all_to_all(blocks, ("part", "lon"), 0, 0, tiled=True)
    southward = [(i, i + 1) for i in range(groups - 1)]
    northward = [(i + 1, i) for i in range(groups - 1)]
    north = lax.ppermute(blocks[(PAIR - 1) * chunks :, cells - TILE : cells, :], "group", southward)
    south = lax.ppermute(blocks[:chunks, :TILE, :], "group", northward)
    info = blocks[:, cells : cells + tiles, :16].reshape(PAIR * chunks, tiles * 16)
    edge = jax.ShapeDtypeStruct((2 * chunks, width), f32)
    phi, top, bottom = pl.pallas_call(
        interpolate_kernel,
        out_shape=(jax.ShapeDtypeStruct((chunks, rows, width), f32), edge, edge),
        in_specs=[smem(), anywhere(), anywhere(), anywhere()],
        out_specs=(vmem(), vmem(), vmem()),
        scratch_shapes=[
            pltpu.VMEM((2 * chunks, rows + 2 * TILE, width), f32),
            pltpu.SemaphoreType.DMA((2 + PAIR,)),
        ],
        compiler_params=limit,
    )(info, blocks, north, south)
    above = lax.ppermute(bottom, "group", southward)
    below = lax.ppermute(top, "group", northward)
    member = lax.axis_index("part") * chunks + lax.axis_index("lon")
    scalars = jnp.stack(
        [
            lax.dynamic_index_in_dim(hyper_coef.reshape(-1), member, 0, keepdims=False),
            (group > 0).astype(f32),
            (group < groups - 1).astype(f32),
        ]
    )
    psi = pl.pallas_call(
        diffuse_kernel,
        out_shape=jax.ShapeDtypeStruct((count, cells, width), f32),
        in_specs=[smem(), vmem(), vmem(), vmem()],
        out_specs=vmem(),
        scratch_shapes=[
            pltpu.VMEM((chunks, rows + 2 * PAD, width), f32),
            pltpu.VMEM((chunks, rows + 2 * PAD, width), f32),
        ],
        compiler_params=limit,
    )(scalars, phi, above, below)
    psi = lax.all_to_all(psi, ("part", "lon"), 0, 0, tiled=True)
    lower, upper, inverse = vertical_tables(vert_coef)
    return pl.pallas_call(
        functools.partial(vertical_kernel, levels),
        grid=(fcount,),
        out_shape=jax.ShapeDtypeStruct((fcount, levels, cells, width), f32),
        in_specs=[
            smem(),
            smem(),
            smem(),
            pl.BlockSpec((levels, cells, width), lambda field: (field, 0, 0)),
        ],
        out_specs=pl.BlockSpec((1, levels, cells, width), lambda field: (field, 0, 0, 0)),
        compiler_params=limit,
    )(lower, upper, inverse, psi)


def solution(mesh):
    lat, lon = mesh.shape["lat"], mesh.shape["lon"]
    grouped = Mesh(mesh.devices.reshape(lat // PAIR, PAIR, lon), ("group", "part", "lon"))
    bands = ("group", "part")
    cells = P(None, None, bands, "lon")
    tiles = P(bands, "lon", None, None)
    return jax.shard_map(
        body,
        mesh=grouped,
        in_specs=(cells, P(), P(), tiles, tiles, tiles, tiles, tiles),
        out_specs=cells,
        check_vma=False,
    )
```

time: 406 us -> 127 us (0.31)
  local copies, waits for them, and re-layouts: 194 us -> 6.05 us
  waiting for transfers between devices: 135 us -> 38.8 us
  blocking collectives: 0 us -> 41.3 us
  starting transfers between devices: 41.4 us -> 21.3 us
  other arithmetic: 19.7 us -> 1.14 us
  Pallas kernels: 0 us -> 17.3 us
  matrix products: 10.9 us -> 0 us
    gather x3 -> x0, local copies, waits for them, and re-layouts: 156 us -> none  [the longest x2 153 us: body(): picked = jnp.take(ext_flat, flat_index.reshape(-1), axis=1)]
    all_to_all x2 -> x1, waiting for transfers between devices: 115 us -> 28.5 us  [body(): psi = lax.all_to_all(psi, ('part', 'lon'), 0, 0, tiled=True)]
    all_to_all x0 -> x1, blocking collectives: none -> 41.3 us  [body(): blocks = lax.all_to_all(blocks, ('part', 'lon'), 0, 0, tiled=True)]
    pallas_call x0 -> x4, Pallas kernels: none -> 17.3 us  [the longest x1 9.29 us: body(): pl.pallas_call(interpolate_kernel, out_shape=(jax.ShapeDtypeStruct((chunk...]
    all_to_all x2 -> x1, starting transfers between devices: 16.8 us -> 4.79 us  [body(): psi = lax.all_to_all(psi, ('part', 'lon'), 0, 0, tiled=True)]
    dot_general x2 -> x0, matrix products: 10.9 us -> none  [the longest x1 6.93 us: body(): jnp.einsum('tflab,tbk->tflak', own_windows, column_place, precision=HIGHE...]
    reshape x3 -> x7, local copies, waits for them, and re-layouts: 14.3 us -> 3.83 us  [the longest x1 0.75 us: body(): shifts.reshape(tiles, 2)]
    ppermute x11 -> x4, waiting for transfers between devices: 20.3 us -> 10.3 us  [the longest x1 6.2 us: body(): lax.ppermute(blocks[(PAIR - 1) * chunks:, cells - TILE:cells, :], 'group'...]
  transfers between devices with their start and end apart: 13 -> 5, of which waited for: 5 -> 4; matrix products, arithmetic and copies ran while one was open for 3% -> 2% of each run, Pallas kernels for 0% -> 0%
where the time goes in v1:
time: 127 us; the launch traced here: 126 us
  blocking collectives  41.3 us (33%)
  waiting for transfers between devices  38.8 us (31%)
  starting transfers between devices  21.3 us (17%)
  Pallas kernels  17.3 us (14%)
  local copies, waits for them, and re-layouts  6.05 us (5%)
    all_to_all x1, blocking collectives, body(): blocks = lax.all_to_all(blocks, ('part', 'lon'), 0, 0, tiled=True)  41.3 us
    all_to_all x1, waiting for transfers between devices, body(): psi = lax.all_to_all(psi, ('part', 'lon'), 0, 0, tiled=True)  28.5 us
    pallas_call x1, Pallas kernels, body(): pl.pallas_call(interpolate_kernel, out_shape=(jax.ShapeDtypeStruct((chunk...  9.29 us
    ppermute x1, waiting for transfers between devices, body(): lax.ppermute(blocks[(PAIR - 1) * chunks:, cells - TILE:cells, :], 'group'...  6.2 us
    pallas_call x1, Pallas kernels, body(): pl.pallas_call(diffuse_kernel, out_shape=jax.ShapeDtypeStruct((count, cel...  5.11 us
    ppermute x1, starting transfers between devices, body(): lax.ppermute(blocks[(PAIR - 1) * chunks:, cells - TILE:cells, :], 'group'...  4.81 us
    all_to_all x1, starting transfers between devices, body(): psi = lax.all_to_all(psi, ('part', 'lon'), 0, 0, tiled=True)  4.79 us
    ppermute x1, starting transfers between devices, body(): below = lax.ppermute(top, 'group', northward)  4.33 us
  transfers between devices with their start and end apart: 5, of which 4 were waited for; matrix products, arithmetic and copies ran while one was open for 2% of the time, Pallas kernels for 0%

profile of v1, /device:TPU:36, one launch (start us, length us, event | category | flops | bytes accessed | tf_op | source)
XLA Modules:
  0.0 126.0 jit_solution(275410497707449980)
XLA Ops:
  0.0 0.7 copy.14.owner_ref
  0.7 0.7 copy.15.row_ref
  1.5 0.7 copy.16.col_ref
  2.2 0.8 copy.17.shifts_ref
  2.9 0.8 copy.18.fracs_ref
  3.7 0.1 pad_add_fusion.1.place_ref
  3.8 0.0 copy-start
  3.8 1.2 copy-done
  5.0 0.6 shard_map.82
  5.6 0.0 copy-start.2
  5.6 41.3 %all_to_all.10.blocks_ref = f32[32,72,128]{2,1,0:T(8,128)S(1)} all-to-all(f32[32,72,128]{2,1,0:T(8,128)S(1)} %shard_map.82), channel_id=1, replica_groups=mesh['group'=8,'part'=2,'lon'=16] {'part','lon'}, dimensions={0} | all-to-all | bytes 2359296 | tf_op jit(solution)/shard_map/all_to_all | solution.py:246
  47.0 0.1 fusion
  47.0 4.8 %collective-permute-start = (f32[16,32,128]{2,1,0:T(8,128)S(1)}, f32[16,32,128]{2,1,0:T(8,128)S(1)}, u32[]{:S(2)}, u32[]{:S(2)}) collective-permute-start(f32[16,32,128]{2,1,0:T(8,128)S(1)} %get-tuple-element.20), channel_id=1, source_target_pairs={{0,32},{32,64},{64,96},{96,128},{128,160},{160,192},{192,224},{1,3... | collective-permute-start | bytes 786440 | tf_op jit(solution)/shard_map/ppermute | solution.py:249
  51.9 3.4 %collective-permute-start.1 = (f32[16,32,128]{2,1,0:T(8,128)S(1)}, f32[16,32,128]{2,1,0:T(8,128)S(1)}, u32[]{:S(2)}, u32[]{:S(2)}) collective-permute-start(f32[16,32,128]{2,1,0:T(8,128)S(1)} %get-tuple-element.19), channel_id=1, source_target_pairs={{32,0},{64,32},{96,64},{128,96},{160,128},{192,160},{224,192},{33,... | collective-permute-start | bytes 786440 | tf_op jit(solution)/shard_map/ppermute | solution.py:250
  55.3 0.0 copy-done.2
  55.3 0.1 reshape.24
  55.4 0.6 dynamic_slice.4
  56.1 0.1 copy.19
  56.2 0.1 copy.20.info_ref
  56.2 6.2 %collective-permute-done.north_ref = f32[16,32,128]{2,1,0:T(8,128)S(1)} collective-permute-done((f32[16,32,128]{2,1,0:T(8,128)S(1)}, f32[16,32,128]{2,1,0:T(8,128)S(1)}, u32[]{:S(2)}, u32[]{:S(2)}) %collective-permute-start) | collective-permute-done | bytes 262176 | tf_op jit(solution)/shard_map/ppermute | solution.py:249
  62.4 2.0 %collective-permute-done.1.south_ref = f32[16,32,128]{2,1,0:T(8,128)S(1)} collective-permute-done((f32[16,32,128]{2,1,0:T(8,128)S(1)}, f32[16,32,128]{2,1,0:T(8,128)S(1)}, u32[]{:S(2)}, u32[]{:S(2)}) %collective-permute-start.1) | collective-permute-done | bytes 262176 | tf_op jit(solution)/shard_map/ppermute | solution.py:250
  64.4 9.3 %shard_map.83 = (f32[16,128,128]{2,1,0:T(8,128)S(1)}, f32[32,128]{1,0:T(8,128)S(1)}, f32[32,128]{1,0:T(8,128)S(1)}) custom-call(f32[32,128]{1,0:T(8,128)S(1)} %copy.20.info_ref, f32[32,72,128]{2,1,0:T(8,128)S(1)} %all_to_all.10.blocks_ref, f32[16,32,128]{2,1,0:T(8,128)S(1)} %collective-permute-done.north_ref, f32[16,32,128]{2,1,0:T(8,128)S(1)} %collective-permute-done.1.south_ref), custom_call_target="tpu_custom_call" | custom-call | tf_op jit(solution)/shard_map/pallas_call | solution.py:253
  73.7 3.9 %collective-permute-start.2 = (f32[32,128]{1,0:T(8,128)S(1)}, f32[32,128]{1,0:T(8,128)S(1)}, u32[]{:S(2)}, u32[]{:S(2)}) collective-permute-start(f32[32,128]{1,0:T(8,128)S(1)} %get-tuple-element.9), channel_id=1, source_target_pairs={{0,32},{32,64},{64,96},{96,128},{128,160},{160,192},{192,224},{1,3... | collective-permute-start | bytes 49160 | tf_op jit(solution)/shard_map/ppermute | solution.py:264
  77.6 4.3 %collective-permute-start.3 = (f32[32,128]{1,0:T(8,128)S(1)}, f32[32,128]{1,0:T(8,128)S(1)}, u32[]{:S(2)}, u32[]{:S(2)}) collective-permute-start(f32[32,128]{1,0:T(8,128)S(1)} %get-tuple-element.10), channel_id=1, source_target_pairs={{32,0},{64,32},{96,64},{128,96},{160,128},{192,160},{224,192},{33,... | collective-permute-start | bytes 49160 | tf_op jit(solution)/shard_map/ppermute | solution.py:265
  81.9 0.7 pad_maximum_fusion.scalars_ref
  82.7 0.0 collective-permute-done.2.north_ref
  82.7 2.1 %collective-permute-done.3.south_ref = f32[32,128]{1,0:T(8,128)S(1)} collective-permute-done((f32[32,128]{1,0:T(8,128)S(1)}, f32[32,128]{1,0:T(8,128)S(1)}, u32[]{:S(2)}, u32[]{:S(2)}) %collective-permute-start.3) | collective-permute-done | bytes 16416 | tf_op jit(solution)/shard_map/ppermute | solution.py:265
  84.7 5.1 %shard_map.84 = f32[32,64,128]{2,1,0:T(8,128)} custom-call(f32[3]{0:T(128)S(1)} %pad_maximum_fusion.scalars_ref, f32[16,128,128]{2,1,0:T(8,128)S(1)} %get-tuple-element.8.phi_ref, f32[32,128]{1,0:T(8,128)S(1)} %collective-permute-done.2.north_ref, f32[32,128]{1,0:T(8,128)S(1)} %collective-permute-done.3.south_ref), custom_call_target="tpu_custom_call" | custom-call | tf_op jit(solution)/shard_map/pallas_call | solution.py:274
  89.9 0.0 copy-start.1
  89.9 4.8 %all-to-all-start.1 = ((f32[32,64,128]{2,1,0:T(8,128)}), f32[32,64,128]{2,1,0:T(8,128)S(1)}, u32[]{:S(2)}, u32[]{:S(2)}) async-start(f32[32,64,128]{2,1,0:T(8,128)} %shard_map.84), calls=%async_computation.1 | async-start | bytes 2097152 | tf_op jit(solution)/shard_map/all_to_all | solution.py:285
  94.7 0.0 copy-done.1
  94.7 0.1 pad_add_fusion
  94.7 0.1 broadcast_divide_fusion
  94.9 0.1 broadcast_divide_fusion.1
  95.0 0.1 stack.22.upper_ref
  95.1 0.1 broadcast_divide_fusion.6
  95.1 0.1 stack.23.inverse_ref
  95.2 28.5 %all-to-all-done.1.psi_ref = f32[32,64,128]{2,1,0:T(8,128)S(1)} async-done(((f32[32,64,128]{2,1,0:T(8,128)}), f32[32,64,128]{2,1,0:T(8,128)S(1)}, u32[]{:S(2)}, u32[]{:S(2)}) %all-to-all-start.1) | async-done | bytes 1048608 | tf_op jit(solution)/shard_map/all_to_all | solution.py:285
  123.8 2.2 %shard_map.85 = f32[4,8,64,128]{3,2,1,0:T(8,128)} custom-call(f32[4,8]{1,0:T(4,128)S(1)} %get-tuple-element.29.lower_ref, f32[4,8]{1,0:T(4,128)S(1)} %stack.22.upper_ref, f32[4,8]{1,0:T(4,128)S(1)} %stack.23.inverse_ref, f32[32,64,128]{2,1,0:T(8,128)S(1)} %all-to-all-done.1.psi_ref), custom_call_target="tpu_custom_call" | custom-call | tf_op jit(solution)/shard_map/pallas_call | solution.py:287
  (1 shorter events, 0.0 us)
Async XLA Ops:
  3.8 1.2 copy-start
  5.6 49.7 %copy-start.2 = (f32[4,8]{1,0:T(4,128)S(1)}, f32[4,8]{1,0:T(4,128)}, u32[]{:S(2)}) copy-start(f32[4,8]{1,0:T(4,128)} %param.9) | copy-start | bytes 388
  47.0 15.4 %collective-permute-start = (f32[16,32,128]{2,1,0:T(8,128)S(1)}, f32[16,32,128]{2,1,0:T(8,128)S(1)}, u32[]{:S(2)}, u32[]{:S(2)}) collective-permute-start(f32[16,32,128]{2,1,0:T(8,128)S(1)} %get-tuple-element.20), channel_id=1, source_target_pairs={{0,32},{32,64},{64,96},{96,128},{128,160},{160,192},{192,224},{1,3... | collective-permute-start | bytes 786440 | tf_op jit(solution)/shard_map/ppermute | solution.py:249
  51.9 12.5 %collective-permute-start.1 = (f32[16,32,128]{2,1,0:T(8,128)S(1)}, f32[16,32,128]{2,1,0:T(8,128)S(1)}, u32[]{:S(2)}, u32[]{:S(2)}) collective-permute-start(f32[16,32,128]{2,1,0:T(8,128)S(1)} %get-tuple-element.19), channel_id=1, source_target_pairs={{32,0},{64,32},{96,64},{128,96},{160,128},{192,160},{224,192},{33,... | collective-permute-start | bytes 786440 | tf_op jit(solution)/shard_map/ppermute | solution.py:250
  73.7 9.0 %collective-permute-start.2 = (f32[32,128]{1,0:T(8,128)S(1)}, f32[32,128]{1,0:T(8,128)S(1)}, u32[]{:S(2)}, u32[]{:S(2)}) collective-permute-start(f32[32,128]{1,0:T(8,128)S(1)} %get-tuple-element.9), channel_id=1, source_target_pairs={{0,32},{32,64},{64,96},{96,128},{128,160},{160,192},{192,224},{1,3... | collective-permute-start | bytes 49160 | tf_op jit(solution)/shard_map/ppermute | solution.py:264
  77.6 7.1 %collective-permute-start.3 = (f32[32,128]{1,0:T(8,128)S(1)}, f32[32,128]{1,0:T(8,128)S(1)}, u32[]{:S(2)}, u32[]{:S(2)}) collective-permute-start(f32[32,128]{1,0:T(8,128)S(1)} %get-tuple-element.10), channel_id=1, source_target_pairs={{32,0},{64,32},{96,64},{128,96},{160,128},{192,160},{224,192},{33,... | collective-permute-start | bytes 49160 | tf_op jit(solution)/shard_map/ppermute | solution.py:265
  89.9 4.8 %copy-start.1 = (f32[4,7]{1,0:T(4,128)S(1)}, f32[4,7]{1,0:T(4,128)}, u32[]{:S(2)}) copy-start(f32[4,7]{1,0:T(4,128)} %param.10) | copy-start | bytes 340
  89.9 33.9 %all-to-all-start.1 = ((f32[32,64,128]{2,1,0:T(8,128)}), f32[32,64,128]{2,1,0:T(8,128)S(1)}, u32[]{:S(2)}, u32[]{:S(2)}) async-start(f32[32,64,128]{2,1,0:T(8,128)} %shard_map.84), calls=%async_computation.1 | async-start | bytes 2097152 | tf_op jit(solution)/shard_map/all_to_all | solution.py:285

commit v2 on v1

v2 whole, which is shorter than its diff:
```python
import functools

import jax
import jax.numpy as jnp
from jax import lax
from jax.experimental import pallas as pl
from jax.experimental.pallas import tpu as pltpu
from jax.sharding import Mesh, PartitionSpec as P

TILE = 32
FRACS = 16
LANES = 128
INFO_ROWS = 8
PAIR = 2
TAPS = 4
SPAN = 40


def cubic_weights(fraction_index):
    fraction = fraction_index.astype(jnp.float32) / FRACS
    return (
        -fraction * (fraction - 1.0) * (fraction - 2.0) / 6.0,
        (fraction + 1.0) * (fraction - 1.0) * (fraction - 2.0) / 2.0,
        -(fraction + 1.0) * fraction * (fraction - 2.0) / 2.0,
        (fraction + 1.0) * fraction * (fraction - 1.0) / 6.0,
    )


def swapped():
    return lax.rem(lax.axis_index("group"), 2)


def pack_kernel(
    tile_rows, tile_cols, last_row, fields_ref, owner_ref, row_ref, col_ref, shifts_ref, fracs_ref, out_ref, table_ref, sem
):
    count, cells = fields_ref.shape[0], fields_ref.shape[1]
    half = count // PAIR
    swap = swapped()
    copies = []
    for part in range(PAIR):
        source = lax.bitwise_xor(part, swap) * half
        copies.append(
            pltpu.make_async_copy(
                fields_ref.at[pl.ds(source, half)], out_ref.at[part * half : (part + 1) * half, 0:cells, :], sem.at[part]
            )
        )
    for copy in copies:
        copy.start()
    tiles = owner_ref.shape[1]
    group = lax.axis_index("group")
    band = group * PAIR + lax.axis_index("part")
    table_ref[...] = jnp.zeros(table_ref.shape, jnp.int32)
    table_ref[0:1, 0:tiles] = owner_ref[...]
    table_ref[1:2, 0:tiles] = row_ref[...]
    table_ref[2:3, 0:tiles] = col_ref[...]
    table_ref[3:5, 0:tiles] = shifts_ref[...]
    table_ref[5:7, 0:tiles] = fracs_ref[...]
    table = table_ref[...]
    owner, dep_row, dep_col = table[0:1], table[1:2], table[2:3]
    shift_row, shift_col, frac_row, frac_col = table[3:4], table[4:5], table[5:6], table[6:7]
    dep_tile = jnp.clip(band * tile_rows - 1 + dep_row, 0, last_row)
    start = TILE * (dep_tile - (group * PAIR * tile_rows - 1)) + shift_row - 1
    column = TILE * dep_col + shift_col - 1
    wrapped = jnp.where(dep_col == tile_cols - 1, TILE, 0)
    position = lax.rem(lax.broadcasted_iota(jnp.int32, (1, LANES), 1), tile_cols)
    turn = lax.bitwise_and(LANES + TILE * position - column, LANES - 1)
    shape = (INFO_ROWS, LANES)
    index = lax.broadcasted_iota(jnp.int32, shape, 0)
    lane = lax.broadcasted_iota(jnp.int32, shape, 1)
    info = jnp.zeros(shape, jnp.float32)
    for place, value in enumerate(cubic_weights(frac_row) + cubic_weights(frac_col)):
        info = jnp.where(index == place, value, info)
    places = jnp.zeros(shape, jnp.int32)
    for place, value in enumerate((start, owner, wrapped, turn)):
        places = jnp.where(index == place, value, places)
    info = jnp.where(lane < tiles, info, pltpu.roll(places.astype(jnp.float32), tiles, 1))
    for block in range(count):
        out_ref[block, cells:, :] = info
    for copy in copies:
        copy.wait()


def interpolate_kernel(
    places_ref, blocks_ref, north_ref, south_ref, phi_ref, top_ref, bottom_ref, ext_ref, pass_ref, sem
):
    chunks, halo = north_ref.shape[0], north_ref.shape[1]
    cells = phi_ref.shape[1] // PAIR
    tile_rows = cells // TILE
    tile_cols = LANES // TILE
    tiles = tile_rows * tile_cols
    copies = [
        pltpu.make_async_copy(north_ref, ext_ref.at[:, 0:halo, :], sem.at[0]),
        pltpu.make_async_copy(south_ref, ext_ref.at[:, halo + PAIR * cells : 2 * halo + PAIR * cells, :], sem.at[1]),
    ]
    for band in range(PAIR):
        copies.append(
            pltpu.make_async_copy(
                blocks_ref.at[band * chunks : (band + 1) * chunks, 0:cells, :],
                ext_ref.at[:, halo + band * cells : halo + (band + 1) * cells, :],
                sem.at[2 + band],
            )
        )
    for copy in copies:
        copy.start()
    for copy in copies:
        copy.wait()
    lane = lax.broadcasted_iota(jnp.int32, (SPAN, LANES), 1)
    lane_info = lax.broadcasted_iota(jnp.int32, (INFO_ROWS, LANES), 1)
    first_even = lane < 48
    first_odd = (lane >= 16) & (lane < 80)
    even_group = [lax.bitwise_and(lane - tap, TILE) == 0 for tap in range(TAPS)]

    def columns(device, tile_row, slot):
        own = lane_info // TILE + tile_row * tile_cols
        weights = jnp.take_along_axis(blocks_ref[device, cells:, :], own, axis=1)

        def window(tile_col):
            tile = tile_row * tile_cols + tile_col
            start, source, wrapped, turn = (places_ref[device, place * tiles + tile] for place in range(4))
            after = lax.rem(source + 1, chunks)
            rows = pl.ds(start, SPAN)
            return pltpu.roll(jnp.where(lane < wrapped, ext_ref[after, rows, :], ext_ref[source, rows, :]), turn, 1)

        evens = jnp.where(first_even, window(0), window(2))
        odds = jnp.where(first_odd, window(1), window(3))
        total = None
        for tap in range(TAPS):
            value = jnp.where(even_group[tap], evens, odds)
            if tap:
                value = pltpu.roll(value, LANES - tap, 1)
            value = weights[TAPS + tap : TAPS + tap + 1] * value
            total = value if total is None else total + value
        pass_ref[slot] = total
        return weights

    def rows_of(device, tile_row, slot, weights):
        band = device // chunks
        total = None
        for tap in range(TAPS):
            value = weights[tap : tap + 1] * pass_ref[slot, tap : tap + TILE, :]
            total = value if total is None else total + value
        first = pl.multiple_of(band * cells + tile_row * TILE, TILE)
        phi_ref[lax.rem(device, chunks), pl.ds(first, TILE), :] = total

    together = pass_ref.shape[0] // tile_rows

    def step(index, carry):
        work = []
        for place in range(together):
            device = index * together + place
            for tile_row in range(tile_rows):
                slot = place * tile_rows + tile_row
                work.append((device, tile_row, slot, columns(device, tile_row, slot)))
        for item in work:
            rows_of(*item)
        return carry

    lax.fori_loop(0, PAIR * chunks // together, step, 0)
    for chunk in range(chunks):
        top_ref[2 * chunk : 2 * chunk + 2, :] = phi_ref[chunk, 0:2, :]
        bottom_ref[2 * chunk : 2 * chunk + 2, :] = phi_ref[chunk, PAIR * cells - 2 : PAIR * cells, :]


PAD = 8


def laplacian(ref, chunks, chunk, first, count):
    lane = lax.broadcasted_iota(jnp.int32, (count, LANES), 1)
    west = lax.rem(chunk + chunks - 1, chunks)
    east = lax.rem(chunk + 1, chunks)
    here = ref[chunk, first : first + count, :]
    from_west = pltpu.roll(jnp.where(lane == LANES - 1, ref[west, first : first + count, :], here), 1, 1)
    from_east = pltpu.roll(jnp.where(lane == 0, ref[east, first : first + count, :], here), LANES - 1, 1)
    beside = ref[chunk, first + 1 : first + 1 + count, :] + ref[chunk, first - 1 : first - 1 + count, :] + from_west + from_east
    return beside - 4.0 * here


def own_coef(coef_ref, half):
    levels = coef_ref.shape[1]
    member = lax.bitwise_xor(lax.axis_index("part"), swapped()) * half + lax.axis_index("lon")
    return coef_ref[member // levels, lax.rem(member, levels)]


def diffuse_kernel(coef_ref, phi_ref, psi_ref, lap_ref):
    chunks, rows = phi_ref.shape[0], phi_ref.shape[1]
    cells = rows // PAIR
    coef = own_coef(coef_ref, chunks)

    def first_pass(chunk, carry):
        lap_ref[chunk, PAD - 1 : rows - PAD + 1, :] = laplacian(phi_ref, chunks, chunk, PAD - 1, rows - 2 * PAD + 2)
        return carry

    def second_pass(chunk, carry):
        psi = phi_ref[chunk, PAD : rows - PAD, :] - coef * laplacian(lap_ref, chunks, chunk, PAD, rows - 2 * PAD)
        psi_ref[chunk, 0:PAD, :] = jnp.zeros((PAD, LANES), jnp.float32)
        psi_ref[chunk, PAD:, :] = psi[0 : cells - PAD]
        psi_ref[chunks + chunk, 0 : cells - PAD, :] = psi[cells - PAD :]
        psi_ref[chunks + chunk, cells - PAD :, :] = jnp.zeros((PAD, LANES), jnp.float32)
        return carry

    lax.fori_loop(0, chunks, first_pass, 0)
    lax.fori_loop(0, chunks, second_pass, 0)


def mend_kernel(groups, coef_ref, phi_ref, north_ref, south_ref, inner_ref, psi_ref, ext_ref, lap_ref, edge_ref, sem):
    chunks, rows = phi_ref.shape[0], phi_ref.shape[1]
    cells = rows // PAIR
    coef = own_coef(coef_ref, chunks)
    group = lax.axis_index("group")
    has_north = jnp.where(group > 0, 1.0, 0.0)
    has_south = jnp.where(group < groups - 1, 1.0, 0.0)
    zeros = jnp.zeros((PAD, LANES), jnp.float32)

    for side in range(2):
        for chunk in range(chunks):
            place = side * chunks + chunk
            ext_ref[place, 0:PAD, :] = zeros
            ext_ref[place, 4 * PAD :, :] = zeros
            if side == 0:
                ext_ref[place, PAD : 2 * PAD, :] = zeros
                ext_ref[place, 2 * PAD - 2 : 2 * PAD, :] = north_ref[2 * chunk : 2 * chunk + 2, :]
                ext_ref[place, 2 * PAD : 4 * PAD, :] = phi_ref[chunk, 0 : 2 * PAD, :]
            else:
                ext_ref[place, PAD : 3 * PAD, :] = phi_ref[chunk, rows - 2 * PAD :, :]
                ext_ref[place, 3 * PAD : 4 * PAD, :] = zeros
                ext_ref[place, 3 * PAD : 3 * PAD + 2, :] = south_ref[2 * chunk : 2 * chunk + 2, :]
    for side in range(2):
        own = pl.ds(side * chunks, chunks)
        for chunk in range(chunks):
            lap_ref[side * chunks + chunk, PAD : 4 * PAD, :] = laplacian(ext_ref.at[own], chunks, chunk, PAD, 3 * PAD)
        for chunk in range(chunks):
            place = side * chunks + chunk
            if side == 0:
                lap_ref[place, PAD : 2 * PAD, :] = lap_ref[place, PAD : 2 * PAD, :] * has_north
            else:
                lap_ref[place, 3 * PAD : 4 * PAD, :] = lap_ref[place, 3 * PAD : 4 * PAD, :] * has_south
        for chunk in range(chunks):
            twice = laplacian(lap_ref.at[own], chunks, chunk, 2 * PAD, PAD)
            here = phi_ref[chunk, 0:PAD, :] if side == 0 else phi_ref[chunk, rows - PAD :, :]
            edge_ref[side * chunks + chunk] = here - coef * twice
    copies = [
        pltpu.make_async_copy(edge_ref.at[0:chunks], psi_ref.at[0:chunks, 0:PAD, :], sem.at[0]),
        pltpu.make_async_copy(
            edge_ref.at[chunks : 2 * chunks], psi_ref.at[(PAIR - 1) * chunks :, cells - PAD : cells, :], sem.at[1]
        ),
    ]
    for copy in copies:
        copy.start()
    for copy in copies:
        copy.wait()


def vertical_kernel(levels, lower_ref, upper_ref, inverse_ref, psi_ref, out_ref):
    field = pl.program_id(0)
    source = lax.bitwise_xor(field, swapped() * (pl.num_programs(0) // PAIR)) * levels
    sweep = []
    for level in range(levels):
        rhs = psi_ref[source + level]
        if level:
            rhs = rhs + lower_ref[field, level] * sweep[-1]
        sweep.append(rhs * inverse_ref[field, level])
    value = sweep[-1]
    out_ref[0, levels - 1] = value
    for level in range(levels - 2, -1, -1):
        value = sweep[level] - upper_ref[field, level] * value
        out_ref[0, level] = value


def vertical_tables(vert_coef):
    fcount = vert_coef.shape[0]
    levels = vert_coef.shape[1] + 1
    zero_column = jnp.zeros((fcount, 1), jnp.float32)
    lower_coef = jnp.concatenate([zero_column, vert_coef], axis=1)
    upper_coef = jnp.concatenate([vert_coef, zero_column], axis=1)
    diagonal = 1.0 + lower_coef + upper_coef
    uppers, inverses = [], []
    for level in range(levels):
        denominator = diagonal[:, level]
        if level:
            denominator = denominator + lower_coef[:, level] * uppers[-1]
        inverses.append(1.0 / denominator)
        uppers.append(-upper_coef[:, level] / denominator)
    return lower_coef, jnp.stack(uppers, axis=1), jnp.stack(inverses, axis=1)


SMEM = pltpu.MemorySpace.SMEM
VMEM = pltpu.MemorySpace.VMEM


def smem():
    return pl.BlockSpec(memory_space=SMEM)


def vmem():
    return pl.BlockSpec(memory_space=VMEM)


def anywhere():
    return pl.BlockSpec(memory_space=pl.ANY)


def body(fields, hyper_coef, vert_coef, dep_owner, dep_row, dep_col, shifts, fracs):
    fcount, levels, cells, width = fields.shape
    count = fcount * levels
    chunks = lax.axis_size("lon")
    groups = lax.axis_size("group")
    tile_rows = cells // TILE
    tile_cols = width // TILE
    tiles = tile_rows * tile_cols
    rows = PAIR * cells
    f32 = jnp.float32
    limit = pltpu.CompilerParams(vmem_limit_bytes=48 * 1024 * 1024)

    blocks = pl.pallas_call(
        functools.partial(pack_kernel, tile_rows, tile_cols, groups * PAIR * tile_rows - 2),
        out_shape=jax.ShapeDtypeStruct((count, cells + INFO_ROWS, width), f32),
        in_specs=[anywhere(), vmem(), vmem(), vmem(), vmem(), vmem()],
        out_specs=vmem(),
        scratch_shapes=[pltpu.VMEM((8, LANES), jnp.int32), pltpu.SemaphoreType.DMA((PAIR,))],
        compiler_params=limit,
    )(
        fields.reshape(count, cells, width),
        dep_owner.reshape(1, tiles),
        dep_row.reshape(1, tiles),
        dep_col.reshape(1, tiles),
        shifts.reshape(tiles, 2).T,
        fracs.reshape(tiles, 2).T,
    )
    blocks = lax.all_to_all(blocks, ("part", "lon"), 0, 0, tiled=True)
    southward = [
        (group * PAIR + part, (group + 1) * PAIR + PAIR - 1 - part) for group in range(groups - 1) for part in range(PAIR)
    ]
    northward = [(target, source) for source, target in southward]
    bands = ("group", "part")
    north = lax.ppermute(blocks[(PAIR - 1) * chunks :, cells - TILE : cells, :], bands, southward)
    south = lax.ppermute(blocks[:chunks, :TILE, :], bands, northward)
    places = blocks[:, cells : cells + 4, tiles : 2 * tiles].astype(jnp.int32).reshape(PAIR * chunks, 4 * tiles)
    edge = jax.ShapeDtypeStruct((2 * chunks, width), f32)
    phi, top, bottom = pl.pallas_call(
        interpolate_kernel,
        out_shape=(jax.ShapeDtypeStruct((chunks, rows, width), f32), edge, edge),
        in_specs=[smem(), vmem(), vmem(), vmem()],
        out_specs=(vmem(), vmem(), vmem()),
        scratch_shapes=[
            pltpu.VMEM((chunks, rows + 2 * TILE + 8, width), f32),
            pltpu.VMEM((2 * tile_rows, SPAN, width), f32),
            pltpu.SemaphoreType.DMA((2 + PAIR,)),
        ],
        compiler_params=limit,
    )(places, blocks, north, south)
    above = lax.ppermute(bottom, bands, southward)
    below = lax.ppermute(top, bands, northward)
    psi_shape = jax.ShapeDtypeStruct((count, cells, width), f32)
    psi = pl.pallas_call(
        diffuse_kernel,
        out_shape=psi_shape,
        in_specs=[smem(), vmem()],
        out_specs=vmem(),
        scratch_shapes=[pltpu.VMEM((chunks, rows, width), f32)],
        compiler_params=limit,
    )(hyper_coef, phi)
    psi = pl.pallas_call(
        functools.partial(mend_kernel, groups),
        out_shape=psi_shape,
        in_specs=[smem(), vmem(), vmem(), vmem(), anywhere()],
        out_specs=anywhere(),
        input_output_aliases={4: 0},
        scratch_shapes=[
            pltpu.VMEM((2 * chunks, 5 * PAD, width), f32),
            pltpu.VMEM((2 * chunks, 5 * PAD, width), f32),
            pltpu.VMEM((2 * chunks, PAD, width), f32),
            pltpu.SemaphoreType.DMA((2,)),
        ],
        compiler_params=limit,
    )(hyper_coef, phi, above, below, psi)
    psi = lax.all_to_all(psi, ("part", "lon"), 0, 0, tiled=True)
    lower, upper, inverse = vertical_tables(vert_coef)
    return pl.pallas_call(
        functools.partial(vertical_kernel, levels),
        grid=(fcount,),
        out_shape=jax.ShapeDtypeStruct((fcount, levels, cells, width), f32),
        in_specs=[smem(), smem(), smem(), vmem()],
        out_specs=pl.BlockSpec((1, levels, cells, width), lambda field: (field, 0, 0, 0)),
        compiler_params=limit,
    )(lower, upper, inverse, psi)


def solution(mesh):
    lat, lon = mesh.shape["lat"], mesh.shape["lon"]
    grouped = Mesh(mesh.devices.reshape(lat // PAIR, PAIR, lon), ("group", "part", "lon"))
    bands = ("group", "part")
    cells = P(None, None, bands, "lon")
    tiles = P(bands, "lon", None, None)
    return jax.shard_map(
        body,
        mesh=grouped,
        in_specs=(cells, P(), P(), tiles, tiles, tiles, tiles, tiles),
        out_specs=cells,
        check_vma=False,
    )
```

time: 127 us -> 120 us (0.945)
  Pallas kernels: 17.3 us -> 15.6 us
  starting transfers between devices: 21.3 us -> 19.7 us
  waiting for transfers between devices: 38.8 us -> 37.3 us
    reshape x7 -> x1, local copies, waits for them, and re-layouts: 3.83 us -> 0.07 us  [body(): blocks[:, cells:cells + 4, tiles:2 * tiles].astype(jnp.int32)]
    unnamed x6 -> x16, local copies, waits for them, and re-layouts: 1.23 us -> 4.56 us
    pallas_call x1, Pallas kernels: 9.29 us -> 6.55 us  [body(): pl.pallas_call(interpolate_kernel, out_shape=(jax.ShapeDtypeStruct((chunk...]
    ppermute x4, starting transfers between devices: 16.5 us -> 15 us  [the longest x1 5.24 us: body(): above = lax.ppermute(bottom, bands, southward)]
    ppermute x4, waiting for transfers between devices: 10.3 us -> 8.83 us  [the longest x1 8.83 us: body(): south = lax.ppermute(blocks[:chunks, :TILE, :], bands, northward)]
    pallas_call x2 -> x3, Pallas kernels: 5.74 us -> 6.78 us  [the longest x1 4.88 us: body(): pl.pallas_call(diffuse_kernel, out_shape=psi_shape, in_specs=[smem(), vme...]
  transfers between devices with their start and end apart: 5 -> 5, of which waited for: 4 -> 2; matrix products, arithmetic and copies ran while one was open for 2% -> 1% of each run, Pallas kernels for 0% -> 4%
where the time goes in v2:
time: 120 us
  blocking collectives  41.3 us (34%)
  waiting for transfers between devices  37.3 us (31%)
  starting transfers between devices  19.7 us (16%)
  Pallas kernels  15.6 us (13%)
  local copies, waits for them, and re-layouts  4.97 us (4%)
    all_to_all x1, blocking collectives, body(): blocks = lax.all_to_all(blocks, ('part', 'lon'), 0, 0, tiled=True)  41.3 us
    all_to_all x1, waiting for transfers between devices, body(): psi = lax.all_to_all(psi, ('part', 'lon'), 0, 0, tiled=True)  28.5 us
    ppermute x1, waiting for transfers between devices, body(): south = lax.ppermute(blocks[:chunks, :TILE, :], bands, northward)  8.83 us
    pallas_call x1, Pallas kernels, body(): pl.pallas_call(interpolate_kernel, out_shape=(jax.ShapeDtypeStruct((chunk...  6.55 us
    ppermute x1, starting transfers between devices, body(): above = lax.ppermute(bottom, bands, southward)  5.24 us
    pallas_call x1, Pallas kernels, body(): pl.pallas_call(diffuse_kernel, out_shape=psi_shape, in_specs=[smem(), vme...  4.88 us
    all_to_all x1, starting transfers between devices, body(): psi = lax.all_to_all(psi, ('part', 'lon'), 0, 0, tiled=True)  4.67 us
    unnamed x16, local copies, waits for them, and re-layouts  4.56 us
  transfers between devices with their start and end apart: 5, of which 2 were waited for; matrix products, arithmetic and copies ran while one was open for 1% of the time, Pallas kernels for 4%

profile of v2, /device:TPU:36, one launch (start us, length us, event | category | flops | bytes accessed | tf_op | source)
XLA Modules:
  0.0 119.5 jit_solution(2564576997188794600)
XLA Ops:
  0.0 0.0 copy-start
  0.0 1.2 %copy-done = f32[4,8,64,128]{3,2,1,0:T(8,128)S(1)} copy-done((f32[4,8,64,128]{3,2,1,0:T(8,128)S(1)}, f32[4,8,64,128]{3,2,1,0:T(8,128)}, u32[]{:S(2)}) %copy-start) | copy-done | bytes 1048600
  1.2 0.0 copy-start.2
  1.2 0.7 copy-done.2
  1.9 0.0 copy-start.3
  1.9 0.7 copy-done.3
  2.6 0.0 copy-start.4
  2.6 0.7 copy-done.4
  3.2 0.0 copy-start.5
  3.2 0.7 copy-done.5
  3.9 0.0 copy-start.6
  3.9 0.7 copy-done.6
  4.6 0.2 shard_map.82
  4.7 41.3 %all_to_all.10.blocks_ref = f32[32,72,128]{2,1,0:T(8,128)S(1)} all-to-all(f32[32,72,128]{2,1,0:T(8,128)S(1)} %shard_map.82), channel_id=1, replica_groups=mesh['group'=8,'part'=2,'lon'=16] {'part','lon'}, dimensions={0} | all-to-all | bytes 2359296 | tf_op jit(solution)/shard_map/all_to_all | solution.py:329
  46.1 0.1 fusion
  46.2 0.0 copy-start.1
  46.2 3.8 %collective-permute-start.1 = (f32[16,32,128]{2,1,0:T(8,128)S(1)}, f32[16,32,128]{2,1,0:T(8,128)S(1)}, u32[]{:S(2)}, u32[]{:S(2)}) collective-permute-start(f32[16,32,128]{2,1,0:T(8,128)S(1)} %get-tuple-element.19), channel_id=1, source_target_pairs={{48,0},{32,16},{80,32},{64,48},{112,64},{96,80},{144,96},{128,112}... | collective-permute-start | bytes 786440 | tf_op jit(solution)/shard_map/ppermute | solution.py:336
  50.0 3.2 %collective-permute-start = (f32[16,32,128]{2,1,0:T(8,128)S(1)}, f32[16,32,128]{2,1,0:T(8,128)S(1)}, u32[]{:S(2)}, u32[]{:S(2)}) collective-permute-start(f32[16,32,128]{2,1,0:T(8,128)S(1)} %get-tuple-element.20), channel_id=1, source_target_pairs={{0,48},{16,32},{32,80},{48,64},{64,112},{80,96},{96,144},{112,128}... | collective-permute-start | bytes 786440 | tf_op jit(solution)/shard_map/ppermute | solution.py:335
  53.2 0.1 slice_convert_fusion
  53.3 0.1 copy.12
  53.4 0.1 copy.13.places_ref
  53.5 8.8 %collective-permute-done.1.south_ref = f32[16,32,128]{2,1,0:T(8,128)S(1)} collective-permute-done((f32[16,32,128]{2,1,0:T(8,128)S(1)}, f32[16,32,128]{2,1,0:T(8,128)S(1)}, u32[]{:S(2)}, u32[]{:S(2)}) %collective-permute-start.1) | collective-permute-done | bytes 262176 | tf_op jit(solution)/shard_map/ppermute | solution.py:336
  62.3 0.0 collective-permute-done.north_ref
  62.3 6.6 %shard_map.83 = (f32[16,128,128]{2,1,0:T(8,128)S(1)}, f32[32,128]{1,0:T(8,128)S(1)}, f32[32,128]{1,0:T(8,128)S(1)}) custom-call(s32[32,32]{1,0:T(8,128)S(1)} %copy.13.places_ref, f32[32,72,128]{2,1,0:T(8,128)S(1)} %all_to_all.10.blocks_ref, f32[16,32,128]{2,1,0:T(8,128)S(1)} %collective-permute-done.north_ref, ...), custom_call_target="tpu_custom_call" | custom-call | tf_op jit(solution)/shard_map/pallas_call | solution.py:339
  68.9 5.2 %collective-permute-start.2 = (f32[32,128]{1,0:T(8,128)S(1)}, f32[32,128]{1,0:T(8,128)S(1)}, u32[]{:S(2)}, u32[]{:S(2)}) collective-permute-start(f32[32,128]{1,0:T(8,128)S(1)} %get-tuple-element.9), channel_id=1, source_target_pairs={{0,48},{16,32},{32,80},{48,64},{64,112},{80,96},{96,144},{112,128}... | collective-permute-start | bytes 49160 | tf_op jit(solution)/shard_map/ppermute | solution.py:351
  74.1 2.7 %collective-permute-start.3 = (f32[32,128]{1,0:T(8,128)S(1)}, f32[32,128]{1,0:T(8,128)S(1)}, u32[]{:S(2)}, u32[]{:S(2)}) collective-permute-start(f32[32,128]{1,0:T(8,128)S(1)} %get-tuple-element.10), channel_id=1, source_target_pairs={{48,0},{32,16},{80,32},{64,48},{112,64},{96,80},{144,96},{128,112}... | collective-permute-start | bytes 49160 | tf_op jit(solution)/shard_map/ppermute | solution.py:352
  76.9 0.0 copy-done.1
  76.9 4.9 %shard_map.84.inner_ref = f32[32,64,128]{2,1,0:T(8,128)} custom-call(f32[4,8]{1,0:T(4,128)S(1)} %copy-done.1, f32[16,128,128]{2,1,0:T(8,128)S(1)} %get-tuple-element.8.phi_ref), custom_call_target="tpu_custom_call" | custom-call | tf_op jit(solution)/shard_map/pallas_call | solution.py:354
  81.7 0.0 collective-permute-done.2.north_ref
  81.7 0.0 collective-permute-done.3.south_ref
  81.7 1.7 %shard_map.85 = f32[32,64,128]{2,1,0:T(8,128)} custom-call(f32[4,8]{1,0:T(4,128)S(1)} %copy-done.1, f32[16,128,128]{2,1,0:T(8,128)S(1)} %get-tuple-element.8.phi_ref, f32[32,128]{1,0:T(8,128)S(1)} %collective-permute-done.2.north_ref, f32[32,128]{1,0:T(8,128)S(1)} %collective-permute-done.3.south_ref, ...), custom_call_target="tpu_custom_call", output_to_operand_aliasing={{}: (4, {})} | custom-call | tf_op jit(solution)/shard_map/pallas_call | solution.py:362
  83.5 0.0 copy-start.7
  83.5 4.7 %all-to-all-start.1 = ((f32[32,64,128]{2,1,0:T(8,128)}), f32[32,64,128]{2,1,0:T(8,128)S(1)}, u32[]{:S(2)}, u32[]{:S(2)}) async-start(f32[32,64,128]{2,1,0:T(8,128)} %shard_map.85), calls=%async_computation.1 | async-start | bytes 2097152 | tf_op jit(solution)/shard_map/all_to_all | solution.py:376
  88.2 0.0 copy-done.7
  88.2 0.1 pad_add_fusion
  88.2 0.1 broadcast_divide_fusion
  88.4 0.1 broadcast_divide_fusion.1
  88.5 0.1 stack.4.upper_ref
  88.6 0.1 broadcast_divide_fusion.6
  88.6 0.1 stack.5.inverse_ref
  88.7 28.5 %all-to-all-done.1.psi_ref = f32[32,64,128]{2,1,0:T(8,128)S(1)} async-done(((f32[32,64,128]{2,1,0:T(8,128)}), f32[32,64,128]{2,1,0:T(8,128)S(1)}, u32[]{:S(2)}, u32[]{:S(2)}) %all-to-all-start.1) | async-done | bytes 1048608 | tf_op jit(solution)/shard_map/all_to_all | solution.py:376
  117.2 2.3 %shard_map.86 = f32[4,8,64,128]{3,2,1,0:T(8,128)} custom-call(f32[4,8]{1,0:T(4,128)S(1)} %get-tuple-element.29.lower_ref, f32[4,8]{1,0:T(4,128)S(1)} %stack.4.upper_ref, f32[4,8]{1,0:T(4,128)S(1)} %stack.5.inverse_ref, f32[32,64,128]{2,1,0:T(8,128)S(1)} %all-to-all-done.1.psi_ref), custom_call_target="tpu_custom_call" | custom-call | tf_op jit(solution)/shard_map/pallas_call | solution.py:378
Async XLA Ops:
  0.0 1.2 %copy-start = (f32[4,8,64,128]{3,2,1,0:T(8,128)S(1)}, f32[4,8,64,128]{3,2,1,0:T(8,128)}, u32[]{:S(2)}) copy-start(f32[4,8,64,128]{3,2,1,0:T(8,128)} %param.8) | copy-start | bytes 3145732
  1.2 0.7 copy-start.2
  1.9 0.7 copy-start.3
  2.6 0.7 copy-start.4
  3.2 0.7 copy-start.5
  3.9 0.7 copy-start.6
  46.2 30.7 %copy-start.1 = (f32[4,8]{1,0:T(4,128)S(1)}, f32[4,8]{1,0:T(4,128)}, u32[]{:S(2)}) copy-start(f32[4,8]{1,0:T(4,128)} %coef_ref.3) | copy-start | bytes 388
  46.2 16.2 %collective-permute-start.1 = (f32[16,32,128]{2,1,0:T(8,128)S(1)}, f32[16,32,128]{2,1,0:T(8,128)S(1)}, u32[]{:S(2)}, u32[]{:S(2)}) collective-permute-start(f32[16,32,128]{2,1,0:T(8,128)S(1)} %get-tuple-element.19), channel_id=1, source_target_pairs={{48,0},{32,16},{80,32},{64,48},{112,64},{96,80},{144,96},{128,112}... | collective-permute-start | bytes 786440 | tf_op jit(solution)/shard_map/ppermute | solution.py:336
  50.0 12.3 %collective-permute-start = (f32[16,32,128]{2,1,0:T(8,128)S(1)}, f32[16,32,128]{2,1,0:T(8,128)S(1)}, u32[]{:S(2)}, u32[]{:S(2)}) collective-permute-start(f32[16,32,128]{2,1,0:T(8,128)S(1)} %get-tuple-element.20), channel_id=1, source_target_pairs={{0,48},{16,32},{32,80},{48,64},{64,112},{80,96},{96,144},{112,128}... | collective-permute-start | bytes 786440 | tf_op jit(solution)/shard_map/ppermute | solution.py:335
  68.9 12.9 %collective-permute-start.2 = (f32[32,128]{1,0:T(8,128)S(1)}, f32[32,128]{1,0:T(8,128)S(1)}, u32[]{:S(2)}, u32[]{:S(2)}) collective-permute-start(f32[32,128]{1,0:T(8,128)S(1)} %get-tuple-element.9), channel_id=1, source_target_pairs={{0,48},{16,32},{32,80},{48,64},{64,112},{80,96},{96,144},{112,128}... | collective-permute-start | bytes 49160 | tf_op jit(solution)/shard_map/ppermute | solution.py:351
  74.1 7.6 %collective-permute-start.3 = (f32[32,128]{1,0:T(8,128)S(1)}, f32[32,128]{1,0:T(8,128)S(1)}, u32[]{:S(2)}, u32[]{:S(2)}) collective-permute-start(f32[32,128]{1,0:T(8,128)S(1)} %get-tuple-element.10), channel_id=1, source_target_pairs={{48,0},{32,16},{80,32},{64,48},{112,64},{96,80},{144,96},{128,112}... | collective-permute-start | bytes 49160 | tf_op jit(solution)/shard_map/ppermute | solution.py:352
  83.5 4.7 %copy-start.7 = (f32[4,7]{1,0:T(4,128)S(1)}, f32[4,7]{1,0:T(4,128)}, u32[]{:S(2)}) copy-start(f32[4,7]{1,0:T(4,128)} %param.10) | copy-start | bytes 340
  83.5 33.8 %all-to-all-start.1 = ((f32[32,64,128]{2,1,0:T(8,128)}), f32[32,64,128]{2,1,0:T(8,128)S(1)}, u32[]{:S(2)}, u32[]{:S(2)}) async-start(f32[32,64,128]{2,1,0:T(8,128)} %shard_map.85), calls=%async_computation.1 | async-start | bytes 2097152 | tf_op jit(solution)/shard_map/all_to_all | solution.py:376

commit v3 on v2

v3 whole, which is shorter than its diff:
```python
import functools

import jax
import jax.numpy as jnp
from jax import lax
from jax.experimental import pallas as pl
from jax.experimental.pallas import tpu as pltpu
from jax.sharding import PartitionSpec as P

TILE = 32
FRACS = 16
LANES = 128
INFO_ROWS = 8
HALVES = 2
TAPS = 4
SPAN = 40


def cubic_weights(fraction_index):
    fraction = fraction_index.astype(jnp.float32) / FRACS
    return (
        -fraction * (fraction - 1.0) * (fraction - 2.0) / 6.0,
        (fraction + 1.0) * (fraction - 1.0) * (fraction - 2.0) / 2.0,
        -(fraction + 1.0) * fraction * (fraction - 2.0) / 2.0,
        (fraction + 1.0) * fraction * (fraction - 1.0) / 6.0,
    )


def pack_kernel(tile_rows, tile_cols, last_row, fields_ref, table_ref, out_ref, wide_ref, sem):
    count, cells = out_ref.shape[0], fields_ref.shape[1]
    copy = pltpu.make_async_copy(fields_ref.at[0:count], out_ref.at[:, 0:cells, :], sem.at[0])
    copy.start()
    entries, tiles = table_ref.shape
    band = lax.axis_index("lat")
    wide_ref[...] = jnp.zeros(wide_ref.shape, jnp.int32)
    wide_ref[0:entries, 0:tiles] = table_ref[...]
    table = wide_ref[...]
    owner, dep_row, dep_col = table[0:1], table[1:2], table[2:3]
    shift_row, shift_col, frac_row, frac_col = table[3:4], table[4:5], table[5:6], table[6:7]
    dep_tile = jnp.clip(band * tile_rows - 1 + dep_row, 0, last_row)
    start = TILE * (dep_tile - (band * tile_rows - 1)) + shift_row - 1
    column = TILE * dep_col + shift_col - 1
    wrapped = jnp.where(dep_col == tile_cols - 1, TILE, 0)
    position = lax.rem(lax.broadcasted_iota(jnp.int32, (1, LANES), 1), tile_cols)
    turn = lax.bitwise_and(LANES + TILE * position - column, LANES - 1)
    shape = (INFO_ROWS, LANES)
    index = lax.broadcasted_iota(jnp.int32, shape, 0)
    lane = lax.broadcasted_iota(jnp.int32, shape, 1)
    info = jnp.zeros(shape, jnp.float32)
    for place, value in enumerate(cubic_weights(frac_row) + cubic_weights(frac_col)):
        info = jnp.where(index == place, value, info)
    places = jnp.zeros(shape, jnp.int32)
    for place, value in enumerate((start, owner, wrapped, turn)):
        places = jnp.where(index == place, value, places)
    info = jnp.where(lane < tiles, info, pltpu.roll(places.astype(jnp.float32), tiles, 1))
    for block in range(count):
        out_ref[block, cells:, :] = info
    copy.wait()


def interpolate_kernel(
    places_ref, info_ref, blocks_ref, north_ref, south_ref, phi_ref, top_ref, bottom_ref, ext_ref, pass_ref, sem
):
    chunks, halo = north_ref.shape[0], north_ref.shape[1]
    cells = phi_ref.shape[1]
    tile_rows = cells // TILE
    tile_cols = LANES // TILE
    tiles = tile_rows * tile_cols
    copies = [
        pltpu.make_async_copy(north_ref, ext_ref.at[:, 0:halo, :], sem.at[0]),
        pltpu.make_async_copy(blocks_ref.at[:, 0:cells, :], ext_ref.at[:, halo : halo + cells, :], sem.at[1]),
        pltpu.make_async_copy(south_ref, ext_ref.at[:, halo + cells : 2 * halo + cells, :], sem.at[2]),
    ]
    for copy in copies:
        copy.start()
    for copy in copies:
        copy.wait()
    lane = lax.broadcasted_iota(jnp.int32, (SPAN, LANES), 1)
    lane_info = lax.broadcasted_iota(jnp.int32, (INFO_ROWS, LANES), 1)
    first_even = lane < 48
    first_odd = (lane >= 16) & (lane < 80)
    even_group = [lax.bitwise_and(lane - tap, TILE) == 0 for tap in range(TAPS)]

    def columns(device, tile_row, slot):
        own = lane_info // TILE + tile_row * tile_cols
        weights = jnp.take_along_axis(info_ref[device, cells:, :], own, axis=1)

        def window(tile_col):
            tile = tile_row * tile_cols + tile_col
            start, source, wrapped, turn = (places_ref[device, place * tiles + tile] for place in range(4))
            after = lax.rem(source + 1, chunks)
            rows = pl.ds(start, SPAN)
            return pltpu.roll(jnp.where(lane < wrapped, ext_ref[after, rows, :], ext_ref[source, rows, :]), turn, 1)

        evens = jnp.where(first_even, window(0), window(2))
        odds = jnp.where(first_odd, window(1), window(3))
        total = None
        for tap in range(TAPS):
            value = jnp.where(even_group[tap], evens, odds)
            if tap:
                value = pltpu.roll(value, LANES - tap, 1)
            value = weights[TAPS + tap : TAPS + tap + 1] * value
            total = value if total is None else total + value
        pass_ref[slot] = total
        return weights

    def rows_of(device, tile_row, slot, weights):
        total = None
        for tap in range(TAPS):
            value = weights[tap : tap + 1] * pass_ref[slot, tap : tap + TILE, :]
            total = value if total is None else total + value
        phi_ref[device, tile_row * TILE : (tile_row + 1) * TILE, :] = total

    together = pass_ref.shape[0] // tile_rows

    def step(index, carry):
        work = []
        for place in range(together):
            device = index * together + place
            for tile_row in range(tile_rows):
                slot = place * tile_rows + tile_row
                work.append((device, tile_row, slot, columns(device, tile_row, slot)))
        for item in work:
            rows_of(*item)
        return carry

    lax.fori_loop(0, chunks // together, step, 0)
    for chunk in range(chunks):
        top_ref[2 * chunk : 2 * chunk + 2, :] = phi_ref[chunk, 0:2, :]
        bottom_ref[2 * chunk : 2 * chunk + 2, :] = phi_ref[chunk, cells - 2 : cells, :]


PAD = 8


def laplacian(ref, chunks, chunk, first, count):
    lane = lax.broadcasted_iota(jnp.int32, (count, LANES), 1)
    west = lax.rem(chunk + chunks - 1, chunks)
    east = lax.rem(chunk + 1, chunks)
    here = ref[chunk, first : first + count, :]
    from_west = pltpu.roll(jnp.where(lane == LANES - 1, ref[west, first : first + count, :], here), 1, 1)
    from_east = pltpu.roll(jnp.where(lane == 0, ref[east, first : first + count, :], here), LANES - 1, 1)
    beside = ref[chunk, first + 1 : first + 1 + count, :] + ref[chunk, first - 1 : first - 1 + count, :] + from_west + from_east
    return beside - 4.0 * here


def own_coef(coef_ref, half, chunks):
    levels = coef_ref.shape[1]
    member = half * chunks + lax.axis_index("lon")
    return coef_ref[member // levels, lax.rem(member, levels)]


def diffuse_kernel(half, coef_ref, phi_ref, psi_ref, lap_ref):
    chunks, cells = phi_ref.shape[0], phi_ref.shape[1]
    coef = own_coef(coef_ref, half, chunks)

    def first_pass(chunk, carry):
        lap_ref[chunk, PAD - 1 : cells - PAD + 1, :] = laplacian(phi_ref, chunks, chunk, PAD - 1, cells - 2 * PAD + 2)
        return carry

    def second_pass(chunk, carry):
        twice = laplacian(lap_ref, chunks, chunk, PAD, cells - 2 * PAD)
        psi_ref[chunk] = phi_ref[chunk, PAD : cells - PAD, :] - coef * twice
        return carry

    lax.fori_loop(0, chunks, first_pass, 0)
    lax.fori_loop(0, chunks, second_pass, 0)


def mend_kernel(half, coef_ref, phi_ref, north_ref, south_ref, inner_ref, psi_ref, ext_ref, lap_ref):
    chunks, cells = phi_ref.shape[0], phi_ref.shape[1]
    coef = own_coef(coef_ref, half, chunks)
    band = lax.axis_index("lat")
    has_north = jnp.where(band > 0, 1.0, 0.0)
    has_south = jnp.where(band < lax.axis_size("lat") - 1, 1.0, 0.0)
    zeros = jnp.zeros((PAD, LANES), jnp.float32)
    for chunk in range(chunks):
        place = chunk
        psi_ref[chunk, PAD : cells - PAD, :] = inner_ref[chunk]
        ext_ref[place, 0:PAD, :] = zeros
        ext_ref[place, 4 * PAD :, :] = zeros
        ext_ref[place, PAD : 2 * PAD, :] = zeros
        ext_ref[place, 2 * PAD - 2 : 2 * PAD, :] = north_ref[2 * chunk : 2 * chunk + 2, :]
        ext_ref[place, 2 * PAD : 4 * PAD, :] = phi_ref[chunk, 0 : 2 * PAD, :]
        place = chunks + chunk
        ext_ref[place, 0:PAD, :] = zeros
        ext_ref[place, 4 * PAD :, :] = zeros
        ext_ref[place, PAD : 3 * PAD, :] = phi_ref[chunk, cells - 2 * PAD :, :]
        ext_ref[place, 3 * PAD : 4 * PAD, :] = zeros
        ext_ref[place, 3 * PAD : 3 * PAD + 2, :] = south_ref[2 * chunk : 2 * chunk + 2, :]
    for side in range(2):
        own = pl.ds(side * chunks, chunks)
        for chunk in range(chunks):
            once = laplacian(ext_ref.at[own], chunks, chunk, PAD, 3 * PAD)
            place = side * chunks + chunk
            if side == 0:
                lap_ref[place, PAD : 2 * PAD, :] = once[0:PAD] * has_north
                lap_ref[place, 2 * PAD : 4 * PAD, :] = once[PAD:]
            else:
                lap_ref[place, PAD : 3 * PAD, :] = once[0 : 2 * PAD]
                lap_ref[place, 3 * PAD : 4 * PAD, :] = once[2 * PAD :] * has_south
    for side in range(2):
        own = pl.ds(side * chunks, chunks)
        rows = slice(0, PAD) if side == 0 else slice(cells - PAD, cells)
        for chunk in range(chunks):
            twice = laplacian(lap_ref.at[own], chunks, chunk, 2 * PAD, PAD)
            psi_ref[chunk, rows, :] = phi_ref[chunk, rows, :] - coef * twice


def vertical_kernel(levels, half, lower_ref, upper_ref, inverse_ref, psi_ref, *refs):
    out_ref = refs[-1]
    local = pl.program_id(0)
    field = half * pl.num_programs(0) + local
    sweep = []
    for level in range(levels):
        rhs = psi_ref[level]
        if level:
            rhs = rhs + lower_ref[field, level] * sweep[-1]
        sweep.append(rhs * inverse_ref[field, level])
    value = sweep[-1]
    out_ref[0, levels - 1] = value
    for level in range(levels - 2, -1, -1):
        value = sweep[level] - upper_ref[field, level] * value
        out_ref[0, level] = value


def vertical_tables(vert_coef):
    fcount = vert_coef.shape[0]
    levels = vert_coef.shape[1] + 1
    zero_column = jnp.zeros((fcount, 1), jnp.float32)
    lower_coef = jnp.concatenate([zero_column, vert_coef], axis=1)
    upper_coef = jnp.concatenate([vert_coef, zero_column], axis=1)
    diagonal = 1.0 + lower_coef + upper_coef
    uppers, inverses = [], []
    for level in range(levels):
        denominator = diagonal[:, level]
        if level:
            denominator = denominator + lower_coef[:, level] * uppers[-1]
        inverses.append(1.0 / denominator)
        uppers.append(-upper_coef[:, level] / denominator)
    return lower_coef, jnp.stack(uppers, axis=1), jnp.stack(inverses, axis=1)


SMEM = pltpu.MemorySpace.SMEM
VMEM = pltpu.MemorySpace.VMEM


def smem():
    return pl.BlockSpec(memory_space=SMEM)


def vmem():
    return pl.BlockSpec(memory_space=VMEM)


def anywhere():
    return pl.BlockSpec(memory_space=pl.ANY)


LIMIT = pltpu.CompilerParams(vmem_limit_bytes=48 * 1024 * 1024)


def along_lat(value, by):
    peers = lax.axis_size("lat")
    return lax.ppermute(value, "lat", [(i, i + by) for i in range(peers) if 0 <= i + by < peers])


def interpolated(places, info, blocks, north, south, cells):
    chunks, _, width = blocks.shape
    tile_rows = cells // TILE
    edge = jax.ShapeDtypeStruct((2 * chunks, width), jnp.float32)
    return pl.pallas_call(
        interpolate_kernel,
        out_shape=(jax.ShapeDtypeStruct((chunks, cells, width), jnp.float32), edge, edge),
        in_specs=[smem(), vmem(), vmem(), vmem(), vmem()],
        out_specs=(vmem(), vmem(), vmem()),
        scratch_shapes=[
            pltpu.VMEM((chunks, cells + 2 * TILE + 8, width), jnp.float32),
            pltpu.VMEM((2 * tile_rows, SPAN, width), jnp.float32),
            pltpu.SemaphoreType.DMA((3,)),
        ],
        compiler_params=LIMIT,
        name="interpolate",
    )(places, info, blocks, north, south)


def diffused(half, hyper_coef, phi):
    chunks, cells, width = phi.shape
    return pl.pallas_call(
        functools.partial(diffuse_kernel, half),
        out_shape=jax.ShapeDtypeStruct((chunks, cells - 2 * PAD, width), jnp.float32),
        in_specs=[smem(), vmem()],
        out_specs=vmem(),
        scratch_shapes=[pltpu.VMEM(phi.shape, jnp.float32)],
        compiler_params=LIMIT,
        name="diffuse",
    )(hyper_coef, phi)


def mended(half, hyper_coef, phi, above, below, inner):
    chunks, cells, width = phi.shape
    return pl.pallas_call(
        functools.partial(mend_kernel, half),
        out_shape=jax.ShapeDtypeStruct(phi.shape, jnp.float32),
        in_specs=[smem(), vmem(), vmem(), vmem(), vmem()],
        out_specs=vmem(),
        scratch_shapes=[
            pltpu.VMEM((2 * chunks, 5 * PAD, width), jnp.float32),
            pltpu.VMEM((2 * chunks, 5 * PAD, width), jnp.float32),
        ],
        compiler_params=LIMIT,
        name="mend",
    )(hyper_coef, phi, above, below, inner)


def solved(half, tables, psi, shape, earlier):
    fcount, levels, cells, width = shape
    part = fcount // HALVES
    operands = tables + (psi,) if earlier is None else tables + (psi, earlier)
    return pl.pallas_call(
        functools.partial(vertical_kernel, levels, half),
        grid=(part,),
        out_shape=jax.ShapeDtypeStruct(shape, jnp.float32),
        in_specs=[smem(), smem(), smem(), pl.BlockSpec((levels, cells, width), lambda field: (field, 0, 0))]
        + ([] if earlier is None else [anywhere()]),
        out_specs=pl.BlockSpec((1, levels, cells, width), lambda field: (half * part + field, 0, 0, 0)),
        input_output_aliases={} if earlier is None else {4: 0},
        compiler_params=LIMIT,
        name="solve",
    )(*operands)


def body(fields, hyper_coef, vert_coef, dep_owner, dep_row, dep_col, shifts, fracs):
    fcount, levels, cells, width = fields.shape
    chunks = lax.axis_size("lon")
    tile_rows = cells // TILE
    tile_cols = width // TILE
    tiles = tile_rows * tile_cols
    flat = fields.reshape(fcount * levels, cells, width)
    table = jnp.concatenate(
        [
            dep_owner.reshape(1, tiles),
            dep_row.reshape(1, tiles),
            dep_col.reshape(1, tiles),
            shifts.reshape(tiles, 2).T,
            fracs.reshape(tiles, 2).T,
        ],
        axis=0,
    )
    packed = pl.pallas_call(
        functools.partial(pack_kernel, tile_rows, tile_cols, lax.axis_size("lat") * tile_rows - 2),
        out_shape=jax.ShapeDtypeStruct((chunks, cells + INFO_ROWS, width), jnp.float32),
        in_specs=[anywhere(), vmem()],
        out_specs=vmem(),
        scratch_shapes=[pltpu.VMEM((8, LANES), jnp.int32), pltpu.SemaphoreType.DMA((1,))],
        compiler_params=LIMIT,
        name="pack",
    )(flat, table)
    blocks = [lax.all_to_all(packed, "lon", 0, 0, tiled=True), lax.all_to_all(flat[chunks:], "lon", 0, 0, tiled=True)]
    info = blocks[0]
    places = info[:, cells : cells + 4, tiles : 2 * tiles].astype(jnp.int32).reshape(chunks, 4 * tiles)
    tables = vertical_tables(vert_coef)
    out = None
    psis = []
    for half in range(HALVES):
        north = along_lat(blocks[half][:, cells - TILE : cells, :], 1)
        south = along_lat(blocks[half][:, :TILE, :], -1)
        phi, top, bottom = interpolated(places, info, blocks[half], north, south, cells)
        above = along_lat(bottom, 1)
        below = along_lat(top, -1)
        inner = diffused(half, hyper_coef, phi)
        psi = mended(half, hyper_coef, phi, above, below, inner)
        psis.append(lax.all_to_all(psi, "lon", 0, 0, tiled=True))
    for half in range(HALVES):
        out = solved(half, tables, psis[half], fields.shape, out)
    return out


def solution(mesh):
    cells = P(None, None, "lat", "lon")
    tiles = P("lat", "lon", None, None)
    return jax.shard_map(
        body,
        mesh=mesh,
        in_specs=(cells, P(), P(), tiles, tiles, tiles, tiles, tiles),
        out_specs=cells,
        check_vma=False,
    )
```

time: 120 us -> 135 us (1.12)
  the two profiles are of different devices: /device:TPU:36 before, /device:TPU:7 now
where the time goes in v3:
time: 135 us; the launch traced here: 134 us
  starting transfers between devices  56.6 us (42%)
  waiting for transfers between devices  52.5 us (39%)
  Pallas kernels  21.3 us (16%)
  local copies, waits for them, and re-layouts  3.25 us (2%)
    ppermute x8, starting transfers between devices, along_lat(): lax.ppermute(value, 'lat', [(i, i + by) for i in range(peers) if 0 <= i +...  27.6 us
    ppermute x8, waiting for transfers between devices, along_lat(): lax.ppermute(value, 'lat', [(i, i + by) for i in range(peers) if 0 <= i +...  19.4 us
    all_to_all x1, waiting for transfers between devices, body(): lax.all_to_all(packed, 'lon', 0, 0, tiled=True)  17.8 us
    all_to_all x2, starting transfers between devices, body(): psis.append(lax.all_to_all(psi, 'lon', 0, 0, tiled=True))  16.4 us
    all_to_all x2, waiting for transfers between devices, body(): psis.append(lax.all_to_all(psi, 'lon', 0, 0, tiled=True))  15.2 us
    all_to_all x1, starting transfers between devices, body(): lax.all_to_all(packed, 'lon', 0, 0, tiled=True)  9.16 us
    pallas_call x2, Pallas kernels, interpolated(): pl.pallas_call(interpolate_kernel, out_shape=(jax.ShapeDtypeStruct((chunk...  7.14 us
    pallas_call x2, Pallas kernels, diffused(): pl.pallas_call(functools.partial(diffuse_kernel, half), out_shape=jax.Sha...  6.71 us
  transfers between devices with their start and end apart: 12, of which 6 were waited for; matrix products, arithmetic and copies ran while one was open for 1% of the time, Pallas kernels for 14%

profile of v3, /device:TPU:7, one launch (start us, length us, event | category | flops | bytes accessed | tf_op | source)
XLA Modules:
  0.0 134.4 jit_solution(6362384208906891356)
XLA Ops:
  0.0 0.0 copy-start.5
  0.0 0.0 copy-start.7
  0.0 0.0 copy-start.8
  0.0 0.0 copy-start.4
  0.0 0.0 copy-start.6
  0.0 0.7 copy-done.5
  0.7 0.0 copy-done.7
  0.7 0.0 copy-done.8
  0.7 0.0 copy-done.4
  0.7 0.0 copy-done.6
  0.8 0.0 copy-start
  0.8 1.2 copy-done
  2.0 0.0 copy-start.1
  2.0 1.0 pack.1
  2.9 9.2 %all-to-all-start = ((f32[16,72,128]{2,1,0:T(8,128)}), f32[16,72,128]{2,1,0:T(8,128)S(1)}, u32[]{:S(2)}, u32[]{:S(2)}) async-start(f32[16,72,128]{2,1,0:T(8,128)} %pack.1), calls=%async_computation | async-start | bytes 1179648 | tf_op jit(solution)/shard_map/all_to_all | solution.py:359
  12.1 0.0 copy-done.1
  12.1 0.8 slice.89
  13.0 17.8 %all-to-all-done.info_ref.blocks_ref = f32[16,72,128]{2,1,0:T(8,128)S(1)} async-done(((f32[16,72,128]{2,1,0:T(8,128)}), f32[16,72,128]{2,1,0:T(8,128)S(1)}, u32[]{:S(2)}, u32[]{:S(2)}) %all-to-all-start) | async-done | bytes 589856 | tf_op jit(solution)/shard_map/all_to_all | solution.py:359
  30.8 3.5 %all-to-all-start.1 = ((f32[16,64,128]{2,1,0:T(8,128)}), f32[16,64,128]{2,1,0:T(8,128)S(1)}, u32[]{:S(2)}, u32[]{:S(2)}) async-start(f32[16,64,128]{2,1,0:T(8,128)} %bitcast.9), calls=%async_computation.1 | async-start | bytes 1048576 | tf_op jit(solution)/shard_map/all_to_all | solution.py:359
  34.2 0.1 fusion
  34.3 4.9 %collective-permute-start.5 = (f32[16,32,128]{2,1,0:T(8,128)S(1)}, f32[16,32,128]{2,1,0:T(8,128)S(1)}, u32[]{:S(2)}, u32[]{:S(2)}) collective-permute-start(f32[16,32,128]{2,1,0:T(8,128)S(1)} %get-tuple-element.25), channel_id=1, source_target_pairs={{16,0},{32,16},{48,32},{64,48},{80,64},{96,80},{112,96},{128,112},... | collective-permute-start | bytes 786440 | tf_op jit(solution)/shard_map/ppermute | solution.py:265
  39.2 1.9 %collective-permute-start.4 = (f32[16,32,128]{2,1,0:T(8,128)S(1)}, f32[16,32,128]{2,1,0:T(8,128)S(1)}, u32[]{:S(2)}, u32[]{:S(2)}) collective-permute-start(f32[16,32,128]{2,1,0:T(8,128)S(1)} %get-tuple-element.26), channel_id=1, source_target_pairs={{0,16},{16,32},{32,48},{48,64},{64,80},{80,96},{96,112},{112,128},... | collective-permute-start | bytes 786440 | tf_op jit(solution)/shard_map/ppermute | solution.py:265
  41.2 0.1 slice_convert_fusion
  41.2 0.1 copy.13
  41.3 0.1 copy.14.places_ref
  41.4 3.9 %collective-permute-done.5.south_ref = f32[16,32,128]{2,1,0:T(8,128)S(1)} collective-permute-done((f32[16,32,128]{2,1,0:T(8,128)S(1)}, f32[16,32,128]{2,1,0:T(8,128)S(1)}, u32[]{:S(2)}, u32[]{:S(2)}) %collective-permute-start.5) | collective-permute-done | bytes 262176 | tf_op jit(solution)/shard_map/ppermute | solution.py:265
  45.3 5.9 %collective-permute-done.4.north_ref = f32[16,32,128]{2,1,0:T(8,128)S(1)} collective-permute-done((f32[16,32,128]{2,1,0:T(8,128)S(1)}, f32[16,32,128]{2,1,0:T(8,128)S(1)}, u32[]{:S(2)}, u32[]{:S(2)}) %collective-permute-start.4) | collective-permute-done | bytes 262176 | tf_op jit(solution)/shard_map/ppermute | solution.py:265
  51.2 3.6 %interpolate.3 = (f32[16,64,128]{2,1,0:T(8,128)S(1)}, f32[32,128]{1,0:T(8,128)S(1)}, f32[32,128]{1,0:T(8,128)S(1)}) custom-call(s32[16,32]{1,0:T(8,128)S(1)} %copy.14.places_ref, f32[16,72,128]{2,1,0:T(8,128)S(1)} %all-to-all-done.info_ref.blocks_ref, f32[16,72,128]{2,1,0:T(8,128)S(1)} %all-to-all-done.info_ref.blocks_ref, ...), custom_call_target="tpu_custom_call" | custom-call | tf_op jit(solution)/shard_map/interpolate/pallas_call | solution.py:272
  54.8 0.0 copy-start.2
  54.8 1.9 %collective-permute-start.6 = (f32[32,128]{1,0:T(8,128)S(1)}, f32[32,128]{1,0:T(8,128)S(1)}, u32[]{:S(2)}, u32[]{:S(2)}) collective-permute-start(f32[32,128]{1,0:T(8,128)S(1)} %get-tuple-element.15), channel_id=1, source_target_pairs={{0,16},{16,32},{32,48},{48,64},{64,80},{80,96},{96,112},{112,128},... | collective-permute-start | bytes 49160 | tf_op jit(solution)/shard_map/ppermute | solution.py:265
  56.7 5.5 %collective-permute-start.7 = (f32[32,128]{1,0:T(8,128)S(1)}, f32[32,128]{1,0:T(8,128)S(1)}, u32[]{:S(2)}, u32[]{:S(2)}) collective-permute-start(f32[32,128]{1,0:T(8,128)S(1)} %get-tuple-element.16), channel_id=1, source_target_pairs={{16,0},{32,16},{48,32},{64,48},{80,64},{96,80},{112,96},{128,112},... | collective-permute-start | bytes 49160 | tf_op jit(solution)/shard_map/ppermute | solution.py:265
  62.2 0.0 copy-done.2
  62.2 3.4 %diffuse.3.inner_ref = f32[16,48,128]{2,1,0:T(8,128)S(1)} custom-call(f32[4,8]{1,0:T(4,128)S(1)} %copy-done.2, f32[16,64,128]{2,1,0:T(8,128)S(1)} %get-tuple-element.14.phi_ref), custom_call_target="tpu_custom_call" | custom-call | tf_op jit(solution)/shard_map/diffuse/pallas_call | solution.py:289
  65.6 0.0 collective-permute-done.6.north_ref
  65.6 0.0 collective-permute-done.7.south_ref
  65.6 1.8 %mend.3 = f32[16,64,128]{2,1,0:T(8,128)} custom-call(f32[4,8]{1,0:T(4,128)S(1)} %copy-done.2, f32[16,64,128]{2,1,0:T(8,128)S(1)} %get-tuple-element.14.phi_ref, f32[32,128]{1,0:T(8,128)S(1)} %collective-permute-done.6.north_ref, f32[32,128]{1,0:T(8,128)S(1)} %collective-permute-done.7.south_ref, f32[16,48,128]{2,1,0:T(8,128)S(1)} %diffuse.3.inner_ref), custom_call_target="tpu_custom_call" | custom-call | tf_op jit(solution)/shard_map/mend/pallas_call | solution.py:302
  67.4 0.0 all-to-all-done.1.blocks_ref
  67.4 7.6 %all-to-all-start.3 = ((f32[16,64,128]{2,1,0:T(8,128)}), f32[16,64,128]{2,1,0:T(8,128)S(1)}, u32[]{:S(2)}, u32[]{:S(2)}) async-start(f32[16,64,128]{2,1,0:T(8,128)} %mend.3), calls=%async_computation.3 | async-start | bytes 1048576 | tf_op jit(solution)/shard_map/all_to_all | solution.py:373
  75.1 4.1 %collective-permute-start.1 = (f32[16,32,128]{2,1,0:T(8,128)S(1)}, f32[16,32,128]{2,1,0:T(8,128)S(1)}, u32[]{:S(2)}, u32[]{:S(2)}) collective-permute-start(f32[16,32,128]{2,1,0:T(8,128)S(1)} %get-tuple-element.27), channel_id=1, source_target_pairs={{16,0},{32,16},{48,32},{64,48},{80,64},{96,80},{112,96},{128,112},... | collective-permute-start | bytes 786440 | tf_op jit(solution)/shard_map/ppermute | solution.py:265
  79.2 1.9 %collective-permute-start = (f32[16,32,128]{2,1,0:T(8,128)S(1)}, f32[16,32,128]{2,1,0:T(8,128)S(1)}, u32[]{:S(2)}, u32[]{:S(2)}) collective-permute-start(f32[16,32,128]{2,1,0:T(8,128)S(1)} %get-tuple-element.28), channel_id=1, source_target_pairs={{0,16},{16,32},{32,48},{48,64},{64,80},{80,96},{96,112},{112,128},... | collective-permute-start | bytes 786440 | tf_op jit(solution)/shard_map/ppermute | solution.py:265
  81.1 3.8 %collective-permute-done.1.south_ref = f32[16,32,128]{2,1,0:T(8,128)S(1)} collective-permute-done((f32[16,32,128]{2,1,0:T(8,128)S(1)}, f32[16,32,128]{2,1,0:T(8,128)S(1)}, u32[]{:S(2)}, u32[]{:S(2)}) %collective-permute-start.1) | collective-permute-done | bytes 262176 | tf_op jit(solution)/shard_map/ppermute | solution.py:265
  84.8 5.9 %collective-permute-done.north_ref = f32[16,32,128]{2,1,0:T(8,128)S(1)} collective-permute-done((f32[16,32,128]{2,1,0:T(8,128)S(1)}, f32[16,32,128]{2,1,0:T(8,128)S(1)}, u32[]{:S(2)}, u32[]{:S(2)}) %collective-permute-start) | collective-permute-done | bytes 262176 | tf_op jit(solution)/shard_map/ppermute | solution.py:265
  90.7 3.6 %interpolate.2 = (f32[16,64,128]{2,1,0:T(8,128)S(1)}, f32[32,128]{1,0:T(8,128)S(1)}, f32[32,128]{1,0:T(8,128)S(1)}) custom-call(s32[16,32]{1,0:T(8,128)S(1)} %copy.14.places_ref, f32[16,72,128]{2,1,0:T(8,128)S(1)} %all-to-all-done.info_ref.blocks_ref, f32[16,64,128]{2,1,0:T(8,128)S(1)} %all-to-all-done.1.blocks_ref, ...), custom_call_target="tpu_custom_call" | custom-call | tf_op jit(solution)/shard_map/interpolate/pallas_call | solution.py:272
  94.3 1.9 %collective-permute-start.2 = (f32[32,128]{1,0:T(8,128)S(1)}, f32[32,128]{1,0:T(8,128)S(1)}, u32[]{:S(2)}, u32[]{:S(2)}) collective-permute-start(f32[32,128]{1,0:T(8,128)S(1)} %get-tuple-element.12), channel_id=1, source_target_pairs={{0,16},{16,32},{32,48},{48,64},{64,80},{80,96},{96,112},{112,128},... | collective-permute-start | bytes 49160 | tf_op jit(solution)/shard_map/ppermute | solution.py:265
  96.2 5.5 %collective-permute-start.3 = (f32[32,128]{1,0:T(8,128)S(1)}, f32[32,128]{1,0:T(8,128)S(1)}, u32[]{:S(2)}, u32[]{:S(2)}) collective-permute-start(f32[32,128]{1,0:T(8,128)S(1)} %get-tuple-element.13), channel_id=1, source_target_pairs={{16,0},{32,16},{48,32},{64,48},{80,64},{96,80},{112,96},{128,112},... | collective-permute-start | bytes 49160 | tf_op jit(solution)/shard_map/ppermute | solution.py:265
  101.7 3.4 %diffuse.2.inner_ref = f32[16,48,128]{2,1,0:T(8,128)S(1)} custom-call(f32[4,8]{1,0:T(4,128)S(1)} %copy-done.2, f32[16,64,128]{2,1,0:T(8,128)S(1)} %get-tuple-element.11.phi_ref), custom_call_target="tpu_custom_call" | custom-call | tf_op jit(solution)/shard_map/diffuse/pallas_call | solution.py:289
  105.1 0.0 collective-permute-done.2.north_ref
  105.1 0.0 collective-permute-done.3.south_ref
  105.1 1.8 %mend.2 = f32[16,64,128]{2,1,0:T(8,128)} custom-call(f32[4,8]{1,0:T(4,128)S(1)} %copy-done.2, f32[16,64,128]{2,1,0:T(8,128)S(1)} %get-tuple-element.11.phi_ref, f32[32,128]{1,0:T(8,128)S(1)} %collective-permute-done.2.north_ref, f32[32,128]{1,0:T(8,128)S(1)} %collective-permute-done.3.south_ref, f32[16,48,128]{2,1,0:T(8,128)S(1)} %diffuse.2.inner_ref), custom_call_target="tpu_custom_call" | custom-call | tf_op jit(solution)/shard_map/mend/pallas_call | solution.py:302
  106.9 0.0 copy-start.3
  106.9 0.0 all-to-all-done.3.psi_ref
  106.9 8.7 %all-to-all-start.2 = ((f32[16,64,128]{2,1,0:T(8,128)}), f32[16,64,128]{2,1,0:T(8,128)S(1)}, u32[]{:S(2)}, u32[]{:S(2)}) async-start(f32[16,64,128]{2,1,0:T(8,128)} %mend.2), calls=%async_computation.2 | async-start | bytes 1048576 | tf_op jit(solution)/shard_map/all_to_all | solution.py:373
  115.6 0.0 copy-done.3
  115.6 0.1 pad_add_fusion
  115.7 0.1 broadcast_divide_fusion
  115.8 0.1 broadcast_divide_fusion.1
  115.9 0.1 stack.4.upper_ref
  116.0 0.1 broadcast_divide_fusion.6
  116.1 0.1 stack.5.inverse_ref
  116.2 1.5 %solve.2.refs_0_ = f32[4,8,64,128]{3,2,1,0:T(8,128)} custom-call(f32[4,8]{1,0:T(4,128)S(1)} %get-tuple-element.37.lower_ref, f32[4,8]{1,0:T(4,128)S(1)} %stack.4.upper_ref, f32[4,8]{1,0:T(4,128)S(1)} %stack.5.inverse_ref, f32[16,64,128]{2,1,0:T(8,128)S(1)} %all-to-all-done.3.psi_ref), custom_call_target="tpu_custom_call" | custom-call | tf_op jit(solution)/shard_map/solve/pallas_call | solution.py:320
  117.7 15.2 %all-to-all-done.2.psi_ref = f32[16,64,128]{2,1,0:T(8,128)S(1)} async-done(((f32[16,64,128]{2,1,0:T(8,128)}), f32[16,64,128]{2,1,0:T(8,128)S(1)}, u32[]{:S(2)}, u32[]{:S(2)}) %all-to-all-start.2) | async-done | bytes 524320 | tf_op jit(solution)/shard_map/all_to_all | solution.py:373
  132.9 1.5 %solve.3 = f32[4,8,64,128]{3,2,1,0:T(8,128)} custom-call(f32[4,8]{1,0:T(4,128)S(1)} %get-tuple-element.37.lower_ref, f32[4,8]{1,0:T(4,128)S(1)} %stack.4.upper_ref, f32[4,8]{1,0:T(4,128)S(1)} %stack.5.inverse_ref, f32[16,64,128]{2,1,0:T(8,128)S(1)} %all-to-all-done.2.psi_ref, f32[4,8,64,128]{3,2,1,0:T(8,128)} %solve.2.refs_0_), custom_call_target="tpu_custom_call", output_to_operand_aliasing={{}: (4, {})} | custom-call | tf_op jit(solution)/shard_map/solve/pallas_call | solution.py:320
  (2 shorter events, 0.1 us)
Async XLA Ops:
  0.0 0.7 copy-start.5
  0.0 0.7 copy-start.7
  0.0 0.7 copy-start.8
  0.0 0.7 copy-start.4
  0.0 0.7 copy-start.6
  0.8 1.2 copy-start
  2.0 10.1 %copy-start.1 = (f32[4,8,64,128]{3,2,1,0:T(8,128)S(1)}, f32[4,8,64,128]{3,2,1,0:T(8,128)}, u32[]{:S(2)}) copy-start(f32[4,8,64,128]{3,2,1,0:T(8,128)} %param.8) | copy-start | bytes 3145732
  2.9 27.8 %all-to-all-start = ((f32[16,72,128]{2,1,0:T(8,128)}), f32[16,72,128]{2,1,0:T(8,128)S(1)}, u32[]{:S(2)}, u32[]{:S(2)}) async-start(f32[16,72,128]{2,1,0:T(8,128)} %pack.1), calls=%async_computation | async-start | bytes 1179648 | tf_op jit(solution)/shard_map/all_to_all | solution.py:359
  30.8 36.6 %all-to-all-start.1 = ((f32[16,64,128]{2,1,0:T(8,128)}), f32[16,64,128]{2,1,0:T(8,128)S(1)}, u32[]{:S(2)}, u32[]{:S(2)}) async-start(f32[16,64,128]{2,1,0:T(8,128)} %bitcast.9), calls=%async_computation.1 | async-start | bytes 1048576 | tf_op jit(solution)/shard_map/all_to_all | solution.py:359
  34.3 11.0 %collective-permute-start.5 = (f32[16,32,128]{2,1,0:T(8,128)S(1)}, f32[16,32,128]{2,1,0:T(8,128)S(1)}, u32[]{:S(2)}, u32[]{:S(2)}) collective-permute-start(f32[16,32,128]{2,1,0:T(8,128)S(1)} %get-tuple-element.25), channel_id=1, source_target_pairs={{16,0},{32,16},{48,32},{64,48},{80,64},{96,80},{112,96},{128,112},... | collective-permute-start | bytes 786440 | tf_op jit(solution)/shard_map/ppermute | solution.py:265
  39.2 12.0 %collective-permute-start.4 = (f32[16,32,128]{2,1,0:T(8,128)S(1)}, f32[16,32,128]{2,1,0:T(8,128)S(1)}, u32[]{:S(2)}, u32[]{:S(2)}) collective-permute-start(f32[16,32,128]{2,1,0:T(8,128)S(1)} %get-tuple-element.26), channel_id=1, source_target_pairs={{0,16},{16,32},{32,48},{48,64},{64,80},{80,96},{96,112},{112,128},... | collective-permute-start | bytes 786440 | tf_op jit(solution)/shard_map/ppermute | solution.py:265
  54.8 7.4 %copy-start.2 = (f32[4,8]{1,0:T(4,128)S(1)}, f32[4,8]{1,0:T(4,128)}, u32[]{:S(2)}) copy-start(f32[4,8]{1,0:T(4,128)} %coef_ref.7) | copy-start | bytes 388
  54.8 10.8 %collective-permute-start.6 = (f32[32,128]{1,0:T(8,128)S(1)}, f32[32,128]{1,0:T(8,128)S(1)}, u32[]{:S(2)}, u32[]{:S(2)}) collective-permute-start(f32[32,128]{1,0:T(8,128)S(1)} %get-tuple-element.15), channel_id=1, source_target_pairs={{0,16},{16,32},{32,48},{48,64},{64,80},{80,96},{96,112},{112,128},... | collective-permute-start | bytes 49160 | tf_op jit(solution)/shard_map/ppermute | solution.py:265
  56.7 8.9 %collective-permute-start.7 = (f32[32,128]{1,0:T(8,128)S(1)}, f32[32,128]{1,0:T(8,128)S(1)}, u32[]{:S(2)}, u32[]{:S(2)}) collective-permute-start(f32[32,128]{1,0:T(8,128)S(1)} %get-tuple-element.16), channel_id=1, source_target_pairs={{16,0},{32,16},{48,32},{64,48},{80,64},{96,80},{112,96},{128,112},... | collective-permute-start | bytes 49160 | tf_op jit(solution)/shard_map/ppermute | solution.py:265
  67.4 39.5 %all-to-all-start.3 = ((f32[16,64,128]{2,1,0:T(8,128)}), f32[16,64,128]{2,1,0:T(8,128)S(1)}, u32[]{:S(2)}, u32[]{:S(2)}) async-start(f32[16,64,128]{2,1,0:T(8,128)} %mend.3), calls=%async_computation.3 | async-start | bytes 1048576 | tf_op jit(solution)/shard_map/all_to_all | solution.py:373
  75.1 9.8 %collective-permute-start.1 = (f32[16,32,128]{2,1,0:T(8,128)S(1)}, f32[16,32,128]{2,1,0:T(8,128)S(1)}, u32[]{:S(2)}, u32[]{:S(2)}) collective-permute-start(f32[16,32,128]{2,1,0:T(8,128)S(1)} %get-tuple-element.27), channel_id=1, source_target_pairs={{16,0},{32,16},{48,32},{64,48},{80,64},{96,80},{112,96},{128,112},... | collective-permute-start | bytes 786440 | tf_op jit(solution)/shard_map/ppermute | solution.py:265
  79.2 11.5 %collective-permute-start = (f32[16,32,128]{2,1,0:T(8,128)S(1)}, f32[16,32,128]{2,1,0:T(8,128)S(1)}, u32[]{:S(2)}, u32[]{:S(2)}) collective-permute-start(f32[16,32,128]{2,1,0:T(8,128)S(1)} %get-tuple-element.28), channel_id=1, source_target_pairs={{0,16},{16,32},{32,48},{48,64},{64,80},{80,96},{96,112},{112,128},... | collective-permute-start | bytes 786440 | tf_op jit(solution)/shard_map/ppermute | solution.py:265
  94.3 10.8 %collective-permute-start.2 = (f32[32,128]{1,0:T(8,128)S(1)}, f32[32,128]{1,0:T(8,128)S(1)}, u32[]{:S(2)}, u32[]{:S(2)}) collective-permute-start(f32[32,128]{1,0:T(8,128)S(1)} %get-tuple-element.12), channel_id=1, source_target_pairs={{0,16},{16,32},{32,48},{48,64},{64,80},{80,96},{96,112},{112,128},... | collective-permute-start | bytes 49160 | tf_op jit(solution)/shard_map/ppermute | solution.py:265
  96.2 8.9 %collective-permute-start.3 = (f32[32,128]{1,0:T(8,128)S(1)}, f32[32,128]{1,0:T(8,128)S(1)}, u32[]{:S(2)}, u32[]{:S(2)}) collective-permute-start(f32[32,128]{1,0:T(8,128)S(1)} %get-tuple-element.13), channel_id=1, source_target_pairs={{16,0},{32,16},{48,32},{64,48},{80,64},{96,80},{112,96},{128,112},... | collective-permute-start | bytes 49160 | tf_op jit(solution)/shard_map/ppermute | solution.py:265
  106.9 8.7 %copy-start.3 = (f32[4,7]{1,0:T(4,128)S(1)}, f32[4,7]{1,0:T(4,128)}, u32[]{:S(2)}) copy-start(f32[4,7]{1,0:T(4,128)} %param.10) | copy-start | bytes 340
  106.9 26.0 %all-to-all-start.2 = ((f32[16,64,128]{2,1,0:T(8,128)}), f32[16,64,128]{2,1,0:T(8,128)S(1)}, u32[]{:S(2)}, u32[]{:S(2)}) async-start(f32[16,64,128]{2,1,0:T(8,128)} %mend.2), calls=%async_computation.2 | async-start | bytes 1048576 | tf_op jit(solution)/shard_map/all_to_all | solution.py:373

commit v4 on v2

v4 whole, which is shorter than its diff:
```python
import functools

import jax
import jax.numpy as jnp
import numpy as np
from jax import lax
from jax.experimental import pallas as pl
from jax.experimental.pallas import tpu as pltpu
from jax.sharding import Mesh, PartitionSpec as P

TILE = 32
FRACS = 16
LANES = 128
INFO_ROWS = 8
PAIR = 2
TAPS = 4
SPAN = 40


def cubic_weights(fraction_index):
    fraction = fraction_index.astype(jnp.float32) / FRACS
    return (
        -fraction * (fraction - 1.0) * (fraction - 2.0) / 6.0,
        (fraction + 1.0) * (fraction - 1.0) * (fraction - 2.0) / 2.0,
        -(fraction + 1.0) * fraction * (fraction - 2.0) / 2.0,
        (fraction + 1.0) * fraction * (fraction - 1.0) / 6.0,
    )


def swapped():
    return lax.rem(lax.axis_index("group"), 2)


def pack_kernel(tile_rows, tile_cols, last_row, fields_ref, table_ref, out_ref, wide_ref, sem):
    count, cells = fields_ref.shape[0], fields_ref.shape[1]
    half = count // PAIR
    swap = swapped()
    copies = []
    for part in range(PAIR):
        source = lax.bitwise_xor(part, swap) * half
        copies.append(
            pltpu.make_async_copy(
                fields_ref.at[pl.ds(source, half)], out_ref.at[part * half : (part + 1) * half, 0:cells, :], sem.at[part]
            )
        )
    for copy in copies:
        copy.start()
    entries, tiles = table_ref.shape
    group = lax.axis_index("group")
    band = group * PAIR + lax.axis_index("part")
    wide_ref[...] = jnp.zeros(wide_ref.shape, jnp.int32)
    wide_ref[0:entries, 0:tiles] = table_ref[...]
    table = wide_ref[...]
    owner, dep_row, dep_col = table[0:1], table[1:2], table[2:3]
    shift_row, shift_col, frac_row, frac_col = table[3:4], table[4:5], table[5:6], table[6:7]
    dep_tile = jnp.clip(band * tile_rows - 1 + dep_row, 0, last_row)
    start = TILE * (dep_tile - (group * PAIR * tile_rows - 1)) + shift_row - 1
    column = TILE * dep_col + shift_col - 1
    wrapped = jnp.where(dep_col == tile_cols - 1, TILE, 0)
    position = lax.rem(lax.broadcasted_iota(jnp.int32, (1, LANES), 1), tile_cols)
    turn = lax.bitwise_and(LANES + TILE * position - column, LANES - 1)
    shape = (INFO_ROWS, LANES)
    index = lax.broadcasted_iota(jnp.int32, shape, 0)
    lane = lax.broadcasted_iota(jnp.int32, shape, 1)
    info = jnp.zeros(shape, jnp.float32)
    for place, value in enumerate(cubic_weights(frac_row) + cubic_weights(frac_col)):
        info = jnp.where(index == place, value, info)
    places = jnp.zeros(shape, jnp.int32)
    for place, value in enumerate((start, owner, wrapped, turn)):
        places = jnp.where(index == place, value, places)
    info = jnp.where(lane < tiles, info, pltpu.roll(places.astype(jnp.float32), tiles, 1))
    for block in range(count):
        out_ref[block, cells:, :] = info
    for copy in copies:
        copy.wait()


def parts(value):
    high = value.astype(jnp.bfloat16)
    return high, (value - high.astype(jnp.float32)).astype(jnp.bfloat16)


def tap_matrix():
    matrix = np.zeros((2 * LANES, (TAPS - 1) * LANES), np.float32)
    for tap in range(1, TAPS):
        for lane in range(LANES):
            odd = (lane // TILE) % 2
            matrix[odd * LANES + (lane + tap) % LANES, (tap - 1) * LANES + lane] = 1.0
    return jnp.asarray(matrix, jnp.bfloat16)


def beside_matrix():
    matrix = np.zeros((3 * LANES, LANES), np.float32)
    for lane in range(LANES):
        matrix[LANES + lane - 1, lane] = 1.0
        matrix[LANES + lane + 1, lane] = 1.0
    return jnp.asarray(matrix, jnp.bfloat16)


PAD = 8


def interpolate_kernel(
    places_ref, blocks_ref, north_ref, south_ref, taps_ref, phi_ref, top_ref, bottom_ref, ext_ref, pass_ref, sem
):
    chunks, halo = north_ref.shape[0], north_ref.shape[1]
    rows = phi_ref.shape[1] - 2 * PAD
    cells = rows // PAIR
    tile_rows = cells // TILE
    tile_cols = LANES // TILE
    tiles = tile_rows * tile_cols
    copies = [
        pltpu.make_async_copy(north_ref, ext_ref.at[:, 0:halo, :], sem.at[0]),
        pltpu.make_async_copy(south_ref, ext_ref.at[:, halo + rows : 2 * halo + rows, :], sem.at[1]),
    ]
    for band in range(PAIR):
        copies.append(
            pltpu.make_async_copy(
                blocks_ref.at[band * chunks : (band + 1) * chunks, 0:cells, :],
                ext_ref.at[:, halo + band * cells : halo + (band + 1) * cells, :],
                sem.at[2 + band],
            )
        )
    for copy in copies:
        copy.start()
    for chunk in range(chunks):
        phi_ref[chunk, 0:PAD, :] = jnp.zeros((PAD, LANES), jnp.float32)
        phi_ref[chunk, PAD + rows :, :] = jnp.zeros((PAD, LANES), jnp.float32)
    for copy in copies:
        copy.wait()
    lane = lax.broadcasted_iota(jnp.int32, (SPAN, LANES), 1)
    lane_info = lax.broadcasted_iota(jnp.int32, (INFO_ROWS, LANES), 1)
    first_even = lane < 48
    first_odd = (lane >= 16) & (lane < 80)
    even_group = lax.bitwise_and(lane, TILE) == 0
    together = pass_ref.shape[0] // tile_rows

    def windows(device, tile_row):
        def window(tile_col):
            tile = tile_row * tile_cols + tile_col
            start, source, wrapped, turn = (places_ref[device, place * tiles + tile] for place in range(4))
            after = lax.rem(source + 1, chunks)
            span = pl.ds(start, SPAN)
            return pltpu.roll(jnp.where(lane < wrapped, ext_ref[after, span, :], ext_ref[source, span, :]), turn, 1)

        return jnp.where(first_even, window(0), window(2)), jnp.where(first_odd, window(1), window(3))

    def step(index, carry):
        work = [(index * together + place, tile_row) for place in range(together) for tile_row in range(tile_rows)]
        pairs = [windows(*item) for item in work]
        evens = jnp.concatenate([pair[0] for pair in pairs], axis=0)
        odds = jnp.concatenate([pair[1] for pair in pairs], axis=0)
        even_parts, odd_parts = parts(evens), parts(odds)
        moved = None
        for which in range(2):
            part = jnp.dot(
                jnp.concatenate([even_parts[which], odd_parts[which]], axis=1),
                taps_ref[...],
                preferred_element_type=jnp.float32,
            )
            moved = part if moved is None else moved + part
        for slot, (device, tile_row) in enumerate(work):
            own = lane_info // TILE + tile_row * tile_cols
            weights = jnp.take_along_axis(blocks_ref[device, cells:, :], own, axis=1)
            total = weights[TAPS : TAPS + 1] * jnp.where(even_group, *pairs[slot])
            here = slice(slot * SPAN, (slot + 1) * SPAN)
            for tap in range(1, TAPS):
                total = total + weights[TAPS + tap : TAPS + tap + 1] * moved[here, (tap - 1) * LANES : tap * LANES]
            pass_ref[slot] = total
            total = None
            for tap in range(TAPS):
                value = weights[tap : tap + 1] * pass_ref[slot, tap : tap + TILE, :]
                total = value if total is None else total + value
            first = pl.multiple_of(PAD + (device // chunks) * cells + tile_row * TILE, PAD)
            phi_ref[lax.rem(device, chunks), pl.ds(first, TILE), :] = total
        return carry

    lax.fori_loop(0, PAIR * chunks // together, step, 0)
    for row in range(2):
        for chunk in range(chunks):
            place = row * chunks + chunk
            top_ref[place : place + 1, :] = phi_ref[chunk, PAD + row : PAD + row + 1, :]
            bottom_ref[place : place + 1, :] = phi_ref[chunk, PAD + rows - 2 + row : PAD + rows - 1 + row, :]


def own_coef(coef_ref, half):
    levels = coef_ref.shape[1]
    member = lax.bitwise_xor(lax.axis_index("part"), swapped()) * half + lax.axis_index("lon")
    return coef_ref[member // levels, lax.rem(member, levels)]


TOGETHER = 4


def diffuse_kernel(groups, coef_ref, phi_ref, beside_ref, psi_ref, lap_ref, high_ref, low_ref):
    chunks, rows = phi_ref.shape[0], phi_ref.shape[1] - 2 * PAD
    cells = rows // PAIR
    coef = own_coef(coef_ref, chunks)
    group = lax.axis_index("group")
    has_north = jnp.where(group > 0, 1.0, 0.0)
    has_south = jnp.where(group < groups - 1, 1.0, 0.0)
    together = min(TOGETHER, chunks)

    def laplacian(ref, store):
        for chunk in range(chunks):
            high, low = parts(ref[chunk, PAD : PAD + rows, :])
            high_ref[chunk], low_ref[chunk] = high, low

        def step(index, carry):
            members = [index * together + place for place in range(together)]
            sums = None
            for part_ref in (high_ref, low_ref):
                left = [
                    jnp.concatenate([part_ref[lax.rem(chunk + chunks + by, chunks)] for chunk in members], axis=0)
                    for by in (-1, 0, 1)
                ]
                part = jnp.dot(jnp.concatenate(left, axis=1), beside_ref[...], preferred_element_type=jnp.float32)
                sums = part if sums is None else sums + part
            for place, chunk in enumerate(members):
                around = ref[chunk, PAD + 1 : PAD + 1 + rows, :] + ref[chunk, PAD - 1 : PAD - 1 + rows, :]
                store(chunk, around + sums[place * rows : (place + 1) * rows] - 4.0 * ref[chunk, PAD : PAD + rows, :])
            return carry

        lax.fori_loop(0, chunks // together, step, 0)

    def keep(chunk, value):
        lap_ref[chunk, PAD : PAD + rows, :] = value
        lap_ref[chunk, PAD - 1 : PAD, :] = phi_ref[chunk, PAD : PAD + 1, :] * has_north
        lap_ref[chunk, PAD + rows : PAD + rows + 1, :] = phi_ref[chunk, PAD + rows - 1 : PAD + rows, :] * has_south

    def finish(chunk, value):
        psi = phi_ref[chunk, PAD : PAD + rows, :] - coef * value
        for band in range(PAIR):
            psi_ref[band * chunks + chunk] = psi[band * cells : (band + 1) * cells]

    laplacian(phi_ref, keep)
    laplacian(lap_ref, finish)


def mend_kernel(coef_ref, north_ref, south_ref, inner_ref, psi_ref):
    count, cells = psi_ref.shape[0], psi_ref.shape[1]
    chunks = count // PAIR
    coef = own_coef(coef_ref, chunks)
    shape = (chunks, LANES)
    lane = lax.broadcasted_iota(jnp.int32, shape, 1)

    def near_far(near, far):
        west = pltpu.roll(jnp.where(lane == LANES - 1, pltpu.roll(near, 1, 0), near), 1, 1)
        east = pltpu.roll(jnp.where(lane == 0, pltpu.roll(near, chunks - 1, 0), near), LANES - 1, 1)
        return coef * (far + 2.0 * (west + east) - 8.0 * near), coef * near

    psi_ref[...] = inner_ref[...]
    north = near_far(north_ref[chunks:, :], north_ref[0:chunks, :])
    south = near_far(south_ref[0:chunks, :], south_ref[chunks:, :])
    for chunk in range(chunks):
        low = chunk + (PAIR - 1) * chunks
        for row in range(2):
            here = slice(row, row + 1)
            psi_ref[chunk, here, :] = inner_ref[chunk, here, :] - north[row][chunk : chunk + 1]
            here = slice(cells - 1 - row, cells - row)
            psi_ref[low, here, :] = inner_ref[low, here, :] - south[row][chunk : chunk + 1]


def vertical_kernel(levels, lower_ref, upper_ref, inverse_ref, psi_ref, out_ref):
    field = pl.program_id(0)
    source = lax.bitwise_xor(field, swapped() * (pl.num_programs(0) // PAIR)) * levels
    step = 16
    for first in range(0, psi_ref.shape[1], step):
        rows = slice(first, first + step)
        sweep = []
        for level in range(levels):
            rhs = psi_ref[source + level, rows, :]
            if level:
                rhs = rhs + lower_ref[field, level] * sweep[-1]
            sweep.append(rhs * inverse_ref[field, level])
        value = sweep[-1]
        out_ref[0, levels - 1, rows, :] = value
        for level in range(levels - 2, -1, -1):
            value = sweep[level] - upper_ref[field, level] * value
            out_ref[0, level, rows, :] = value


def vertical_tables(vert_coef):
    fcount = vert_coef.shape[0]
    levels = vert_coef.shape[1] + 1
    zero_column = jnp.zeros((fcount, 1), jnp.float32)
    lower_coef = jnp.concatenate([zero_column, vert_coef], axis=1)
    upper_coef = jnp.concatenate([vert_coef, zero_column], axis=1)
    diagonal = 1.0 + lower_coef + upper_coef
    uppers, inverses = [], []
    for level in range(levels):
        denominator = diagonal[:, level]
        if level:
            denominator = denominator + lower_coef[:, level] * uppers[-1]
        inverses.append(1.0 / denominator)
        uppers.append(-upper_coef[:, level] / denominator)
    return lower_coef, jnp.stack(uppers, axis=1), jnp.stack(inverses, axis=1)


SMEM = pltpu.MemorySpace.SMEM
VMEM = pltpu.MemorySpace.VMEM


def smem():
    return pl.BlockSpec(memory_space=SMEM)


def vmem():
    return pl.BlockSpec(memory_space=VMEM)


def anywhere():
    return pl.BlockSpec(memory_space=pl.ANY)


def body(fields, hyper_coef, vert_coef, dep_owner, dep_row, dep_col, shifts, fracs):
    fcount, levels, cells, width = fields.shape
    count = fcount * levels
    chunks = lax.axis_size("lon")
    groups = lax.axis_size("group")
    tile_rows = cells // TILE
    tile_cols = width // TILE
    tiles = tile_rows * tile_cols
    rows = PAIR * cells
    f32 = jnp.float32
    limit = pltpu.CompilerParams(vmem_limit_bytes=48 * 1024 * 1024)

    table = jnp.concatenate(
        [
            dep_owner.reshape(1, tiles),
            dep_row.reshape(1, tiles),
            dep_col.reshape(1, tiles),
            shifts.reshape(tiles, 2).T,
            fracs.reshape(tiles, 2).T,
        ],
        axis=0,
    )
    blocks = pl.pallas_call(
        functools.partial(pack_kernel, tile_rows, tile_cols, groups * PAIR * tile_rows - 2),
        out_shape=jax.ShapeDtypeStruct((count, cells + INFO_ROWS, width), f32),
        in_specs=[anywhere(), vmem()],
        out_specs=vmem(),
        scratch_shapes=[pltpu.VMEM((8, LANES), jnp.int32), pltpu.SemaphoreType.DMA((PAIR,))],
        compiler_params=limit,
        name="pack",
    )(fields.reshape(count, cells, width), table)
    blocks = lax.all_to_all(blocks, ("part", "lon"), 0, 0, tiled=True)
    southward = [
        (group * PAIR + part, (group + 1) * PAIR + PAIR - 1 - part) for group in range(groups - 1) for part in range(PAIR)
    ]
    northward = [(target, source) for source, target in southward]
    bands = ("group", "part")
    north = lax.ppermute(blocks[(PAIR - 1) * chunks :, cells - TILE : cells, :], bands, southward)
    south = lax.ppermute(blocks[:chunks, :TILE, :], bands, northward)
    places = blocks[:, cells : cells + 4, tiles : 2 * tiles].astype(jnp.int32).reshape(PAIR * chunks, 4 * tiles)
    edge = jax.ShapeDtypeStruct((2 * chunks, width), f32)
    phi, top, bottom = pl.pallas_call(
        interpolate_kernel,
        out_shape=(jax.ShapeDtypeStruct((chunks, rows + 2 * PAD, width), f32), edge, edge),
        in_specs=[smem(), vmem(), vmem(), vmem(), vmem()],
        out_specs=(vmem(), vmem(), vmem()),
        scratch_shapes=[
            pltpu.VMEM((chunks, rows + 2 * TILE + 8, width), f32),
            pltpu.VMEM((min(8, chunks) * tile_rows, SPAN, width), f32),
            pltpu.SemaphoreType.DMA((2 + PAIR,)),
        ],
        compiler_params=limit,
        name="interpolate",
    )(places, blocks, north, south, tap_matrix())
    above = lax.ppermute(bottom, bands, southward)
    below = lax.ppermute(top, bands, northward)
    psi_shape = jax.ShapeDtypeStruct((count, cells, width), f32)
    inner = pl.pallas_call(
        functools.partial(diffuse_kernel, groups),
        out_shape=psi_shape,
        in_specs=[smem(), vmem(), vmem()],
        out_specs=vmem(),
        scratch_shapes=[
            pltpu.VMEM((chunks, rows + 2 * PAD, width), f32),
            pltpu.VMEM((chunks, rows, width), jnp.bfloat16),
            pltpu.VMEM((chunks, rows, width), jnp.bfloat16),
        ],
        compiler_params=limit,
        name="diffuse",
    )(hyper_coef, phi, beside_matrix())
    psi = pl.pallas_call(
        mend_kernel,
        out_shape=psi_shape,
        in_specs=[smem(), vmem(), vmem(), vmem()],
        out_specs=vmem(),
        compiler_params=limit,
        name="mend",
    )(hyper_coef, above, below, inner)
    psi = lax.all_to_all(psi, ("part", "lon"), 0, 0, tiled=True)
    lower, upper, inverse = vertical_tables(vert_coef)
    return pl.pallas_call(
        functools.partial(vertical_kernel, levels),
        grid=(fcount,),
        out_shape=jax.ShapeDtypeStruct((fcount, levels, cells, width), f32),
        in_specs=[smem(), smem(), smem(), vmem()],
        out_specs=pl.BlockSpec((1, levels, cells, width), lambda field: (field, 0, 0, 0)),
        compiler_params=limit,
    )(lower, upper, inverse, psi)


def solution(mesh):
    lat, lon = mesh.shape["lat"], mesh.shape["lon"]
    grouped = Mesh(mesh.devices.reshape(lat // PAIR, PAIR, lon), ("group", "part", "lon"))
    bands = ("group", "part")
    cells = P(None, None, bands, "lon")
    tiles = P(bands, "lon", None, None)
    return jax.shard_map(
        body,
        mesh=grouped,
        in_specs=(cells, P(), P(), tiles, tiles, tiles, tiles, tiles),
        out_specs=cells,
        check_vma=False,
    )
```

time: 120 us -> 114 us (0.950)
  Pallas kernels: 15.6 us -> 12.4 us
  local copies, waits for them, and re-layouts: 4.97 us -> 2.41 us
    unnamed x16 -> x10, local copies, waits for them, and re-layouts: 4.56 us -> 1.24 us
    pallas_call x1, Pallas kernels: 6.55 us -> 4.46 us  [body(): pl.pallas_call(interpolate_kernel, out_shape=(jax.ShapeDtypeStruct((chunk...]
    pallas_call x2, Pallas kernels: 6.59 us -> 5.38 us  [the longest x1 3.73 us: body(): pl.pallas_call(functools.partial(diffuse_kernel, groups), out_shape=psi_s...]
  transfers between devices with their start and end apart: 5 -> 5, of which waited for: 2 -> 3; matrix products, arithmetic and copies ran while one was open for 1% -> 1% of each run, Pallas kernels for 4% -> 3%
where the time goes in v4:
time: 114 us
  blocking collectives  41.3 us (36%)
  waiting for transfers between devices  37.7 us (33%)
  starting transfers between devices  19.6 us (17%)
  Pallas kernels  12.4 us (11%)
  local copies, waits for them, and re-layouts  2.41 us (2%)
    all_to_all x1, blocking collectives, body(): blocks = lax.all_to_all(blocks, ('part', 'lon'), 0, 0, tiled=True)  41.3 us
    all_to_all x1, waiting for transfers between devices, body(): psi = lax.all_to_all(psi, ('part', 'lon'), 0, 0, tiled=True)  28.5 us
    ppermute x1, waiting for transfers between devices, body(): south = lax.ppermute(blocks[:chunks, :TILE, :], bands, northward)  8.83 us
    ppermute x1, starting transfers between devices, body(): above = lax.ppermute(bottom, bands, southward)  5.24 us
    pallas_call x1, Pallas kernels, body(): pl.pallas_call(interpolate_kernel, out_shape=(jax.ShapeDtypeStruct((chunk...  4.46 us
    all_to_all x1, starting transfers between devices, body(): psi = lax.all_to_all(psi, ('part', 'lon'), 0, 0, tiled=True)  4.45 us
    ppermute x1, starting transfers between devices, body(): south = lax.ppermute(blocks[:chunks, :TILE, :], bands, northward)  3.96 us
    pallas_call x1, Pallas kernels, body(): pl.pallas_call(functools.partial(diffuse_kernel, groups), out_shape=psi_s...  3.73 us
  transfers between devices with their start and end apart: 5, of which 3 were waited for; matrix products, arithmetic and copies ran while one was open for 1% of the time, Pallas kernels for 3%

profile of v4, /device:TPU:36, one launch (start us, length us, event | category | flops | bytes accessed | tf_op | source)
XLA Modules:
  0.0 114.1 jit_solution(15690387253570412949)
XLA Ops:
  0.0 0.8 concatenate.11.table_ref
  0.8 0.0 copy-start
  0.8 1.2 %copy-done = f32[4,8,64,128]{3,2,1,0:T(8,128)S(1)} copy-done((f32[4,8,64,128]{3,2,1,0:T(8,128)S(1)}, f32[4,8,64,128]{3,2,1,0:T(8,128)}, u32[]{:S(2)}) %copy-start) | copy-done | bytes 1048600
  2.0 0.2 pack.1
  2.2 41.3 %all_to_all.10.blocks_ref = f32[32,72,128]{2,1,0:T(8,128)S(1)} all-to-all(f32[32,72,128]{2,1,0:T(8,128)S(1)} %pack.1), channel_id=1, replica_groups=mesh['group'=8,'part'=2,'lon'=16] {'part','lon'}, dimensions={0} | all-to-all | bytes 2359296 | tf_op jit(solution)/shard_map/all_to_all | solution.py:347
  43.5 0.0 copy-start.1
  43.5 0.1 fusion
  43.6 0.0 copy-start.2
  43.6 0.0 copy-start.3
  43.6 4.0 %collective-permute-start.1 = (f32[16,32,128]{2,1,0:T(8,128)S(1)}, f32[16,32,128]{2,1,0:T(8,128)S(1)}, u32[]{:S(2)}, u32[]{:S(2)}) collective-permute-start(f32[16,32,128]{2,1,0:T(8,128)S(1)} %get-tuple-element.19), channel_id=1, source_target_pairs={{48,0},{32,16},{80,32},{64,48},{112,64},{96,80},{144,96},{128,112}... | collective-permute-start | bytes 786440 | tf_op jit(solution)/shard_map/ppermute | solution.py:354
  47.6 3.2 %collective-permute-start = (f32[16,32,128]{2,1,0:T(8,128)S(1)}, f32[16,32,128]{2,1,0:T(8,128)S(1)}, u32[]{:S(2)}, u32[]{:S(2)}) collective-permute-start(f32[16,32,128]{2,1,0:T(8,128)S(1)} %get-tuple-element.20), channel_id=1, source_target_pairs={{0,48},{16,32},{32,80},{48,64},{64,112},{80,96},{96,144},{112,128}... | collective-permute-start | bytes 786440 | tf_op jit(solution)/shard_map/ppermute | solution.py:353
  50.8 0.1 slice_convert_fusion
  50.9 0.1 copy.13
  51.0 0.1 copy.14.places_ref
  51.1 8.8 %collective-permute-done.1.south_ref = f32[16,32,128]{2,1,0:T(8,128)S(1)} collective-permute-done((f32[16,32,128]{2,1,0:T(8,128)S(1)}, f32[16,32,128]{2,1,0:T(8,128)S(1)}, u32[]{:S(2)}, u32[]{:S(2)}) %collective-permute-start.1) | collective-permute-done | bytes 262176 | tf_op jit(solution)/shard_map/ppermute | solution.py:354
  59.9 0.0 collective-permute-done.north_ref
  59.9 0.0 copy-done.1
  59.9 4.5 %interpolate.1 = (f32[16,144,128]{2,1,0:T(8,128)S(1)}, f32[32,128]{1,0:T(8,128)S(1)}, f32[32,128]{1,0:T(8,128)S(1)}) custom-call(s32[32,32]{1,0:T(8,128)S(1)} %copy.14.places_ref, f32[32,72,128]{2,1,0:T(8,128)S(1)} %all_to_all.10.blocks_ref, f32[16,32,128]{2,1,0:T(8,128)S(1)} %collective-permute-done.north_ref, ...), custom_call_target="tpu_custom_call" | custom-call | tf_op jit(solution)/shard_map/interpolate/pallas_call | solution.py:357
  64.4 5.2 %collective-permute-start.2 = (f32[32,128]{1,0:T(8,128)S(1)}, f32[32,128]{1,0:T(8,128)S(1)}, u32[]{:S(2)}, u32[]{:S(2)}) collective-permute-start(f32[32,128]{1,0:T(8,128)S(1)} %get-tuple-element.8), channel_id=1, source_target_pairs={{0,48},{16,32},{32,80},{48,64},{64,112},{80,96},{96,144},{112,128}... | collective-permute-start | bytes 49160 | tf_op jit(solution)/shard_map/ppermute | solution.py:370
  69.6 2.7 %collective-permute-start.3 = (f32[32,128]{1,0:T(8,128)S(1)}, f32[32,128]{1,0:T(8,128)S(1)}, u32[]{:S(2)}, u32[]{:S(2)}) collective-permute-start(f32[32,128]{1,0:T(8,128)S(1)} %get-tuple-element.9), channel_id=1, source_target_pairs={{48,0},{32,16},{80,32},{64,48},{112,64},{96,80},{144,96},{128,112}... | collective-permute-start | bytes 49160 | tf_op jit(solution)/shard_map/ppermute | solution.py:371
  72.3 0.0 copy-done.2
  72.3 0.0 copy-done.3
  72.4 3.7 %diffuse.1.inner_ref = f32[32,64,128]{2,1,0:T(8,128)S(1)} custom-call(f32[4,8]{1,0:T(4,128)S(1)} %copy-done.3, f32[16,144,128]{2,1,0:T(8,128)S(1)} %get-tuple-element.10.phi_ref, bf16[384,128]{1,0:T(8,128)(2,1)S(1)} %copy-done.2), custom_call_target="tpu_custom_call" | custom-call | tf_op jit(solution)/shard_map/diffuse/pallas_call | solution.py:373
  76.1 0.0 collective-permute-done.2.north_ref
  76.1 0.3 collective-permute-done.3.south_ref
  76.5 1.6 %mend.1 = f32[32,64,128]{2,1,0:T(8,128)} custom-call(f32[4,8]{1,0:T(4,128)S(1)} %copy-done.3, f32[32,128]{1,0:T(8,128)S(1)} %collective-permute-done.2.north_ref, f32[32,128]{1,0:T(8,128)S(1)} %collective-permute-done.3.south_ref, f32[32,64,128]{2,1,0:T(8,128)S(1)} %diffuse.1.inner_ref), custom_call_target="tpu_custom_call" | custom-call | tf_op jit(solution)/shard_map/mend/pallas_call | solution.py:386
  78.1 0.0 copy-start.4
  78.1 4.5 %all-to-all-start.1 = ((f32[32,64,128]{2,1,0:T(8,128)}), f32[32,64,128]{2,1,0:T(8,128)S(1)}, u32[]{:S(2)}, u32[]{:S(2)}) async-start(f32[32,64,128]{2,1,0:T(8,128)} %mend.1), calls=%async_computation.1 | async-start | bytes 2097152 | tf_op jit(solution)/shard_map/all_to_all | solution.py:394
  82.6 0.0 copy-done.4
  82.6 0.1 pad_add_fusion
  82.7 0.1 broadcast_divide_fusion
  82.8 0.1 broadcast_divide_fusion.1
  82.9 0.1 stack.4.upper_ref
  83.0 0.1 broadcast_divide_fusion.6
  83.1 0.1 stack.5.inverse_ref
  83.2 28.5 %all-to-all-done.1.psi_ref = f32[32,64,128]{2,1,0:T(8,128)S(1)} async-done(((f32[32,64,128]{2,1,0:T(8,128)}), f32[32,64,128]{2,1,0:T(8,128)S(1)}, u32[]{:S(2)}, u32[]{:S(2)}) %all-to-all-start.1) | async-done | bytes 1048608 | tf_op jit(solution)/shard_map/all_to_all | solution.py:394
  111.7 2.4 %shard_map.100 = f32[4,8,64,128]{3,2,1,0:T(8,128)} custom-call(f32[4,8]{1,0:T(4,128)S(1)} %get-tuple-element.29.lower_ref, f32[4,8]{1,0:T(4,128)S(1)} %stack.4.upper_ref, f32[4,8]{1,0:T(4,128)S(1)} %stack.5.inverse_ref, f32[32,64,128]{2,1,0:T(8,128)S(1)} %all-to-all-done.1.psi_ref), custom_call_target="tpu_custom_call" | custom-call | tf_op jit(solution)/shard_map/pallas_call | solution.py:396
Async XLA Ops:
  0.8 1.2 %copy-start = (f32[4,8,64,128]{3,2,1,0:T(8,128)S(1)}, f32[4,8,64,128]{3,2,1,0:T(8,128)}, u32[]{:S(2)}) copy-start(f32[4,8,64,128]{3,2,1,0:T(8,128)} %param.10) | copy-start | bytes 3145732
  43.5 16.4 %copy-start.1 = (bf16[256,384]{1,0:T(8,128)(2,1)S(1)}, bf16[256,384]{1,0:T(8,128)(2,1)}, u32[]{:S(2)}) copy-start(bf16[256,384]{1,0:T(8,128)(2,1)} %constant.4.clone.taps_ref) | copy-start | bytes 589828
  43.6 28.8 %copy-start.2 = (bf16[384,128]{1,0:T(8,128)(2,1)S(1)}, bf16[384,128]{1,0:T(8,128)(2,1)}, u32[]{:S(2)}) copy-start(bf16[384,128]{1,0:T(8,128)(2,1)} %constant.12.clone.beside_ref) | copy-start | bytes 294916
  43.6 28.8 %copy-start.3 = (f32[4,8]{1,0:T(4,128)S(1)}, f32[4,8]{1,0:T(4,128)}, u32[]{:S(2)}) copy-start(f32[4,8]{1,0:T(4,128)} %coef_ref.3) | copy-start | bytes 388
  43.6 16.3 %collective-permute-start.1 = (f32[16,32,128]{2,1,0:T(8,128)S(1)}, f32[16,32,128]{2,1,0:T(8,128)S(1)}, u32[]{:S(2)}, u32[]{:S(2)}) collective-permute-start(f32[16,32,128]{2,1,0:T(8,128)S(1)} %get-tuple-element.19), channel_id=1, source_target_pairs={{48,0},{32,16},{80,32},{64,48},{112,64},{96,80},{144,96},{128,112}... | collective-permute-start | bytes 786440 | tf_op jit(solution)/shard_map/ppermute | solution.py:354
  47.6 12.3 %collective-permute-start = (f32[16,32,128]{2,1,0:T(8,128)S(1)}, f32[16,32,128]{2,1,0:T(8,128)S(1)}, u32[]{:S(2)}, u32[]{:S(2)}) collective-permute-start(f32[16,32,128]{2,1,0:T(8,128)S(1)} %get-tuple-element.20), channel_id=1, source_target_pairs={{0,48},{16,32},{32,80},{48,64},{64,112},{80,96},{96,144},{112,128}... | collective-permute-start | bytes 786440 | tf_op jit(solution)/shard_map/ppermute | solution.py:353
  64.4 11.7 %collective-permute-start.2 = (f32[32,128]{1,0:T(8,128)S(1)}, f32[32,128]{1,0:T(8,128)S(1)}, u32[]{:S(2)}, u32[]{:S(2)}) collective-permute-start(f32[32,128]{1,0:T(8,128)S(1)} %get-tuple-element.8), channel_id=1, source_target_pairs={{0,48},{16,32},{32,80},{48,64},{64,112},{80,96},{96,144},{112,128}... | collective-permute-start | bytes 49160 | tf_op jit(solution)/shard_map/ppermute | solution.py:370
  69.6 6.8 %collective-permute-start.3 = (f32[32,128]{1,0:T(8,128)S(1)}, f32[32,128]{1,0:T(8,128)S(1)}, u32[]{:S(2)}, u32[]{:S(2)}) collective-permute-start(f32[32,128]{1,0:T(8,128)S(1)} %get-tuple-element.9), channel_id=1, source_target_pairs={{48,0},{32,16},{80,32},{64,48},{112,64},{96,80},{144,96},{128,112}... | collective-permute-start | bytes 49160 | tf_op jit(solution)/shard_map/ppermute | solution.py:371
  78.1 4.5 %copy-start.4 = (f32[4,7]{1,0:T(4,128)S(1)}, f32[4,7]{1,0:T(4,128)}, u32[]{:S(2)}) copy-start(f32[4,7]{1,0:T(4,128)} %param.12) | copy-start | bytes 340
  78.1 33.6 %all-to-all-start.1 = ((f32[32,64,128]{2,1,0:T(8,128)}), f32[32,64,128]{2,1,0:T(8,128)S(1)}, u32[]{:S(2)}, u32[]{:S(2)}) async-start(f32[32,64,128]{2,1,0:T(8,128)} %mend.1), calls=%async_computation.1 | async-start | bytes 2097152 | tf_op jit(solution)/shard_map/all_to_all | solution.py:394

commit v5 on v4

--- a/solution.py
+++ b/solution.py
@@ -237,21 +237,25 @@
     laplacian(lap_ref, finish)
 
 
-def mend_kernel(coef_ref, north_ref, south_ref, inner_ref, psi_ref):
+def mend_kernel(groups, coef_ref, north_ref, south_ref, inner_ref, psi_ref):
     count, cells = psi_ref.shape[0], psi_ref.shape[1]
     chunks = count // PAIR
     coef = own_coef(coef_ref, chunks)
     shape = (chunks, LANES)
     lane = lax.broadcasted_iota(jnp.int32, shape, 1)
 
-    def near_far(near, far):
+    group = lax.axis_index("group")
+    has_north = jnp.where(group > 0, 1.0, 0.0)
+    has_south = jnp.where(group < groups - 1, 1.0, 0.0)
+
+    def near_far(near, far, coef):
         west = pltpu.roll(jnp.where(lane == LANES - 1, pltpu.roll(near, 1, 0), near), 1, 1)
         east = pltpu.roll(jnp.where(lane == 0, pltpu.roll(near, chunks - 1, 0), near), LANES - 1, 1)
         return coef * (far + 2.0 * (west + east) - 8.0 * near), coef * near
 
     psi_ref[...] = inner_ref[...]
-    north = near_far(north_ref[chunks:, :], north_ref[0:chunks, :])
-    south = near_far(south_ref[0:chunks, :], south_ref[chunks:, :])
+    north = near_far(north_ref[chunks:, :], north_ref[0:chunks, :], coef * has_north)
+    south = near_far(south_ref[0:chunks, :], south_ref[chunks:, :], coef * has_south)
     for chunk in range(chunks):
         low = chunk + (PAIR - 1) * chunks
         for row in range(2):
@@ -261,23 +265,31 @@
             psi_ref[low, here, :] = inner_ref[low, here, :] - south[row][chunk : chunk + 1]
 
 
-def vertical_kernel(levels, lower_ref, upper_ref, inverse_ref, psi_ref, out_ref):
-    field = pl.program_id(0)
-    source = lax.bitwise_xor(field, swapped() * (pl.num_programs(0) // PAIR)) * levels
+def vertical_kernel(lower_ref, upper_ref, inverse_ref, psi_ref, out_ref, held_ref, sem):
+    fcount, levels, cells, _ = held_ref.shape
     step = 16
-    for first in range(0, psi_ref.shape[1], step):
-        rows = slice(first, first + step)
-        sweep = []
-        for level in range(levels):
-            rhs = psi_ref[source + level, rows, :]
-            if level:
-                rhs = rhs + lower_ref[field, level] * sweep[-1]
-            sweep.append(rhs * inverse_ref[field, level])
-        value = sweep[-1]
-        out_ref[0, levels - 1, rows, :] = value
-        for level in range(levels - 2, -1, -1):
-            value = sweep[level] - upper_ref[field, level] * value
-            out_ref[0, level, rows, :] = value
+    copies = []
+    swap = swapped()
+    for field in range(fcount):
+        source = lax.bitwise_xor(field, swap * (fcount // PAIR)) * levels
+        for first in range(0, cells, step):
+            rows = slice(first, first + step)
+            sweep = []
+            for level in range(levels):
+                rhs = psi_ref[source + level, rows, :]
+                if level:
+                    rhs = rhs + lower_ref[field, level] * sweep[-1]
+                sweep.append(rhs * inverse_ref[field, level])
+            value = sweep[-1]
+            held_ref[field, levels - 1, rows, :] = value
+            for level in range(levels - 2, -1, -1):
+                value = sweep[level] - upper_ref[field, level] * value
+                held_ref[field, level, rows, :] = value
+        copy = pltpu.make_async_copy(held_ref.at[field], out_ref.at[field], sem.at[field])
+        copy.start()
+        copies.append(copy)
+    for copy in copies:
+        copy.wait()
 
 
 def vertical_tables(vert_coef):
@@ -346,7 +358,7 @@
     )(fields.reshape(count, cells, width), table)
     blocks = lax.all_to_all(blocks, ("part", "lon"), 0, 0, tiled=True)
     southward = [
-        (group * PAIR + part, (group + 1) * PAIR + PAIR - 1 - part) for group in range(groups - 1) for part in range(PAIR)
+        (group * PAIR + part, (group + 1) % groups * PAIR + PAIR - 1 - part) for group in range(groups) for part in range(PAIR)
     ]
     northward = [(target, source) for source, target in southward]
     bands = ("group", "part")
@@ -384,7 +396,7 @@
         name="diffuse",
     )(hyper_coef, phi, beside_matrix())
     psi = pl.pallas_call(
-        mend_kernel,
+        functools.partial(mend_kernel, groups),
         out_shape=psi_shape,
         in_specs=[smem(), vmem(), vmem(), vmem()],
         out_specs=vmem(),
@@ -394,12 +406,13 @@
     psi = lax.all_to_all(psi, ("part", "lon"), 0, 0, tiled=True)
     lower, upper, inverse = vertical_tables(vert_coef)
     return pl.pallas_call(
-        functools.partial(vertical_kernel, levels),
-        grid=(fcount,),
+        vertical_kernel,
         out_shape=jax.ShapeDtypeStruct((fcount, levels, cells, width), f32),
         in_specs=[smem(), smem(), smem(), vmem()],
-        out_specs=pl.BlockSpec((1, levels, cells, width), lambda field: (field, 0, 0, 0)),
+        out_specs=anywhere(),
+        scratch_shapes=[pltpu.VMEM((fcount, levels, cells, width), f32), pltpu.SemaphoreType.DMA((fcount,))],
         compiler_params=limit,
+        name="solve",
     )(lower, upper, inverse, psi)
 
 

time: 114 us -> 110 us (0.965); the launches traced: 114 us -> 108 us
  starting transfers between devices: 19.6 us -> 12.3 us
  waiting for transfers between devices: 37.7 us -> 39.3 us
    ppermute x1, starting transfers between devices: 5.24 us -> 3.01 us  [body(): above = lax.ppermute(bottom, bands, southward)]
    ppermute x1, starting transfers between devices: 3.96 us -> 2 us  [body(): south = lax.ppermute(blocks[:chunks, :TILE, :], bands, northward)]
    ppermute x1, waiting for transfers between devices: 8.83 us -> 10.8 us  [body(): south = lax.ppermute(blocks[:chunks, :TILE, :], bands, northward)]
    ppermute x1, starting transfers between devices: 3.23 us -> 1.32 us  [body(): lax.ppermute(blocks[(PAIR - 1) * chunks:, cells - TILE:cells, :], bands,...]
    ppermute x1, starting transfers between devices: 2.71 us -> 1.2 us  [body(): below = lax.ppermute(top, bands, northward)]
  transfers between devices with their start and end apart: 5 -> 5, of which waited for: 3 -> 2; matrix products, arithmetic and copies ran while one was open for 1% -> 1% of each run, Pallas kernels for 3% -> 3%
where the time goes in v5:
time: 110 us; the launch traced here: 108 us
  blocking collectives  41.3 us (38%)
  waiting for transfers between devices  39.3 us (36%)
  starting transfers between devices  12.3 us (11%)
  Pallas kernels  11.7 us (11%)
  local copies, waits for them, and re-layouts  2.41 us (2%)
    all_to_all x1, blocking collectives, body(): blocks = lax.all_to_all(blocks, ('part', 'lon'), 0, 0, tiled=True)  41.3 us
    all_to_all x1, waiting for transfers between devices, body(): psi = lax.all_to_all(psi, ('part', 'lon'), 0, 0, tiled=True)  28.5 us
    ppermute x1, waiting for transfers between devices, body(): south = lax.ppermute(blocks[:chunks, :TILE, :], bands, northward)  10.8 us
    all_to_all x1, starting transfers between devices, body(): psi = lax.all_to_all(psi, ('part', 'lon'), 0, 0, tiled=True)  4.78 us
    pallas_call x1, Pallas kernels, body(): pl.pallas_call(interpolate_kernel, out_shape=(jax.ShapeDtypeStruct((chunk...  4.46 us
    pallas_call x1, Pallas kernels, body(): pl.pallas_call(functools.partial(diffuse_kernel, groups), out_shape=psi_s...  3.73 us
    ppermute x1, starting transfers between devices, body(): above = lax.ppermute(bottom, bands, southward)  3.01 us
  transfers between devices with their start and end apart: 5, of which 2 were waited for; matrix products, arithmetic and copies ran while one was open for 1% of the time, Pallas kernels for 3%

profile of v5, /device:TPU:36, one launch (start us, length us, event | category | flops | bytes accessed | tf_op | source)
XLA Modules:
  0.0 107.6 jit_solution(3797221093993426566)
XLA Ops:
  0.0 0.8 concatenate.11.table_ref
  0.8 0.0 copy-start
  0.8 1.2 %copy-done = f32[4,8,64,128]{3,2,1,0:T(8,128)S(1)} copy-done((f32[4,8,64,128]{3,2,1,0:T(8,128)S(1)}, f32[4,8,64,128]{3,2,1,0:T(8,128)}, u32[]{:S(2)}) %copy-start) | copy-done | bytes 1048600
  2.0 0.2 pack.1
  2.2 41.3 %all_to_all.10.blocks_ref = f32[32,72,128]{2,1,0:T(8,128)S(1)} all-to-all(f32[32,72,128]{2,1,0:T(8,128)S(1)} %pack.1), channel_id=1, replica_groups=mesh['group'=8,'part'=2,'lon'=16] {'part','lon'}, dimensions={0} | all-to-all | bytes 2359296 | tf_op jit(solution)/shard_map/all_to_all | solution.py:359
  43.5 0.0 copy-start.1
  43.5 0.1 fusion
  43.6 0.0 copy-start.2
  43.6 0.0 copy-start.3
  43.6 2.0 %collective-permute-start.1 = (f32[16,32,128]{2,1,0:T(8,128)S(1)}, f32[16,32,128]{2,1,0:T(8,128)S(1)}, u32[]{:S(2)}, u32[]{:S(2)}) collective-permute-start(f32[16,32,128]{2,1,0:T(8,128)S(1)} %get-tuple-element.19), channel_id=1, source_target_pairs={{48,0},{32,16},{80,32},{64,48},{112,64},{96,80},{144,96},{128,112}... | collective-permute-start | bytes 786440 | tf_op jit(solution)/shard_map/ppermute | solution.py:366
  45.6 1.3 %collective-permute-start = (f32[16,32,128]{2,1,0:T(8,128)S(1)}, f32[16,32,128]{2,1,0:T(8,128)S(1)}, u32[]{:S(2)}, u32[]{:S(2)}) collective-permute-start(f32[16,32,128]{2,1,0:T(8,128)S(1)} %get-tuple-element.20), channel_id=1, source_target_pairs={{0,48},{16,32},{32,80},{48,64},{64,112},{80,96},{96,144},{112,128}... | collective-permute-start | bytes 786440 | tf_op jit(solution)/shard_map/ppermute | solution.py:365
  46.9 0.1 slice_convert_fusion
  47.0 0.1 copy.13
  47.1 0.1 copy.14.places_ref
  47.2 10.8 %collective-permute-done.1.south_ref = f32[16,32,128]{2,1,0:T(8,128)S(1)} collective-permute-done((f32[16,32,128]{2,1,0:T(8,128)S(1)}, f32[16,32,128]{2,1,0:T(8,128)S(1)}, u32[]{:S(2)}, u32[]{:S(2)}) %collective-permute-start.1) | collective-permute-done | bytes 262176 | tf_op jit(solution)/shard_map/ppermute | solution.py:366
  57.9 0.0 collective-permute-done.north_ref
  58.0 0.0 copy-done.1
  58.0 4.5 %interpolate.1 = (f32[16,144,128]{2,1,0:T(8,128)S(1)}, f32[32,128]{1,0:T(8,128)S(1)}, f32[32,128]{1,0:T(8,128)S(1)}) custom-call(s32[32,32]{1,0:T(8,128)S(1)} %copy.14.places_ref, f32[32,72,128]{2,1,0:T(8,128)S(1)} %all_to_all.10.blocks_ref, f32[16,32,128]{2,1,0:T(8,128)S(1)} %collective-permute-done.north_ref, ...), custom_call_target="tpu_custom_call" | custom-call | tf_op jit(solution)/shard_map/interpolate/pallas_call | solution.py:369
  62.4 3.0 %collective-permute-start.2 = (f32[32,128]{1,0:T(8,128)S(1)}, f32[32,128]{1,0:T(8,128)S(1)}, u32[]{:S(2)}, u32[]{:S(2)}) collective-permute-start(f32[32,128]{1,0:T(8,128)S(1)} %get-tuple-element.8), channel_id=1, source_target_pairs={{0,48},{16,32},{32,80},{48,64},{64,112},{80,96},{96,144},{112,128}... | collective-permute-start | bytes 49160 | tf_op jit(solution)/shard_map/ppermute | solution.py:382
  65.4 1.2 %collective-permute-start.3 = (f32[32,128]{1,0:T(8,128)S(1)}, f32[32,128]{1,0:T(8,128)S(1)}, u32[]{:S(2)}, u32[]{:S(2)}) collective-permute-start(f32[32,128]{1,0:T(8,128)S(1)} %get-tuple-element.9), channel_id=1, source_target_pairs={{48,0},{32,16},{80,32},{64,48},{112,64},{96,80},{144,96},{128,112}... | collective-permute-start | bytes 49160 | tf_op jit(solution)/shard_map/ppermute | solution.py:383
  66.6 0.0 copy-done.2
  66.6 0.0 copy-done.3
  66.6 3.7 %diffuse.1.inner_ref = f32[32,64,128]{2,1,0:T(8,128)S(1)} custom-call(f32[4,8]{1,0:T(4,128)S(1)} %copy-done.3, f32[16,144,128]{2,1,0:T(8,128)S(1)} %get-tuple-element.10.phi_ref, bf16[384,128]{1,0:T(8,128)(2,1)S(1)} %copy-done.2), custom_call_target="tpu_custom_call" | custom-call | tf_op jit(solution)/shard_map/diffuse/pallas_call | solution.py:385
  70.4 0.0 collective-permute-done.2.north_ref
  70.4 0.0 collective-permute-done.3.south_ref
  70.4 1.6 %mend.1 = f32[32,64,128]{2,1,0:T(8,128)} custom-call(f32[4,8]{1,0:T(4,128)S(1)} %copy-done.3, f32[32,128]{1,0:T(8,128)S(1)} %collective-permute-done.2.north_ref, f32[32,128]{1,0:T(8,128)S(1)} %collective-permute-done.3.south_ref, f32[32,64,128]{2,1,0:T(8,128)S(1)} %diffuse.1.inner_ref), custom_call_target="tpu_custom_call" | custom-call | tf_op jit(solution)/shard_map/mend/pallas_call | solution.py:398
  72.0 0.0 copy-start.4
  72.0 4.8 %all-to-all-start.1 = ((f32[32,64,128]{2,1,0:T(8,128)}), f32[32,64,128]{2,1,0:T(8,128)S(1)}, u32[]{:S(2)}, u32[]{:S(2)}) async-start(f32[32,64,128]{2,1,0:T(8,128)} %mend.1), calls=%async_computation.1 | async-start | bytes 2097152 | tf_op jit(solution)/shard_map/all_to_all | solution.py:406
  76.8 0.0 copy-done.4
  76.9 0.1 pad_add_fusion
  76.9 0.1 broadcast_divide_fusion
  77.0 0.1 broadcast_divide_fusion.1
  77.2 0.1 stack.4.upper_ref
  77.3 0.1 broadcast_divide_fusion.6
  77.3 0.1 stack.5.inverse_ref
  77.4 28.5 %all-to-all-done.1.psi_ref = f32[32,64,128]{2,1,0:T(8,128)S(1)} async-done(((f32[32,64,128]{2,1,0:T(8,128)}), f32[32,64,128]{2,1,0:T(8,128)S(1)}, u32[]{:S(2)}, u32[]{:S(2)}) %all-to-all-start.1) | async-done | bytes 1048608 | tf_op jit(solution)/shard_map/all_to_all | solution.py:406
  105.9 1.7 %solve.1 = f32[4,8,64,128]{3,2,1,0:T(8,128)} custom-call(f32[4,8]{1,0:T(4,128)S(1)} %get-tuple-element.29.lower_ref, f32[4,8]{1,0:T(4,128)S(1)} %stack.4.upper_ref, f32[4,8]{1,0:T(4,128)S(1)} %stack.5.inverse_ref, f32[32,64,128]{2,1,0:T(8,128)S(1)} %all-to-all-done.1.psi_ref), custom_call_target="tpu_custom_call" | custom-call | tf_op jit(solution)/shard_map/solve/pallas_call | solution.py:408
Async XLA Ops:
  0.8 1.2 %copy-start = (f32[4,8,64,128]{3,2,1,0:T(8,128)S(1)}, f32[4,8,64,128]{3,2,1,0:T(8,128)}, u32[]{:S(2)}) copy-start(f32[4,8,64,128]{3,2,1,0:T(8,128)} %param.10) | copy-start | bytes 3145732
  43.5 14.4 %copy-start.1 = (bf16[256,384]{1,0:T(8,128)(2,1)S(1)}, bf16[256,384]{1,0:T(8,128)(2,1)}, u32[]{:S(2)}) copy-start(bf16[256,384]{1,0:T(8,128)(2,1)} %constant.4.clone.taps_ref) | copy-start | bytes 589828
  43.6 23.1 %copy-start.2 = (bf16[384,128]{1,0:T(8,128)(2,1)S(1)}, bf16[384,128]{1,0:T(8,128)(2,1)}, u32[]{:S(2)}) copy-start(bf16[384,128]{1,0:T(8,128)(2,1)} %constant.12.clone.beside_ref) | copy-start | bytes 294916
  43.6 23.0 %copy-start.3 = (f32[4,8]{1,0:T(4,128)S(1)}, f32[4,8]{1,0:T(4,128)}, u32[]{:S(2)}) copy-start(f32[4,8]{1,0:T(4,128)} %coef_ref.3) | copy-start | bytes 388
  43.6 14.3 %collective-permute-start.1 = (f32[16,32,128]{2,1,0:T(8,128)S(1)}, f32[16,32,128]{2,1,0:T(8,128)S(1)}, u32[]{:S(2)}, u32[]{:S(2)}) collective-permute-start(f32[16,32,128]{2,1,0:T(8,128)S(1)} %get-tuple-element.19), channel_id=1, source_target_pairs={{48,0},{32,16},{80,32},{64,48},{112,64},{96,80},{144,96},{128,112}... | collective-permute-start | bytes 786440 | tf_op jit(solution)/shard_map/ppermute | solution.py:366
  45.6 12.3 %collective-permute-start = (f32[16,32,128]{2,1,0:T(8,128)S(1)}, f32[16,32,128]{2,1,0:T(8,128)S(1)}, u32[]{:S(2)}, u32[]{:S(2)}) collective-permute-start(f32[16,32,128]{2,1,0:T(8,128)S(1)} %get-tuple-element.20), channel_id=1, source_target_pairs={{0,48},{16,32},{32,80},{48,64},{64,112},{80,96},{96,144},{112,128}... | collective-permute-start | bytes 786440 | tf_op jit(solution)/shard_map/ppermute | solution.py:365
  62.4 8.0 %collective-permute-start.2 = (f32[32,128]{1,0:T(8,128)S(1)}, f32[32,128]{1,0:T(8,128)S(1)}, u32[]{:S(2)}, u32[]{:S(2)}) collective-permute-start(f32[32,128]{1,0:T(8,128)S(1)} %get-tuple-element.8), channel_id=1, source_target_pairs={{0,48},{16,32},{32,80},{48,64},{64,112},{80,96},{96,144},{112,128}... | collective-permute-start | bytes 49160 | tf_op jit(solution)/shard_map/ppermute | solution.py:382
  65.4 5.0 %collective-permute-start.3 = (f32[32,128]{1,0:T(8,128)S(1)}, f32[32,128]{1,0:T(8,128)S(1)}, u32[]{:S(2)}, u32[]{:S(2)}) collective-permute-start(f32[32,128]{1,0:T(8,128)S(1)} %get-tuple-element.9), channel_id=1, source_target_pairs={{48,0},{32,16},{80,32},{64,48},{112,64},{96,80},{144,96},{128,112}... | collective-permute-start | bytes 49160 | tf_op jit(solution)/shard_map/ppermute | solution.py:383
  72.0 4.8 %copy-start.4 = (f32[4,7]{1,0:T(4,128)S(1)}, f32[4,7]{1,0:T(4,128)}, u32[]{:S(2)}) copy-start(f32[4,7]{1,0:T(4,128)} %param.12) | copy-start | bytes 340
  72.0 33.9 %all-to-all-start.1 = ((f32[32,64,128]{2,1,0:T(8,128)}), f32[32,64,128]{2,1,0:T(8,128)S(1)}, u32[]{:S(2)}, u32[]{:S(2)}) async-start(f32[32,64,128]{2,1,0:T(8,128)} %mend.1), calls=%async_computation.1 | async-start | bytes 2097152 | tf_op jit(solution)/shard_map/all_to_all | solution.py:406

commit v6 on v5

--- a/solution.py
+++ b/solution.py
@@ -31,23 +31,24 @@
     return lax.rem(lax.axis_index("group"), 2)
 
 
-def pack_kernel(tile_rows, tile_cols, last_row, fields_ref, table_ref, out_ref, wide_ref, sem):
-    count, cells = fields_ref.shape[0], fields_ref.shape[1]
+def pack_kernel(tile_rows, tile_cols, last_row, fields_ref, table_ref, out_ref, rest_ref, wide_ref, sem):
+    count = fields_ref.shape[0]
     half = count // PAIR
     swap = swapped()
+    group = lax.axis_index("group")
+    part = lax.axis_index("part")
+    border = pl.ds(pl.multiple_of(part * TILE, TILE), TILE)
+    inner = pl.ds(pl.multiple_of((1 - part) * TILE, TILE), TILE)
     copies = []
-    for part in range(PAIR):
-        source = lax.bitwise_xor(part, swap) * half
-        copies.append(
-            pltpu.make_async_copy(
-                fields_ref.at[pl.ds(source, half)], out_ref.at[part * half : (part + 1) * half, 0:cells, :], sem.at[part]
-            )
-        )
+    for place in range(PAIR):
+        source = pl.ds(lax.bitwise_xor(place, swap) * half, half)
+        blocks = slice(place * half, (place + 1) * half)
+        copies.append(pltpu.make_async_copy(fields_ref.at[source, border], out_ref.at[blocks, 0:TILE, :], sem.at[2 * place]))
+        copies.append(pltpu.make_async_copy(fields_ref.at[source, inner], rest_ref.at[blocks], sem.at[2 * place + 1]))
     for copy in copies:
         copy.start()
     entries, tiles = table_ref.shape
-    group = lax.axis_index("group")
-    band = group * PAIR + lax.axis_index("part")
+    band = group * PAIR + part
     wide_ref[...] = jnp.zeros(wide_ref.shape, jnp.int32)
     wide_ref[0:entries, 0:tiles] = table_ref[...]
     table = wide_ref[...]
@@ -70,7 +71,7 @@
         places = jnp.where(index == place, value, places)
     info = jnp.where(lane < tiles, info, pltpu.roll(places.astype(jnp.float32), tiles, 1))
     for block in range(count):
-        out_ref[block, cells:, :] = info
+        out_ref[block, TILE:, :] = info
     for copy in copies:
         copy.wait()
 
@@ -90,37 +91,42 @@
 
 
 def beside_matrix():
-    matrix = np.zeros((3 * LANES, LANES), np.float32)
+    matrix = np.zeros((2 * LANES, LANES), np.float32)
     for lane in range(LANES):
-        matrix[LANES + lane - 1, lane] = 1.0
-        matrix[LANES + lane + 1, lane] = 1.0
-    return jnp.asarray(matrix, jnp.bfloat16)
+        if lane > 0:
+            matrix[lane - 1, lane] = 1.0
+        if lane < LANES - 1:
+            matrix[lane + 1, lane] = 1.0
+    matrix[2 * LANES - 1, 0] = 1.0
+    matrix[LANES, LANES - 1] = 1.0
+    return jnp.asarray(np.concatenate([matrix, matrix]), jnp.bfloat16)
 
 
 PAD = 8
 
 
 def interpolate_kernel(
-    places_ref, blocks_ref, north_ref, south_ref, taps_ref, phi_ref, top_ref, bottom_ref, ext_ref, pass_ref, sem
+    places_ref, blocks_ref, rest_ref, north_ref, south_ref, taps_ref, phi_ref, top_ref, bottom_ref, ext_ref, pass_ref, sem
 ):
-    chunks, halo = north_ref.shape[0], north_ref.shape[1]
+    chunks = north_ref.shape[0]
     rows = phi_ref.shape[1] - 2 * PAD
     cells = rows // PAIR
     tile_rows = cells // TILE
     tile_cols = LANES // TILE
     tiles = tile_rows * tile_cols
+    north_half, south_half = slice(0, chunks), slice(chunks, 2 * chunks)
+    sources = [
+        north_ref,
+        blocks_ref.at[north_half, 0:TILE, :],
+        rest_ref.at[north_half],
+        rest_ref.at[south_half],
+        blocks_ref.at[south_half, 0:TILE, :],
+        south_ref,
+    ]
     copies = [
-        pltpu.make_async_copy(north_ref, ext_ref.at[:, 0:halo, :], sem.at[0]),
-        pltpu.make_async_copy(south_ref, ext_ref.at[:, halo + rows : 2 * halo + rows, :], sem.at[1]),
+        pltpu.make_async_copy(source, ext_ref.at[:, place * TILE : (place + 1) * TILE, :], sem.at[place])
+        for place, source in enumerate(sources)
     ]
-    for band in range(PAIR):
-        copies.append(
-            pltpu.make_async_copy(
-                blocks_ref.at[band * chunks : (band + 1) * chunks, 0:cells, :],
-                ext_ref.at[:, halo + band * cells : halo + (band + 1) * cells, :],
-                sem.at[2 + band],
-            )
-        )
     for copy in copies:
         copy.start()
     for chunk in range(chunks):
@@ -161,7 +167,7 @@
             moved = part if moved is None else moved + part
         for slot, (device, tile_row) in enumerate(work):
             own = lane_info // TILE + tile_row * tile_cols
-            weights = jnp.take_along_axis(blocks_ref[device, cells:, :], own, axis=1)
+            weights = jnp.take_along_axis(blocks_ref[device, TILE:, :], own, axis=1)
             total = weights[TAPS : TAPS + 1] * jnp.where(even_group, *pairs[slot])
             here = slice(slot * SPAN, (slot + 1) * SPAN)
             for tap in range(1, TAPS):
@@ -189,7 +195,7 @@
     return coef_ref[member // levels, lax.rem(member, levels)]
 
 
-TOGETHER = 4
+TOGETHER = 8
 
 
 def diffuse_kernel(groups, coef_ref, phi_ref, beside_ref, psi_ref, lap_ref, high_ref, low_ref):
@@ -208,14 +214,24 @@
 
         def step(index, carry):
             members = [index * together + place for place in range(together)]
-            sums = None
+            lane = lax.broadcasted_iota(jnp.int32, (rows, LANES), 1)
+            left = []
             for part_ref in (high_ref, low_ref):
-                left = [
-                    jnp.concatenate([part_ref[lax.rem(chunk + chunks + by, chunks)] for chunk in members], axis=0)
-                    for by in (-1, 0, 1)
-                ]
-                part = jnp.dot(jnp.concatenate(left, axis=1), beside_ref[...], preferred_element_type=jnp.float32)
-                sums = part if sums is None else sums + part
+                left.append(jnp.concatenate([part_ref[chunk] for chunk in members], axis=0))
+                left.append(
+                    jnp.concatenate(
+                        [
+                            jnp.where(
+                                lane == LANES - 1,
+                                part_ref[lax.rem(chunk + chunks - 1, chunks)],
+                                part_ref[lax.rem(chunk + 1, chunks)],
+                            )
+                            for chunk in members
+                        ],
+                        axis=0,
+                    )
+                )
+            sums = jnp.dot(jnp.concatenate(left, axis=1), beside_ref[...], preferred_element_type=jnp.float32)
             for place, chunk in enumerate(members):
                 around = ref[chunk, PAD + 1 : PAD + 1 + rows, :] + ref[chunk, PAD - 1 : PAD - 1 + rows, :]
                 store(chunk, around + sums[place * rows : (place + 1) * rows] - 4.0 * ref[chunk, PAD : PAD + rows, :])
@@ -347,38 +363,44 @@
         ],
         axis=0,
     )
-    blocks = pl.pallas_call(
+    blocks, rest = pl.pallas_call(
         functools.partial(pack_kernel, tile_rows, tile_cols, groups * PAIR * tile_rows - 2),
-        out_shape=jax.ShapeDtypeStruct((count, cells + INFO_ROWS, width), f32),
+        out_shape=(
+            jax.ShapeDtypeStruct((count, TILE + INFO_ROWS, width), f32),
+            jax.ShapeDtypeStruct((count, cells - TILE, width), f32),
+        ),
         in_specs=[anywhere(), vmem()],
-        out_specs=vmem(),
-        scratch_shapes=[pltpu.VMEM((8, LANES), jnp.int32), pltpu.SemaphoreType.DMA((PAIR,))],
+        out_specs=(vmem(), vmem()),
+        scratch_shapes=[pltpu.VMEM((8, LANES), jnp.int32), pltpu.SemaphoreType.DMA((2 * PAIR,))],
         compiler_params=limit,
         name="pack",
     )(fields.reshape(count, cells, width), table)
     blocks = lax.all_to_all(blocks, ("part", "lon"), 0, 0, tiled=True)
+    blocks, rest, vert_coef = lax.optimization_barrier((blocks, rest, vert_coef))
+    rest = lax.all_to_all(rest, ("part", "lon"), 0, 0, tiled=True)
     southward = [
         (group * PAIR + part, (group + 1) % groups * PAIR + PAIR - 1 - part) for group in range(groups) for part in range(PAIR)
     ]
     northward = [(target, source) for source, target in southward]
     bands = ("group", "part")
-    north = lax.ppermute(blocks[(PAIR - 1) * chunks :, cells - TILE : cells, :], bands, southward)
+    north = lax.ppermute(blocks[(PAIR - 1) * chunks :, :TILE, :], bands, southward)
     south = lax.ppermute(blocks[:chunks, :TILE, :], bands, northward)
-    places = blocks[:, cells : cells + 4, tiles : 2 * tiles].astype(jnp.int32).reshape(PAIR * chunks, 4 * tiles)
+    north, tables = lax.optimization_barrier((north, vertical_tables(vert_coef)))
+    places = blocks[:, TILE : TILE + 4, tiles : 2 * tiles].astype(jnp.int32).reshape(PAIR * chunks, 4 * tiles)
     edge = jax.ShapeDtypeStruct((2 * chunks, width), f32)
     phi, top, bottom = pl.pallas_call(
         interpolate_kernel,
         out_shape=(jax.ShapeDtypeStruct((chunks, rows + 2 * PAD, width), f32), edge, edge),
-        in_specs=[smem(), vmem(), vmem(), vmem(), vmem()],
+        in_specs=[smem(), vmem(), vmem(), vmem(), vmem(), vmem()],
         out_specs=(vmem(), vmem(), vmem()),
         scratch_shapes=[
             pltpu.VMEM((chunks, rows + 2 * TILE + 8, width), f32),
-            pltpu.VMEM((min(8, chunks) * tile_rows, SPAN, width), f32),
-            pltpu.SemaphoreType.DMA((2 + PAIR,)),
+            pltpu.VMEM((min(16, chunks) * tile_rows, SPAN, width), f32),
+            pltpu.SemaphoreType.DMA((2 + 2 * PAIR,)),
         ],
         compiler_params=limit,
         name="interpolate",
-    )(places, blocks, north, south, tap_matrix())
+    )(places, blocks, rest, north, south, tap_matrix())
     above = lax.ppermute(bottom, bands, southward)
     below = lax.ppermute(top, bands, northward)
     psi_shape = jax.ShapeDtypeStruct((count, cells, width), f32)
@@ -404,7 +426,6 @@
         name="mend",
     )(hyper_coef, above, below, inner)
     psi = lax.all_to_all(psi, ("part", "lon"), 0, 0, tiled=True)
-    lower, upper, inverse = vertical_tables(vert_coef)
     return pl.pallas_call(
         vertical_kernel,
         out_shape=jax.ShapeDtypeStruct((fcount, levels, cells, width), f32),
@@ -413,7 +434,7 @@
         scratch_shapes=[pltpu.VMEM((fcount, levels, cells, width), f32), pltpu.SemaphoreType.DMA((fcount,))],
         compiler_params=limit,
         name="solve",
-    )(lower, upper, inverse, psi)
+    )(*tables, psi)
 
 
 def solution(mesh):

time: 110 us -> 105 us (0.955)
  waiting for transfers between devices: 39.3 us -> 14.7 us
  blocking collectives: 41.3 us -> 62.8 us
  Pallas kernels: 11.7 us -> 10.1 us
    all_to_all x0 -> x1, blocking collectives: none -> 32.7 us  [body(): psi = lax.all_to_all(psi, ('part', 'lon'), 0, 0, tiled=True)]
    all_to_all x1, waiting for transfers between devices: 28.5 us -> 8.19 us  [body(): rest = lax.all_to_all(rest, ('part', 'lon'), 0, 0, tiled=True)]
    all_to_all x1, blocking collectives: 41.3 us -> 30.1 us  [body(): blocks = lax.all_to_all(blocks, ('part', 'lon'), 0, 0, tiled=True)]
    ppermute x1, waiting for transfers between devices: 10.8 us -> 6.48 us  [body(): south = lax.ppermute(blocks[:chunks, :TILE, :], bands, northward)]
    ppermute x1, starting transfers between devices: 3.01 us -> 0.97 us  [body(): above = lax.ppermute(bottom, bands, southward)]
    ppermute x1, starting transfers between devices: 1.2 us -> 3.24 us  [body(): below = lax.ppermute(top, bands, northward)]
where the time goes in v6:
time: 105 us; the launch traced here: 103 us
  blocking collectives  62.8 us (60%)
  waiting for transfers between devices  14.7 us (14%)
  starting transfers between devices  12.9 us (12%)
  Pallas kernels  10.1 us (10%)
  local copies, waits for them, and re-layouts  2.42 us (2%)
    all_to_all x1, blocking collectives, body(): psi = lax.all_to_all(psi, ('part', 'lon'), 0, 0, tiled=True)  32.7 us
    all_to_all x1, blocking collectives, body(): blocks = lax.all_to_all(blocks, ('part', 'lon'), 0, 0, tiled=True)  30.1 us
    all_to_all x1, waiting for transfers between devices, body(): rest = lax.all_to_all(rest, ('part', 'lon'), 0, 0, tiled=True)  8.19 us
    ppermute x1, waiting for transfers between devices, body(): south = lax.ppermute(blocks[:chunks, :TILE, :], bands, northward)  6.48 us
    all_to_all x1, starting transfers between devices, body(): rest = lax.all_to_all(rest, ('part', 'lon'), 0, 0, tiled=True)  4.32 us
    pallas_call x1, Pallas kernels, body(): pl.pallas_call(interpolate_kernel, out_shape=(jax.ShapeDtypeStruct((chunk...  4.06 us
    ppermute x1, starting transfers between devices, body(): below = lax.ppermute(top, bands, northward)  3.24 us
    pallas_call x1, Pallas kernels, body(): pl.pallas_call(functools.partial(diffuse_kernel, groups), out_shape=psi_s...  2.7 us
  transfers between devices with their start and end apart: 5, of which 2 were waited for; matrix products, arithmetic and copies ran while one was open for 1% of the time, Pallas kernels for 3%

profile of v6, /device:TPU:36, one launch (start us, length us, event | category | flops | bytes accessed | tf_op | source)
XLA Modules:
  0.0 103.4 jit_solution(8226968183816159606)
XLA Ops:
  0.0 0.8 concatenate.9.table_ref
  0.8 0.0 copy-start
  0.8 1.2 %copy-done = f32[4,8,64,128]{3,2,1,0:T(8,128)S(1)} copy-done((f32[4,8,64,128]{3,2,1,0:T(8,128)S(1)}, f32[4,8,64,128]{3,2,1,0:T(8,128)}, u32[]{:S(2)}) %copy-start) | copy-done | bytes 1048600
  2.0 1.0 pack.1
  3.0 30.1 %all_to_all.15.blocks_ref = f32[32,40,128]{2,1,0:T(8,128)S(1)} all-to-all(f32[32,40,128]{2,1,0:T(8,128)S(1)} %get-tuple-element.17), channel_id=1, replica_groups=mesh['group'=8,'part'=2,'lon'=16] {'part','lon'}, dimensions={0} | all-to-all | bytes 1310720 | tf_op jit(solution)/shard_map/all_to_all | solution.py:378
  33.1 0.0 copy-start.4
  33.1 0.0 copy-start.1
  33.1 0.1 fusion
  33.2 2.0 %collective-permute-start = (f32[16,32,128]{2,1,0:T(8,128)S(1)}, f32[16,32,128]{2,1,0:T(8,128)S(1)}, u32[]{:S(2)}, u32[]{:S(2)}) collective-permute-start(f32[16,32,128]{2,1,0:T(8,128)S(1)} %get-tuple-element.38), channel_id=1, source_target_pairs={{0,48},{16,32},{32,80},{48,64},{64,112},{80,96},{96,144},{112,128}... | collective-permute-start | bytes 786440 | tf_op jit(solution)/shard_map/ppermute | solution.py:386
  35.2 4.3 %all-to-all-start.1 = ((f32[32,32,128]{2,1,0:T(8,128)}), f32[32,32,128]{2,1,0:T(8,128)S(1)}, u32[]{:S(2)}, u32[]{:S(2)}) async-start(f32[32,32,128]{2,1,0:T(8,128)} %get-tuple-element.24), calls=%async_computation.1 | async-start | bytes 1048576 | tf_op jit(solution)/shard_map/all_to_all | solution.py:380
  39.5 0.0 copy-start.2
  39.5 0.0 copy-start.3
  39.5 2.3 %collective-permute-start.1 = (f32[16,32,128]{2,1,0:T(8,128)S(1)}, f32[16,32,128]{2,1,0:T(8,128)S(1)}, u32[]{:S(2)}, u32[]{:S(2)}) collective-permute-start(f32[16,32,128]{2,1,0:T(8,128)S(1)} %get-tuple-element.37), channel_id=1, source_target_pairs={{48,0},{32,16},{80,32},{64,48},{112,64},{96,80},{144,96},{128,112}... | collective-permute-start | bytes 786440 | tf_op jit(solution)/shard_map/ppermute | solution.py:387
  41.9 0.0 copy-done.4
  41.9 0.1 pad_add_fusion
  41.9 0.1 broadcast_divide_fusion
  42.0 0.1 slice_convert_fusion
  42.2 0.1 broadcast_divide_fusion.1
  42.3 0.1 copy.13
  42.3 0.1 copy.14.places_ref
  42.4 0.1 stack.4.upper_ref
  42.5 0.1 broadcast_divide_fusion.2
  42.6 0.1 stack.5.inverse_ref
  42.7 0.0 collective-permute-done.north_ref
  42.7 6.5 %collective-permute-done.1.south_ref = f32[16,32,128]{2,1,0:T(8,128)S(1)} collective-permute-done((f32[16,32,128]{2,1,0:T(8,128)S(1)}, f32[16,32,128]{2,1,0:T(8,128)S(1)}, u32[]{:S(2)}, u32[]{:S(2)}) %collective-permute-start.1) | collective-permute-done | bytes 262176 | tf_op jit(solution)/shard_map/ppermute | solution.py:387
  49.2 8.2 %all-to-all-done.1.rest_ref = f32[32,32,128]{2,1,0:T(8,128)S(1)} async-done(((f32[32,32,128]{2,1,0:T(8,128)}), f32[32,32,128]{2,1,0:T(8,128)S(1)}, u32[]{:S(2)}, u32[]{:S(2)}) %all-to-all-start.1) | async-done | bytes 524320 | tf_op jit(solution)/shard_map/all_to_all | solution.py:380
  57.4 0.0 copy-done.1
  57.4 4.1 %interpolate.1 = (f32[16,144,128]{2,1,0:T(8,128)S(1)}, f32[32,128]{1,0:T(8,128)S(1)}, f32[32,128]{1,0:T(8,128)S(1)}) custom-call(s32[32,32]{1,0:T(8,128)S(1)} %copy.14.places_ref, f32[32,40,128]{2,1,0:T(8,128)S(1)} %all_to_all.15.blocks_ref, f32[32,32,128]{2,1,0:T(8,128)S(1)} %all-to-all-done.1.rest_ref, f32[16,32,128]{2,1,0:T(8,128)S(1)} %collective-permute-done.north_ref, ...), custom_call_target="tpu_custom_call" | custom-call | tf_op jit(solution)/shard_map/interpolate/pallas_call | solution.py:391
  61.5 1.0 collective-permute-start.2
  62.4 3.2 %collective-permute-start.3 = (f32[32,128]{1,0:T(8,128)S(1)}, f32[32,128]{1,0:T(8,128)S(1)}, u32[]{:S(2)}, u32[]{:S(2)}) collective-permute-start(f32[32,128]{1,0:T(8,128)S(1)} %get-tuple-element.27), channel_id=1, source_target_pairs={{48,0},{32,16},{80,32},{64,48},{112,64},{96,80},{144,96},{128,112}... | collective-permute-start | bytes 49160 | tf_op jit(solution)/shard_map/ppermute | solution.py:405
  65.7 0.0 copy-done.2
  65.7 0.0 copy-done.3
  65.7 2.7 %diffuse.1.inner_ref = f32[32,64,128]{2,1,0:T(8,128)S(1)} custom-call(f32[4,8]{1,0:T(4,128)S(1)} %copy-done.3, f32[16,144,128]{2,1,0:T(8,128)S(1)} %get-tuple-element.28.phi_ref, bf16[512,128]{1,0:T(8,128)(2,1)S(1)} %copy-done.2), custom_call_target="tpu_custom_call" | custom-call | tf_op jit(solution)/shard_map/diffuse/pallas_call | solution.py:407
  68.4 0.0 collective-permute-done.2.north_ref
  68.4 0.0 collective-permute-done.3.south_ref
  68.4 0.7 mend.1
  69.1 32.7 %all_to_all.16.psi_ref = f32[32,64,128]{2,1,0:T(8,128)S(1)} all-to-all(f32[32,64,128]{2,1,0:T(8,128)S(1)} %mend.1), channel_id=1, replica_groups=mesh['group'=8,'part'=2,'lon'=16] {'part','lon'}, dimensions={0} | all-to-all | bytes 2097152 | tf_op jit(solution)/shard_map/all_to_all | solution.py:428
  101.7 1.7 %solve.1 = f32[4,8,64,128]{3,2,1,0:T(8,128)} custom-call(f32[4,8]{1,0:T(4,128)S(1)} %get-tuple-element.21.lower_ref, f32[4,8]{1,0:T(4,128)S(1)} %stack.4.upper_ref, f32[4,8]{1,0:T(4,128)S(1)} %stack.5.inverse_ref, f32[32,64,128]{2,1,0:T(8,128)S(1)} %all_to_all.16.psi_ref), custom_call_target="tpu_custom_call" | custom-call | tf_op jit(solution)/shard_map/solve/pallas_call | solution.py:429
Async XLA Ops:
  0.8 1.2 %copy-start = (f32[4,8,64,128]{3,2,1,0:T(8,128)S(1)}, f32[4,8,64,128]{3,2,1,0:T(8,128)}, u32[]{:S(2)}) copy-start(f32[4,8,64,128]{3,2,1,0:T(8,128)} %param.10) | copy-start | bytes 3145732
  33.1 8.8 %copy-start.4 = (f32[4,7]{1,0:T(4,128)S(1)}, f32[4,7]{1,0:T(4,128)}, u32[]{:S(2)}) copy-start(f32[4,7]{1,0:T(4,128)} %param.12) | copy-start | bytes 340
  33.1 24.3 %copy-start.1 = (bf16[256,384]{1,0:T(8,128)(2,1)S(1)}, bf16[256,384]{1,0:T(8,128)(2,1)}, u32[]{:S(2)}) copy-start(bf16[256,384]{1,0:T(8,128)(2,1)} %constant.4.clone.taps_ref) | copy-start | bytes 589828
  33.2 9.5 %collective-permute-start = (f32[16,32,128]{2,1,0:T(8,128)S(1)}, f32[16,32,128]{2,1,0:T(8,128)S(1)}, u32[]{:S(2)}, u32[]{:S(2)}) collective-permute-start(f32[16,32,128]{2,1,0:T(8,128)S(1)} %get-tuple-element.38), channel_id=1, source_target_pairs={{0,48},{16,32},{32,80},{48,64},{64,112},{80,96},{96,144},{112,128}... | collective-permute-start | bytes 786440 | tf_op jit(solution)/shard_map/ppermute | solution.py:386
  35.2 22.2 %all-to-all-start.1 = ((f32[32,32,128]{2,1,0:T(8,128)}), f32[32,32,128]{2,1,0:T(8,128)S(1)}, u32[]{:S(2)}, u32[]{:S(2)}) async-start(f32[32,32,128]{2,1,0:T(8,128)} %get-tuple-element.24), calls=%async_computation.1 | async-start | bytes 1048576 | tf_op jit(solution)/shard_map/all_to_all | solution.py:380
  39.5 26.2 %copy-start.2 = (bf16[512,128]{1,0:T(8,128)(2,1)S(1)}, bf16[512,128]{1,0:T(8,128)(2,1)}, u32[]{:S(2)}) copy-start(bf16[512,128]{1,0:T(8,128)(2,1)} %constant.12.clone.beside_ref) | copy-start | bytes 393220
  39.5 26.1 %copy-start.3 = (f32[4,8]{1,0:T(4,128)S(1)}, f32[4,8]{1,0:T(4,128)}, u32[]{:S(2)}) copy-start(f32[4,8]{1,0:T(4,128)} %coef_ref.3) | copy-start | bytes 388
  39.5 9.6 %collective-permute-start.1 = (f32[16,32,128]{2,1,0:T(8,128)S(1)}, f32[16,32,128]{2,1,0:T(8,128)S(1)}, u32[]{:S(2)}, u32[]{:S(2)}) collective-permute-start(f32[16,32,128]{2,1,0:T(8,128)S(1)} %get-tuple-element.37), channel_id=1, source_target_pairs={{48,0},{32,16},{80,32},{64,48},{112,64},{96,80},{144,96},{128,112}... | collective-permute-start | bytes 786440 | tf_op jit(solution)/shard_map/ppermute | solution.py:387
  61.5 6.9 %collective-permute-start.2 = (f32[32,128]{1,0:T(8,128)S(1)}, f32[32,128]{1,0:T(8,128)S(1)}, u32[]{:S(2)}, u32[]{:S(2)}) collective-permute-start(f32[32,128]{1,0:T(8,128)S(1)} %get-tuple-element.26), channel_id=1, source_target_pairs={{0,48},{16,32},{32,80},{48,64},{64,112},{80,96},{96,144},{112,128}... | collective-permute-start | bytes 49160 | tf_op jit(solution)/shard_map/ppermute | solution.py:404
  62.4 6.0 %collective-permute-start.3 = (f32[32,128]{1,0:T(8,128)S(1)}, f32[32,128]{1,0:T(8,128)S(1)}, u32[]{:S(2)}, u32[]{:S(2)}) collective-permute-start(f32[32,128]{1,0:T(8,128)S(1)} %get-tuple-element.27), channel_id=1, source_target_pairs={{48,0},{32,16},{80,32},{64,48},{112,64},{96,80},{144,96},{128,112}... | collective-permute-start | bytes 49160 | tf_op jit(solution)/shard_map/ppermute | solution.py:405

commit v7 on v6

--- a/solution.py
+++ b/solution.py
@@ -43,8 +43,8 @@
     for place in range(PAIR):
         source = pl.ds(lax.bitwise_xor(place, swap) * half, half)
         blocks = slice(place * half, (place + 1) * half)
-        copies.append(pltpu.make_async_copy(fields_ref.at[source, border], out_ref.at[blocks, 0:TILE, :], sem.at[2 * place]))
-        copies.append(pltpu.make_async_copy(fields_ref.at[source, inner], rest_ref.at[blocks], sem.at[2 * place + 1]))
+        copies.append(pltpu.make_async_copy(fields_ref.at[source, border], out_ref.at[blocks], sem.at[2 * place]))
+        copies.append(pltpu.make_async_copy(fields_ref.at[source, inner], rest_ref.at[blocks, 0:TILE, :], sem.at[2 * place + 1]))
     for copy in copies:
         copy.start()
     entries, tiles = table_ref.shape
@@ -66,12 +66,12 @@
     info = jnp.zeros(shape, jnp.float32)
     for place, value in enumerate(cubic_weights(frac_row) + cubic_weights(frac_col)):
         info = jnp.where(index == place, value, info)
-    places = jnp.zeros(shape, jnp.int32)
     for place, value in enumerate((start, owner, wrapped, turn)):
-        places = jnp.where(index == place, value, places)
-    info = jnp.where(lane < tiles, info, pltpu.roll(places.astype(jnp.float32), tiles, 1))
+        first = tiles * (place + 1)
+        value = pltpu.roll(value.astype(jnp.float32), first, 1)
+        info = jnp.where((index == 0) & (lane >= first) & (lane < first + tiles), value, info)
     for block in range(count):
-        out_ref[block, TILE:, :] = info
+        rest_ref[block, TILE:, :] = info
     for copy in copies:
         copy.wait()
 
@@ -117,10 +117,10 @@
     north_half, south_half = slice(0, chunks), slice(chunks, 2 * chunks)
     sources = [
         north_ref,
-        blocks_ref.at[north_half, 0:TILE, :],
-        rest_ref.at[north_half],
-        rest_ref.at[south_half],
-        blocks_ref.at[south_half, 0:TILE, :],
+        blocks_ref.at[north_half],
+        rest_ref.at[north_half, 0:TILE, :],
+        rest_ref.at[south_half, 0:TILE, :],
+        blocks_ref.at[south_half],
         south_ref,
     ]
     copies = [
@@ -144,7 +144,7 @@
     def windows(device, tile_row):
         def window(tile_col):
             tile = tile_row * tile_cols + tile_col
-            start, source, wrapped, turn = (places_ref[device, place * tiles + tile] for place in range(4))
+            start, source, wrapped, turn = (places_ref[device, tiles * place + tile] for place in range(4))
             after = lax.rem(source + 1, chunks)
             span = pl.ds(start, SPAN)
             return pltpu.roll(jnp.where(lane < wrapped, ext_ref[after, span, :], ext_ref[source, span, :]), turn, 1)
@@ -167,7 +167,7 @@
             moved = part if moved is None else moved + part
         for slot, (device, tile_row) in enumerate(work):
             own = lane_info // TILE + tile_row * tile_cols
-            weights = jnp.take_along_axis(blocks_ref[device, TILE:, :], own, axis=1)
+            weights = jnp.take_along_axis(rest_ref[device, TILE:, :], own, axis=1)
             total = weights[TAPS : TAPS + 1] * jnp.where(even_group, *pairs[slot])
             here = slice(slot * SPAN, (slot + 1) * SPAN)
             for tap in range(1, TAPS):
@@ -195,7 +195,7 @@
     return coef_ref[member // levels, lax.rem(member, levels)]
 
 
-TOGETHER = 8
+TOGETHER = 16
 
 
 def diffuse_kernel(groups, coef_ref, phi_ref, beside_ref, psi_ref, lap_ref, high_ref, low_ref):
@@ -366,8 +366,8 @@
     blocks, rest = pl.pallas_call(
         functools.partial(pack_kernel, tile_rows, tile_cols, groups * PAIR * tile_rows - 2),
         out_shape=(
-            jax.ShapeDtypeStruct((count, TILE + INFO_ROWS, width), f32),
-            jax.ShapeDtypeStruct((count, cells - TILE, width), f32),
+            jax.ShapeDtypeStruct((count, TILE, width), f32),
+            jax.ShapeDtypeStruct((count, cells - TILE + INFO_ROWS, width), f32),
         ),
         in_specs=[anywhere(), vmem()],
         out_specs=(vmem(), vmem()),
@@ -378,20 +378,21 @@
     blocks = lax.all_to_all(blocks, ("part", "lon"), 0, 0, tiled=True)
     blocks, rest, vert_coef = lax.optimization_barrier((blocks, rest, vert_coef))
     rest = lax.all_to_all(rest, ("part", "lon"), 0, 0, tiled=True)
+    tables = vertical_tables(vert_coef)
+    ready, tables = lax.optimization_barrier((blocks, tables))
     southward = [
         (group * PAIR + part, (group + 1) % groups * PAIR + PAIR - 1 - part) for group in range(groups) for part in range(PAIR)
     ]
     northward = [(target, source) for source, target in southward]
     bands = ("group", "part")
-    north = lax.ppermute(blocks[(PAIR - 1) * chunks :, :TILE, :], bands, southward)
-    south = lax.ppermute(blocks[:chunks, :TILE, :], bands, northward)
-    north, tables = lax.optimization_barrier((north, vertical_tables(vert_coef)))
-    places = blocks[:, TILE : TILE + 4, tiles : 2 * tiles].astype(jnp.int32).reshape(PAIR * chunks, 4 * tiles)
+    north = lax.ppermute(ready[(PAIR - 1) * chunks :, :TILE, :], bands, southward)
+    south = lax.ppermute(ready[:chunks, :TILE, :], bands, northward)
+    places = rest[:, cells - TILE, tiles : 5 * tiles].astype(jnp.int32)
     edge = jax.ShapeDtypeStruct((2 * chunks, width), f32)
     phi, top, bottom = pl.pallas_call(
         interpolate_kernel,
         out_shape=(jax.ShapeDtypeStruct((chunks, rows + 2 * PAD, width), f32), edge, edge),
-        in_specs=[smem(), vmem(), vmem(), vmem(), vmem(), vmem()],
+        in_specs=[smem()] + [vmem()] * 5,
         out_specs=(vmem(), vmem(), vmem()),
         scratch_shapes=[
             pltpu.VMEM((chunks, rows + 2 * TILE + 8, width), f32),

time: 105 us -> 103 us (0.981)
  blocking collectives: 62.8 us -> 59.8 us
  waiting for transfers between devices: 14.7 us -> 17.3 us
    all_to_all x1, waiting for transfers between devices: 8.19 us -> 16.7 us  [body(): rest = lax.all_to_all(rest, ('part', 'lon'), 0, 0, tiled=True)]
    ppermute x2, waiting for transfers between devices: 6.48 us -> 0.01 us  [the longest x1 0.01 us: body(): south = lax.ppermute(ready[:chunks, :TILE, :], bands, northward)]
    all_to_all x1, blocking collectives: 30.1 us -> 27.3 us  [body(): blocks = lax.all_to_all(blocks, ('part', 'lon'), 0, 0, tiled=True)]
  transfers between devices with their start and end apart: 5 -> 5, of which waited for: 2 -> 2; matrix products, arithmetic and copies ran while one was open for 1% -> 1% of each run, Pallas kernels for 3% -> 2%
where the time goes in v7:
time: 103 us; the launch traced here: 102 us
  blocking collectives  59.8 us (58%)
  waiting for transfers between devices  17.3 us (17%)
  starting transfers between devices  12.1 us (12%)
  Pallas kernels  9.6 us (9%)
  local copies, waits for them, and re-layouts  2.25 us (2%)
    all_to_all x1, blocking collectives, body(): psi = lax.all_to_all(psi, ('part', 'lon'), 0, 0, tiled=True)  32.5 us
    all_to_all x1, blocking collectives, body(): blocks = lax.all_to_all(blocks, ('part', 'lon'), 0, 0, tiled=True)  27.3 us
    all_to_all x1, waiting for transfers between devices, body(): rest = lax.all_to_all(rest, ('part', 'lon'), 0, 0, tiled=True)  16.7 us
    all_to_all x1, starting transfers between devices, body(): rest = lax.all_to_all(rest, ('part', 'lon'), 0, 0, tiled=True)  4.61 us
    pallas_call x1, Pallas kernels, body(): pl.pallas_call(interpolate_kernel, out_shape=(jax.ShapeDtypeStruct((chunk...  4.07 us
    ppermute x1, starting transfers between devices, body(): south = lax.ppermute(ready[:chunks, :TILE, :], bands, northward)  3.06 us
    ppermute x1, starting transfers between devices, body(): below = lax.ppermute(top, bands, northward)  2.24 us
    pallas_call x1, Pallas kernels, body(): pl.pallas_call(functools.partial(diffuse_kernel, groups), out_shape=psi_s...  2.12 us
  transfers between devices with their start and end apart: 5, of which 2 were waited for; matrix products, arithmetic and copies ran while one was open for 1% of the time, Pallas kernels for 2%

profile of v7, /device:TPU:36, one launch (start us, length us, event | category | flops | bytes accessed | tf_op | source)
XLA Modules:
  0.0 101.7 jit_solution(16413184504324396850)
XLA Ops:
  0.0 0.8 concatenate.9.table_ref
  0.8 0.0 copy-start
  0.8 1.2 %copy-done = f32[4,8,64,128]{3,2,1,0:T(8,128)S(1)} copy-done((f32[4,8,64,128]{3,2,1,0:T(8,128)S(1)}, f32[4,8,64,128]{3,2,1,0:T(8,128)}, u32[]{:S(2)}) %copy-start) | copy-done | bytes 1048600
  2.0 1.0 %pack.1 = (f32[32,32,128]{2,1,0:T(8,128)S(1)}, f32[32,40,128]{2,1,0:T(8,128)}) custom-call(f32[32,64,128]{2,1,0:T(8,128)S(1)} %bitcast.11, s32[7,8]{1,0:T(8,128)S(1)} %concatenate.9.table_ref), custom_call_target="tpu_custom_call" | custom-call | tf_op jit(solution)/shard_map/pack/pallas_call | solution.py:366
  3.0 0.0 copy-start.4
  3.1 27.3 %all_to_all.15.blocks_ref = f32[32,32,128]{2,1,0:T(8,128)S(1)} all-to-all(f32[32,32,128]{2,1,0:T(8,128)S(1)} %get-tuple-element.17), channel_id=1, replica_groups=mesh['group'=8,'part'=2,'lon'=16] {'part','lon'}, dimensions={0} | all-to-all | bytes 1048576 | tf_op jit(solution)/shard_map/all_to_all | solution.py:378
  30.4 0.0 copy-start.1
  30.4 4.6 %all-to-all-start.1 = ((f32[32,40,128]{2,1,0:T(8,128)}), f32[32,40,128]{2,1,0:T(8,128)S(1)}, u32[]{:S(2)}, u32[]{:S(2)}) async-start(f32[32,40,128]{2,1,0:T(8,128)} %get-tuple-element.24), calls=%async_computation.1 | async-start | bytes 1310720 | tf_op jit(solution)/shard_map/all_to_all | solution.py:380
  35.0 0.0 copy-done.4
  35.0 0.1 pad_add_fusion
  35.1 0.1 broadcast_divide_fusion
  35.2 0.1 broadcast_divide_fusion.1
  35.3 0.1 stack.4.upper_ref
  35.4 0.1 broadcast_divide_fusion.2
  35.5 0.1 stack.5.inverse_ref
  35.6 0.0 copy-start.2
  35.6 0.0 copy-start.3
  35.6 3.1 %collective-permute-start.1 = (f32[16,32,128]{2,1,0:T(8,128)S(1)}, f32[16,32,128]{2,1,0:T(8,128)S(1)}, u32[]{:S(2)}, u32[]{:S(2)}) collective-permute-start(f32[16,32,128]{2,1,0:T(8,128)S(1)} %get-tuple-element.37), channel_id=1, source_target_pairs={{48,0},{32,16},{80,32},{64,48},{112,64},{96,80},{144,96},{128,112}... | collective-permute-start | bytes 786440 | tf_op jit(solution)/shard_map/ppermute | solution.py:389
  38.7 0.3 collective-permute-start
  38.9 16.7 %all-to-all-done.1.rest_ref = f32[32,40,128]{2,1,0:T(8,128)S(1)} async-done(((f32[32,40,128]{2,1,0:T(8,128)}), f32[32,40,128]{2,1,0:T(8,128)S(1)}, u32[]{:S(2)}, u32[]{:S(2)}) %all-to-all-start.1) | async-done | bytes 655392 | tf_op jit(solution)/shard_map/all_to_all | solution.py:380
  55.6 0.1 slice_convert_fusion
  55.7 0.0 collective-permute-done.1.south_ref
  55.8 0.0 collective-permute-done.north_ref
  55.8 0.0 copy-done.1
  55.8 4.1 %interpolate.1 = (f32[16,144,128]{2,1,0:T(8,128)S(1)}, f32[32,128]{1,0:T(8,128)S(1)}, f32[32,128]{1,0:T(8,128)S(1)}) custom-call(s32[32,32]{1,0:T(8,128)S(1)} %bitcast.12, f32[32,32,128]{2,1,0:T(8,128)S(1)} %all_to_all.15.blocks_ref, f32[32,40,128]{2,1,0:T(8,128)S(1)} %all-to-all-done.1.rest_ref, f32[16,32,128]{2,1,0:T(8,128)S(1)} %collective-permute-done.north_ref, ...), custom_call_target="tpu_custom_call" | custom-call | tf_op jit(solution)/shard_map/interpolate/pallas_call | solution.py:392
  59.9 2.0 %collective-permute-start.2 = (f32[32,128]{1,0:T(8,128)S(1)}, f32[32,128]{1,0:T(8,128)S(1)}, u32[]{:S(2)}, u32[]{:S(2)}) collective-permute-start(f32[32,128]{1,0:T(8,128)S(1)} %get-tuple-element.26), channel_id=1, source_target_pairs={{0,48},{16,32},{32,80},{48,64},{64,112},{80,96},{96,144},{112,128}... | collective-permute-start | bytes 49160 | tf_op jit(solution)/shard_map/ppermute | solution.py:405
  61.8 2.2 %collective-permute-start.3 = (f32[32,128]{1,0:T(8,128)S(1)}, f32[32,128]{1,0:T(8,128)S(1)}, u32[]{:S(2)}, u32[]{:S(2)}) collective-permute-start(f32[32,128]{1,0:T(8,128)S(1)} %get-tuple-element.27), channel_id=1, source_target_pairs={{48,0},{32,16},{80,32},{64,48},{112,64},{96,80},{144,96},{128,112}... | collective-permute-start | bytes 49160 | tf_op jit(solution)/shard_map/ppermute | solution.py:406
  64.1 0.0 copy-done.2
  64.1 0.0 copy-done.3
  64.1 2.1 %diffuse.1.inner_ref = f32[32,64,128]{2,1,0:T(8,128)S(1)} custom-call(f32[4,8]{1,0:T(4,128)S(1)} %copy-done.3, f32[16,144,128]{2,1,0:T(8,128)S(1)} %get-tuple-element.28.phi_ref, bf16[512,128]{1,0:T(8,128)(2,1)S(1)} %copy-done.2), custom_call_target="tpu_custom_call" | custom-call | tf_op jit(solution)/shard_map/diffuse/pallas_call | solution.py:408
  66.2 0.0 collective-permute-done.2.north_ref
  66.2 0.6 collective-permute-done.3.south_ref
  66.8 0.7 mend.1
  67.5 32.5 %all_to_all.16.psi_ref = f32[32,64,128]{2,1,0:T(8,128)S(1)} all-to-all(f32[32,64,128]{2,1,0:T(8,128)S(1)} %mend.1), channel_id=1, replica_groups=mesh['group'=8,'part'=2,'lon'=16] {'part','lon'}, dimensions={0} | all-to-all | bytes 2097152 | tf_op jit(solution)/shard_map/all_to_all | solution.py:429
  100.0 1.7 %solve.1 = f32[4,8,64,128]{3,2,1,0:T(8,128)} custom-call(f32[4,8]{1,0:T(4,128)S(1)} %get-tuple-element.21.lower_ref, f32[4,8]{1,0:T(4,128)S(1)} %stack.4.upper_ref, f32[4,8]{1,0:T(4,128)S(1)} %stack.5.inverse_ref, f32[32,64,128]{2,1,0:T(8,128)S(1)} %all_to_all.16.psi_ref), custom_call_target="tpu_custom_call" | custom-call | tf_op jit(solution)/shard_map/solve/pallas_call | solution.py:430
  (1 shorter events, 0.0 us)
Async XLA Ops:
  0.8 1.2 %copy-start = (f32[4,8,64,128]{3,2,1,0:T(8,128)S(1)}, f32[4,8,64,128]{3,2,1,0:T(8,128)}, u32[]{:S(2)}) copy-start(f32[4,8,64,128]{3,2,1,0:T(8,128)} %param.10) | copy-start | bytes 3145732
  3.0 31.9 %copy-start.4 = (f32[4,7]{1,0:T(4,128)S(1)}, f32[4,7]{1,0:T(4,128)}, u32[]{:S(2)}) copy-start(f32[4,7]{1,0:T(4,128)} %param.12) | copy-start | bytes 340
  30.4 25.4 %copy-start.1 = (bf16[256,384]{1,0:T(8,128)(2,1)S(1)}, bf16[256,384]{1,0:T(8,128)(2,1)}, u32[]{:S(2)}) copy-start(bf16[256,384]{1,0:T(8,128)(2,1)} %constant.4.clone.taps_ref) | copy-start | bytes 589828
  30.4 25.3 %all-to-all-start.1 = ((f32[32,40,128]{2,1,0:T(8,128)}), f32[32,40,128]{2,1,0:T(8,128)S(1)}, u32[]{:S(2)}, u32[]{:S(2)}) async-start(f32[32,40,128]{2,1,0:T(8,128)} %get-tuple-element.24), calls=%async_computation.1 | async-start | bytes 1310720 | tf_op jit(solution)/shard_map/all_to_all | solution.py:380
  35.6 28.5 %copy-start.2 = (bf16[512,128]{1,0:T(8,128)(2,1)S(1)}, bf16[512,128]{1,0:T(8,128)(2,1)}, u32[]{:S(2)}) copy-start(bf16[512,128]{1,0:T(8,128)(2,1)} %constant.12.clone.beside_ref) | copy-start | bytes 393220
  35.6 28.5 %copy-start.3 = (f32[4,8]{1,0:T(4,128)S(1)}, f32[4,8]{1,0:T(4,128)}, u32[]{:S(2)}) copy-start(f32[4,8]{1,0:T(4,128)} %coef_ref.3) | copy-start | bytes 388
  35.6 20.1 %collective-permute-start.1 = (f32[16,32,128]{2,1,0:T(8,128)S(1)}, f32[16,32,128]{2,1,0:T(8,128)S(1)}, u32[]{:S(2)}, u32[]{:S(2)}) collective-permute-start(f32[16,32,128]{2,1,0:T(8,128)S(1)} %get-tuple-element.37), channel_id=1, source_target_pairs={{48,0},{32,16},{80,32},{64,48},{112,64},{96,80},{144,96},{128,112}... | collective-permute-start | bytes 786440 | tf_op jit(solution)/shard_map/ppermute | solution.py:389
  38.7 17.1 %collective-permute-start = (f32[16,32,128]{2,1,0:T(8,128)S(1)}, f32[16,32,128]{2,1,0:T(8,128)S(1)}, u32[]{:S(2)}, u32[]{:S(2)}) collective-permute-start(f32[16,32,128]{2,1,0:T(8,128)S(1)} %get-tuple-element.38), channel_id=1, source_target_pairs={{0,48},{16,32},{32,80},{48,64},{64,112},{80,96},{96,144},{112,128}... | collective-permute-start | bytes 786440 | tf_op jit(solution)/shard_map/ppermute | solution.py:388
  59.9 6.3 %collective-permute-start.2 = (f32[32,128]{1,0:T(8,128)S(1)}, f32[32,128]{1,0:T(8,128)S(1)}, u32[]{:S(2)}, u32[]{:S(2)}) collective-permute-start(f32[32,128]{1,0:T(8,128)S(1)} %get-tuple-element.26), channel_id=1, source_target_pairs={{0,48},{16,32},{32,80},{48,64},{64,112},{80,96},{96,144},{112,128}... | collective-permute-start | bytes 49160 | tf_op jit(solution)/shard_map/ppermute | solution.py:405
  61.8 4.9 %collective-permute-start.3 = (f32[32,128]{1,0:T(8,128)S(1)}, f32[32,128]{1,0:T(8,128)S(1)}, u32[]{:S(2)}, u32[]{:S(2)}) collective-permute-start(f32[32,128]{1,0:T(8,128)S(1)} %get-tuple-element.27), channel_id=1, source_target_pairs={{48,0},{32,16},{80,32},{64,48},{112,64},{96,80},{144,96},{128,112}... | collective-permute-start | bytes 49160 | tf_op jit(solution)/shard_map/ppermute | solution.py:406

commit v8 on v7

--- a/solution.py
+++ b/solution.py
@@ -31,20 +31,32 @@
     return lax.rem(lax.axis_index("group"), 2)
 
 
-def pack_kernel(tile_rows, tile_cols, last_row, fields_ref, table_ref, out_ref, rest_ref, wide_ref, sem):
+def block_copies(fields_ref, place, out_ref, sem):
+    half = fields_ref.shape[0] // PAIR
+    rows = pl.ds(pl.multiple_of(place * TILE, TILE), TILE)
+    return [
+        pltpu.make_async_copy(
+            fields_ref.at[pl.ds(lax.bitwise_xor(part, swapped()) * half, half), rows],
+            out_ref.at[part * half : (part + 1) * half, 0:TILE, :],
+            sem.at[part],
+        )
+        for part in range(PAIR)
+    ]
+
+
+def pack_border_kernel(fields_ref, out_ref, sem):
+    copies = block_copies(fields_ref, lax.axis_index("part"), out_ref, sem)
+    for copy in copies:
+        copy.start()
+    for copy in copies:
+        copy.wait()
+
+
+def pack_inner_kernel(tile_rows, tile_cols, last_row, fields_ref, table_ref, rest_ref, wide_ref, sem):
     count = fields_ref.shape[0]
-    half = count // PAIR
-    swap = swapped()
     group = lax.axis_index("group")
     part = lax.axis_index("part")
-    border = pl.ds(pl.multiple_of(part * TILE, TILE), TILE)
-    inner = pl.ds(pl.multiple_of((1 - part) * TILE, TILE), TILE)
-    copies = []
-    for place in range(PAIR):
-        source = pl.ds(lax.bitwise_xor(place, swap) * half, half)
-        blocks = slice(place * half, (place + 1) * half)
-        copies.append(pltpu.make_async_copy(fields_ref.at[source, border], out_ref.at[blocks], sem.at[2 * place]))
-        copies.append(pltpu.make_async_copy(fields_ref.at[source, inner], rest_ref.at[blocks, 0:TILE, :], sem.at[2 * place + 1]))
+    copies = block_copies(fields_ref, 1 - part, rest_ref, sem)
     for copy in copies:
         copy.start()
     entries, tiles = table_ref.shape
@@ -363,18 +375,25 @@
         ],
         axis=0,
     )
-    blocks, rest = pl.pallas_call(
-        functools.partial(pack_kernel, tile_rows, tile_cols, groups * PAIR * tile_rows - 2),
-        out_shape=(
-            jax.ShapeDtypeStruct((count, TILE, width), f32),
-            jax.ShapeDtypeStruct((count, cells - TILE + INFO_ROWS, width), f32),
-        ),
+    flat = fields.reshape(count, cells, width)
+    blocks = pl.pallas_call(
+        pack_border_kernel,
+        out_shape=jax.ShapeDtypeStruct((count, TILE, width), f32),
+        in_specs=[anywhere()],
+        out_specs=vmem(),
+        scratch_shapes=[pltpu.SemaphoreType.DMA((PAIR,))],
+        compiler_params=limit,
+        name="pack_border",
+    )(flat)
+    rest = pl.pallas_call(
+        functools.partial(pack_inner_kernel, tile_rows, tile_cols, groups * PAIR * tile_rows - 2),
+        out_shape=jax.ShapeDtypeStruct((count, cells - TILE + INFO_ROWS, width), f32),
         in_specs=[anywhere(), vmem()],
-        out_specs=(vmem(), vmem()),
-        scratch_shapes=[pltpu.VMEM((8, LANES), jnp.int32), pltpu.SemaphoreType.DMA((2 * PAIR,))],
-        compiler_params=limit,
-        name="pack",
-    )(fields.reshape(count, cells, width), table)
+        out_specs=vmem(),
+        scratch_shapes=[pltpu.VMEM((8, LANES), jnp.int32), pltpu.SemaphoreType.DMA((PAIR,))],
+        compiler_params=limit,
+        name="pack_inner",
+    )(flat, table)
     blocks = lax.all_to_all(blocks, ("part", "lon"), 0, 0, tiled=True)
     blocks, rest, vert_coef = lax.optimization_barrier((blocks, rest, vert_coef))
     rest = lax.all_to_all(rest, ("part", "lon"), 0, 0, tiled=True)

time: 103 us -> 102 us (level)
  blocking collectives: 59.8 us -> 32.5 us
  waiting for transfers between devices: 17.3 us -> 33.9 us
  starting transfers between devices: 12.1 us -> 21.8 us
    all_to_all x1 -> x0, blocking collectives: 27.3 us -> none  [body(): blocks = lax.all_to_all(blocks, ('part', 'lon'), 0, 0, tiled=True)]
    all_to_all x0 -> x1, waiting for transfers between devices: none -> 16.6 us  [body(): blocks = lax.all_to_all(blocks, ('part', 'lon'), 0, 0, tiled=True)]
    all_to_all x0 -> x1, starting transfers between devices: none -> 9.75 us  [body(): blocks = lax.all_to_all(blocks, ('part', 'lon'), 0, 0, tiled=True)]
  transfers between devices with their start and end apart: 5 -> 6, of which waited for: 2 -> 3; matrix products, arithmetic and copies ran while one was open for 1% -> 1% of each run, Pallas kernels for 2% -> 3%
where the time goes in v8:
time: 102 us; the launch traced here: 101 us
  waiting for transfers between devices  33.9 us (33%)
  blocking collectives  32.5 us (32%)
  starting transfers between devices  21.8 us (21%)
  Pallas kernels  10.4 us (10%)
  local copies, waits for them, and re-layouts  1.54 us (2%)
    all_to_all x1, blocking collectives, body(): psi = lax.all_to_all(psi, ('part', 'lon'), 0, 0, tiled=True)  32.5 us
    all_to_all x1, waiting for transfers between devices, body(): rest = lax.all_to_all(rest, ('part', 'lon'), 0, 0, tiled=True)  16.7 us
    all_to_all x1, waiting for transfers between devices, body(): blocks = lax.all_to_all(blocks, ('part', 'lon'), 0, 0, tiled=True)  16.6 us
    all_to_all x1, starting transfers between devices, body(): blocks = lax.all_to_all(blocks, ('part', 'lon'), 0, 0, tiled=True)  9.75 us
    all_to_all x1, starting transfers between devices, body(): rest = lax.all_to_all(rest, ('part', 'lon'), 0, 0, tiled=True)  4.48 us
    pallas_call x1, Pallas kernels, body(): pl.pallas_call(interpolate_kernel, out_shape=(jax.ShapeDtypeStruct((chunk...  4.08 us
    ppermute x1, starting transfers between devices, body(): south = lax.ppermute(ready[:chunks, :TILE, :], bands, northward)  3.06 us
    ppermute x1, starting transfers between devices, body(): below = lax.ppermute(top, bands, northward)  2.26 us
  transfers between devices with their start and end apart: 6, of which 3 were waited for; matrix products, arithmetic and copies ran while one was open for 1% of the time, Pallas kernels for 3%

profile of v8, /device:TPU:36, one launch (start us, length us, event | category | flops | bytes accessed | tf_op | source)
XLA Modules:
  0.0 100.8 jit_solution(13782214697521563981)
XLA Ops:
  0.0 0.0 copy-start
  0.0 1.2 %copy-done = f32[4,8,64,128]{3,2,1,0:T(8,128)S(1)} copy-done((f32[4,8,64,128]{3,2,1,0:T(8,128)S(1)}, f32[4,8,64,128]{3,2,1,0:T(8,128)}, u32[]{:S(2)}) %copy-start) | copy-done | bytes 1048600
  1.2 0.0 copy-start.6
  1.2 0.0 copy-start.7
  1.2 0.0 copy-start.8
  1.2 0.0 copy-start.9
  1.2 0.0 copy-start.10
  1.2 0.0 copy-start.1
  1.3 0.9 pack_border.1
  2.1 9.8 %all-to-all-start = ((f32[32,32,128]{2,1,0:T(8,128)}), f32[32,32,128]{2,1,0:T(8,128)S(1)}, u32[]{:S(2)}, u32[]{:S(2)}) async-start(f32[32,32,128]{2,1,0:T(8,128)} %pack_border.1), calls=%async_computation | async-start | bytes 1048576 | tf_op jit(solution)/shard_map/all_to_all | solution.py:397
  11.9 0.0 copy-done.6
  11.9 0.0 copy-done.7
  11.9 0.0 copy-done.8
  11.9 0.0 copy-done.9
  11.9 0.0 copy-done.10
  12.0 0.0 copy-done.1
  12.0 0.0 copy-start.5
  12.0 1.0 %pack_inner.1 = f32[32,40,128]{2,1,0:T(8,128)} custom-call(f32[32,64,128]{2,1,0:T(8,128)S(1)} %bitcast.12, s32[7,8]{1,0:T(8,128)S(1)} %concatenate.9.table_ref), custom_call_target="tpu_custom_call" | custom-call | tf_op jit(solution)/shard_map/pack_inner/pallas_call | solution.py:388
  13.0 0.0 copy-start.2
  13.0 16.6 %all-to-all-done.blocks_ref = f32[32,32,128]{2,1,0:T(8,128)S(1)} async-done(((f32[32,32,128]{2,1,0:T(8,128)}), f32[32,32,128]{2,1,0:T(8,128)S(1)}, u32[]{:S(2)}, u32[]{:S(2)}) %all-to-all-start) | async-done | bytes 524320 | tf_op jit(solution)/shard_map/all_to_all | solution.py:397
  29.7 4.5 %all-to-all-start.1 = ((f32[32,40,128]{2,1,0:T(8,128)}), f32[32,40,128]{2,1,0:T(8,128)S(1)}, u32[]{:S(2)}, u32[]{:S(2)}) async-start(f32[32,40,128]{2,1,0:T(8,128)} %pack_inner.1), calls=%async_computation.1 | async-start | bytes 1310720 | tf_op jit(solution)/shard_map/all_to_all | solution.py:399
  34.1 0.0 copy-done.5
  34.2 0.1 pad_add_fusion
  34.2 0.1 broadcast_divide_fusion
  34.3 0.1 broadcast_divide_fusion.1
  34.5 0.1 stack.4.upper_ref
  34.6 0.1 broadcast_divide_fusion.2
  34.6 0.1 stack.5.inverse_ref
  34.8 0.0 copy-start.3
  34.8 0.0 copy-start.4
  34.8 3.1 %collective-permute-start.1 = (f32[16,32,128]{2,1,0:T(8,128)S(1)}, f32[16,32,128]{2,1,0:T(8,128)S(1)}, u32[]{:S(2)}, u32[]{:S(2)}) collective-permute-start(f32[16,32,128]{2,1,0:T(8,128)S(1)} %get-tuple-element.33), channel_id=1, source_target_pairs={{48,0},{32,16},{80,32},{64,48},{112,64},{96,80},{144,96},{128,112}... | collective-permute-start | bytes 786440 | tf_op jit(solution)/shard_map/ppermute | solution.py:408
  37.9 0.3 collective-permute-start
  38.1 16.7 %all-to-all-done.1.rest_ref = f32[32,40,128]{2,1,0:T(8,128)S(1)} async-done(((f32[32,40,128]{2,1,0:T(8,128)}), f32[32,40,128]{2,1,0:T(8,128)S(1)}, u32[]{:S(2)}, u32[]{:S(2)}) %all-to-all-start.1) | async-done | bytes 655392 | tf_op jit(solution)/shard_map/all_to_all | solution.py:399
  54.8 0.1 slice_convert_fusion
  54.9 0.0 collective-permute-done.1.south_ref
  54.9 0.0 collective-permute-done.north_ref
  54.9 0.0 copy-done.2
  55.0 4.1 %interpolate.1 = (f32[16,144,128]{2,1,0:T(8,128)S(1)}, f32[32,128]{1,0:T(8,128)S(1)}, f32[32,128]{1,0:T(8,128)S(1)}) custom-call(s32[32,32]{1,0:T(8,128)S(1)} %bitcast.13, f32[32,32,128]{2,1,0:T(8,128)S(1)} %all-to-all-done.blocks_ref, f32[32,40,128]{2,1,0:T(8,128)S(1)} %all-to-all-done.1.rest_ref, f32[16,32,128]{2,1,0:T(8,128)S(1)} %collective-permute-done.north_ref, ...), custom_call_target="tpu_custom_call" | custom-call | tf_op jit(solution)/shard_map/interpolate/pallas_call | solution.py:411
  59.0 2.0 %collective-permute-start.2 = (f32[32,128]{1,0:T(8,128)S(1)}, f32[32,128]{1,0:T(8,128)S(1)}, u32[]{:S(2)}, u32[]{:S(2)}) collective-permute-start(f32[32,128]{1,0:T(8,128)S(1)} %get-tuple-element.22), channel_id=1, source_target_pairs={{0,48},{16,32},{32,80},{48,64},{64,112},{80,96},{96,144},{112,128}... | collective-permute-start | bytes 49160 | tf_op jit(solution)/shard_map/ppermute | solution.py:424
  61.0 2.3 %collective-permute-start.3 = (f32[32,128]{1,0:T(8,128)S(1)}, f32[32,128]{1,0:T(8,128)S(1)}, u32[]{:S(2)}, u32[]{:S(2)}) collective-permute-start(f32[32,128]{1,0:T(8,128)S(1)} %get-tuple-element.23), channel_id=1, source_target_pairs={{48,0},{32,16},{80,32},{64,48},{112,64},{96,80},{144,96},{128,112}... | collective-permute-start | bytes 49160 | tf_op jit(solution)/shard_map/ppermute | solution.py:425
  63.3 0.0 copy-done.3
  63.3 0.0 copy-done.4
  63.3 2.1 %diffuse.1.inner_ref = f32[32,64,128]{2,1,0:T(8,128)S(1)} custom-call(f32[4,8]{1,0:T(4,128)S(1)} %copy-done.4, f32[16,144,128]{2,1,0:T(8,128)S(1)} %get-tuple-element.24.phi_ref, bf16[512,128]{1,0:T(8,128)(2,1)S(1)} %copy-done.3), custom_call_target="tpu_custom_call" | custom-call | tf_op jit(solution)/shard_map/diffuse/pallas_call | solution.py:427
  65.4 0.0 collective-permute-done.2.north_ref
  65.4 0.6 collective-permute-done.3.south_ref
  66.0 0.7 mend.1
  66.6 32.5 %all_to_all.15.psi_ref = f32[32,64,128]{2,1,0:T(8,128)S(1)} all-to-all(f32[32,64,128]{2,1,0:T(8,128)S(1)} %mend.1), channel_id=1, replica_groups=mesh['group'=8,'part'=2,'lon'=16] {'part','lon'}, dimensions={0} | all-to-all | bytes 2097152 | tf_op jit(solution)/shard_map/all_to_all | solution.py:448
  99.2 1.7 %solve.1 = f32[4,8,64,128]{3,2,1,0:T(8,128)} custom-call(f32[4,8]{1,0:T(4,128)S(1)} %get-tuple-element.17.lower_ref, f32[4,8]{1,0:T(4,128)S(1)} %stack.4.upper_ref, f32[4,8]{1,0:T(4,128)S(1)} %stack.5.inverse_ref, f32[32,64,128]{2,1,0:T(8,128)S(1)} %all_to_all.15.psi_ref), custom_call_target="tpu_custom_call" | custom-call | tf_op jit(solution)/shard_map/solve/pallas_call | solution.py:449
  (2 shorter events, 0.1 us)
Async XLA Ops:
  0.0 1.2 %copy-start = (f32[4,8,64,128]{3,2,1,0:T(8,128)S(1)}, f32[4,8,64,128]{3,2,1,0:T(8,128)}, u32[]{:S(2)}) copy-start(f32[4,8,64,128]{3,2,1,0:T(8,128)} %param.10) | copy-start | bytes 3145732
  1.2 10.7 %copy-start.6 = (s32[1,1,8,2]{2,3,1,0:T(2,128)S(1)}, s32[1,1,8,2]{2,3,1,0:T(2,128)}, u32[]{:S(2)}) copy-start(s32[1,1,8,2]{2,3,1,0:T(2,128)} %param.16) | copy-start | bytes 196
  1.2 10.7 %copy-start.7 = (s32[1,1,8,2]{2,3,1,0:T(2,128)S(1)}, s32[1,1,8,2]{2,3,1,0:T(2,128)}, u32[]{:S(2)}) copy-start(s32[1,1,8,2]{2,3,1,0:T(2,128)} %param.17) | copy-start | bytes 196
  1.2 10.7 %copy-start.8 = (s32[1,1,8,1]{2,3,1,0:T(1,128)S(1)}, s32[1,1,8,1]{2,3,1,0:T(1,128)}, u32[]{:S(2)}) copy-start(s32[1,1,8,1]{2,3,1,0:T(1,128)} %param.13) | copy-start | bytes 100
  1.2 10.7 %copy-start.9 = (s32[1,1,8,1]{2,3,1,0:T(1,128)S(1)}, s32[1,1,8,1]{2,3,1,0:T(1,128)}, u32[]{:S(2)}) copy-start(s32[1,1,8,1]{2,3,1,0:T(1,128)} %param.14) | copy-start | bytes 100
  1.2 10.7 %copy-start.10 = (s32[1,1,8,1]{2,3,1,0:T(1,128)S(1)}, s32[1,1,8,1]{2,3,1,0:T(1,128)}, u32[]{:S(2)}) copy-start(s32[1,1,8,1]{2,3,1,0:T(1,128)} %param.15) | copy-start | bytes 100
  1.2 10.7 %copy-start.1 = (f32[4,8,64,128]{3,2,1,0:T(8,128)S(1)}, f32[4,8,64,128]{3,2,1,0:T(8,128)}, u32[]{:S(2)}) copy-start(f32[4,8,64,128]{3,2,1,0:T(8,128)} %param.10) | copy-start | bytes 3145732
  2.1 27.5 %all-to-all-start = ((f32[32,32,128]{2,1,0:T(8,128)}), f32[32,32,128]{2,1,0:T(8,128)S(1)}, u32[]{:S(2)}, u32[]{:S(2)}) async-start(f32[32,32,128]{2,1,0:T(8,128)} %pack_border.1), calls=%async_computation | async-start | bytes 1048576 | tf_op jit(solution)/shard_map/all_to_all | solution.py:397
  12.0 22.2 %copy-start.5 = (f32[4,7]{1,0:T(4,128)S(1)}, f32[4,7]{1,0:T(4,128)}, u32[]{:S(2)}) copy-start(f32[4,7]{1,0:T(4,128)} %param.12) | copy-start | bytes 340
  13.0 41.9 %copy-start.2 = (bf16[256,384]{1,0:T(8,128)(2,1)S(1)}, bf16[256,384]{1,0:T(8,128)(2,1)}, u32[]{:S(2)}) copy-start(bf16[256,384]{1,0:T(8,128)(2,1)} %constant.4.clone.taps_ref) | copy-start | bytes 589828
  29.7 25.2 %all-to-all-start.1 = ((f32[32,40,128]{2,1,0:T(8,128)}), f32[32,40,128]{2,1,0:T(8,128)S(1)}, u32[]{:S(2)}, u32[]{:S(2)}) async-start(f32[32,40,128]{2,1,0:T(8,128)} %pack_inner.1), calls=%async_computation.1 | async-start | bytes 1310720 | tf_op jit(solution)/shard_map/all_to_all | solution.py:399
  34.8 28.5 %copy-start.3 = (bf16[512,128]{1,0:T(8,128)(2,1)S(1)}, bf16[512,128]{1,0:T(8,128)(2,1)}, u32[]{:S(2)}) copy-start(bf16[512,128]{1,0:T(8,128)(2,1)} %constant.12.clone.beside_ref) | copy-start | bytes 393220
  34.8 28.5 %copy-start.4 = (f32[4,8]{1,0:T(4,128)S(1)}, f32[4,8]{1,0:T(4,128)}, u32[]{:S(2)}) copy-start(f32[4,8]{1,0:T(4,128)} %coef_ref.3) | copy-start | bytes 388
  34.8 20.1 %collective-permute-start.1 = (f32[16,32,128]{2,1,0:T(8,128)S(1)}, f32[16,32,128]{2,1,0:T(8,128)S(1)}, u32[]{:S(2)}, u32[]{:S(2)}) collective-permute-start(f32[16,32,128]{2,1,0:T(8,128)S(1)} %get-tuple-element.33), channel_id=1, source_target_pairs={{48,0},{32,16},{80,32},{64,48},{112,64},{96,80},{144,96},{128,112}... | collective-permute-start | bytes 786440 | tf_op jit(solution)/shard_map/ppermute | solution.py:408
  37.9 17.1 %collective-permute-start = (f32[16,32,128]{2,1,0:T(8,128)S(1)}, f32[16,32,128]{2,1,0:T(8,128)S(1)}, u32[]{:S(2)}, u32[]{:S(2)}) collective-permute-start(f32[16,32,128]{2,1,0:T(8,128)S(1)} %get-tuple-element.34), channel_id=1, source_target_pairs={{0,48},{16,32},{32,80},{48,64},{64,112},{80,96},{96,144},{112,128}... | collective-permute-start | bytes 786440 | tf_op jit(solution)/shard_map/ppermute | solution.py:407
  59.0 6.3 %collective-permute-start.2 = (f32[32,128]{1,0:T(8,128)S(1)}, f32[32,128]{1,0:T(8,128)S(1)}, u32[]{:S(2)}, u32[]{:S(2)}) collective-permute-start(f32[32,128]{1,0:T(8,128)S(1)} %get-tuple-element.22), channel_id=1, source_target_pairs={{0,48},{16,32},{32,80},{48,64},{64,112},{80,96},{96,144},{112,128}... | collective-permute-start | bytes 49160 | tf_op jit(solution)/shard_map/ppermute | solution.py:424
  61.0 4.9 %collective-permute-start.3 = (f32[32,128]{1,0:T(8,128)S(1)}, f32[32,128]{1,0:T(8,128)S(1)}, u32[]{:S(2)}, u32[]{:S(2)}) collective-permute-start(f32[32,128]{1,0:T(8,128)S(1)} %get-tuple-element.23), channel_id=1, source_target_pairs={{48,0},{32,16},{80,32},{64,48},{112,64},{96,80},{144,96},{128,112}... | collective-permute-start | bytes 49160 | tf_op jit(solution)/shard_map/ppermute | solution.py:425
